TPU v7x, 256 devices: a whole 4x4x8 slice. The times are simulated.
256 devices in a mesh: blk: 128 (over z_hi, y, x, core), head: 2 (over z_lo).
Axes of the slice: x: 4, y: 4, z: 8 (z_hi: 4, z_lo: 2; z = z_hi * 2 + z_lo), core: 2. Of those that a mesh axis runs over, the one named last changes fastest.
Arguments:
- cells: bfloat16 [65536, 256], P('blk', 'head'), may hold values from -6 to 6
- w_query: bfloat16 [256, 256], P(None, 'head'), may hold values from -0.375 to 0.375
- w_key: bfloat16 [256, 256], P(None, 'head'), may hold values from -0.375 to 0.375
- w_value: bfloat16 [256, 256], P(None, 'head'), may hold values from -0.375 to 0.375
- w_source: bfloat16 [2, 256, 256], P(None, None, 'head'), may hold values from -0.375 to 0.375
- w_target: bfloat16 [2, 256, 256], P(None, None, 'head'), may hold values from -0.375 to 0.375
- msg_bias: float32 [2, 256], P(None, 'head'), may hold values from -3 to 3
- w_out: bfloat16 [256, 256], P('head'), may hold values from -0.375 to 0.375
- nbr_block: int32 [512, 4], P('blk'), may hold values from 0 to 511, as said below
- edge_src: int32 [65536, 8], P('blk'), may hold values from 0 to 511
- key_blocks: int32 [512, 32], P('blk'), may hold values from 0 to 511, as said below
Outputs:
- updated: bfloat16 [65536, 256], P('blk', 'head')
Inputs may be any that keep to these rules, and one draw needn't show every extreme that they name: `nbr_block`: the source blocks listed for a destination block lie in its own partition of 4 consecutive blocks or in the partition just before or after it on the loop of 128 partitions. `key_blocks`: each row lists 32 key blocks from 32 different partitions; among all key blocks listed by the 4 query blocks of one partition, those that lie in one partition are the same block.
All inputs are finite; a program needn't handle non-finite values.
Results may differ from a plain program's by a relative error of at most 0.0015.
The roundings to bfloat16 on the way count: a program that leaves them out, or rounds other values in their place, can miss the bound.
Values may be sent and summed in bfloat16 or wider, within the bound.
No kernel may reach another device: no remote copies, remote signals or barrier semaphores. Data moves between devices by JAX's collectives and lax.ppermute only.
A program may use at most 128 MiB of HBM per device.

v0:
```python
import jax
import jax.numpy as jnp
from jax import lax
from jax.sharding import PartitionSpec as P

HEAD_DIM = 32
BLOCK = 128


def padded(value, sides, width):
    for axis, dim in sides:
        peers, length = (lax.axis_size(axis), value.shape[dim])
        up = [(i, (i + 1) % peers) for i in range(peers)]
        down = [(j, i) for i, j in up]
        last = lax.slice_in_dim(value, length - width, length, axis=dim)
        initial = lax.slice_in_dim(value, 0, width, axis=dim)
        before = lax.ppermute(last, axis, up)
        after = lax.ppermute(initial, axis, down)
        value = jnp.concatenate([before, value, after], axis=dim)
    return value


def body(
    cells,
    w_query,
    w_key,
    w_value,
    w_source,
    w_target,
    msg_bias,
    w_out,
    nbr_block,
    edge_src,
    key_blocks,
):
    rows = cells.shape[0]
    width = w_query.shape[1]
    heads_here = width // HEAD_DIM
    blk_dev = rows // BLOCK
    nparts = lax.axis_size("blk")
    edge_count = edge_src.shape[1]
    scale = HEAD_DIM ** (-0.5)
    whole = lax.all_gather(cells, "head", axis=1, tiled=True)
    queries = jnp.dot(whole, w_query, preferred_element_type=jnp.float32).astype(jnp.bfloat16)
    keys = jnp.dot(whole, w_key, preferred_element_type=jnp.float32).astype(jnp.bfloat16)
    values = jnp.dot(whole, w_value, preferred_element_type=jnp.float32).astype(jnp.bfloat16)
    source = jnp.einsum("cd,gdk->cgk", whole, w_source, preferred_element_type=jnp.float32)
    source = source.astype(jnp.bfloat16).reshape(rows, 2 * width)
    target = (
        jnp.einsum("cd,gdk->cgk", whole, w_target, preferred_element_type=jnp.float32)
        + msg_bias[None]
    )
    window = padded(source, (("blk", 0),), rows)
    mine = lax.axis_index("blk")
    own_block = jnp.arange(rows, dtype=jnp.int32) // BLOCK
    src_block = nbr_block[own_block[:, None], edge_src // BLOCK]
    offset = (src_block // blk_dev - mine + 1) % nparts
    window_row = offset * rows + src_block % blk_dev * BLOCK + edge_src % BLOCK
    fetched = jnp.take(window, window_row.reshape(-1), axis=0).reshape(rows, edge_count, 2, width)
    pre = fetched.astype(jnp.float32) + target[:, None]
    message = jax.nn.sigmoid(pre[:, :, 0]) * jax.nn.silu(pre[:, :, 1])
    aggregate = jnp.mean(message, axis=1)
    query_heads = queries.reshape(rows, heads_here, HEAD_DIM)
    part_of = key_blocks // blk_dev
    local_of = key_blocks % blk_dev

    def tile(carry, key_piece, value_piece, first):
        source_part = first // rows
        hit = part_of == source_part
        chosen_local = jnp.max(jnp.where(hit, local_of, -1))
        query_uses = jnp.any(hit, axis=1)
        numer, total = carry
        begin = jnp.maximum(chosen_local, 0) * BLOCK
        block_keys = lax.dynamic_slice_in_dim(key_piece, begin, BLOCK, 0)
        block_values = lax.dynamic_slice_in_dim(value_piece, begin, BLOCK, 0)
        row_mask = jnp.repeat(query_uses, BLOCK).astype(jnp.float32)
        scores = (
            jnp.einsum(
                "qhd,khd->hqk",
                query_heads,
                block_keys.reshape(BLOCK, heads_here, HEAD_DIM),
                preferred_element_type=jnp.float32,
            )
            * scale
        )
        weight = jnp.exp(scores) * row_mask[None, :, None]
        total = total + jnp.sum(weight, axis=2)
        added = jnp.einsum(
            "hqk,khd->qhd",
            weight.astype(jnp.bfloat16),
            block_values.reshape(BLOCK, heads_here, HEAD_DIM),
            preferred_element_type=jnp.float32,
        )
        return (numer + added.reshape(rows, width), total)

    initial = (jnp.zeros((rows, width), jnp.float32), jnp.zeros((heads_here, rows), jnp.float32))
    carry = initial
    key_piece = lax.all_gather(keys, "blk", axis=0, tiled=True)
    value_piece = lax.all_gather(values, "blk", axis=0, tiled=True)
    count = key_piece.shape[0]

    def advance(state, turn):
        first = turn * rows
        part_keys = lax.dynamic_slice_in_dim(key_piece, first, rows, 0)
        part_values = lax.dynamic_slice_in_dim(value_piece, first, rows, 0)
        return (tile(state, part_keys, part_values, first), None)

    carry, unused = lax.scan(advance, carry, jnp.arange(count // rows, dtype=jnp.int32))
    numer, total = carry
    mixed = (numer / jnp.repeat(jnp.transpose(total), HEAD_DIM, axis=1)).astype(jnp.bfloat16)
    partial_out = jnp.dot(mixed, w_out, preferred_element_type=jnp.float32)
    attended = lax.psum_scatter(partial_out, "head", scatter_dimension=1, tiled=True)
    return (cells.astype(jnp.float32) + aggregate + attended).astype(jnp.bfloat16)


def solution(mesh):
    in_specs = (
        P("blk", "head"),
        P(None, "head"),
        P(None, "head"),
        P(None, "head"),
        P(None, None, "head"),
        P(None, None, "head"),
        P(None, "head"),
        P("head", None),
        P("blk", None),
        P("blk", None),
        P("blk", None),
    )
    out_specs = P("blk", "head")
    return jax.shard_map(body, mesh=mesh, in_specs=in_specs, out_specs=out_specs, check_vma=False)
```

profile of v0, /device:TPU:8, one launch (start us, length us, event | category | flops | bytes accessed | tf_op | source)
XLA Modules:
  0.0 1105.6 jit_solution(5081986127554945908)
XLA Ops:
  6.5 6.5 all_gather.9
  13.0 1.7 convolution_convert_fusion.2
  14.8 1.7 convolution_convert_fusion.1
  18.2 3.8 collective-permute-start.1
  22.6 34.6 %gather_fusion = s32[4096]{0:T(1024)S(1)} fusion(s32[4,4]{1,0:T(4,128)S(1)} %copy-done.1, s32[4096]{0:T(1024)S(1)} %reshape.116), kind=kCustom, calls=%fused_computation | custom fusion | bytes 65536 | tf_op jit(solution)/shard_map/gather | solution.py:56
  60.5 14.6 %gather_fusion.1 = bf16[4096,256]{1,0:T(8,128)(2,1)S(1)} fusion(bf16[1536,256]{1,0:T(8,128)(2,1)S(1)} %pad_maximum_fusion, s32[4096]{0:T(1024)S(1)} %broadcast_clamp_fusion), kind=kCustom, calls=%fused_computation.1 | custom fusion | bytes 4210688 | tf_op jit(solution)/shard_map/jit(_take)/gather | solution.py:59
  75.2 52.4 %all-gather.3.cloned.1.call-done = bf16[65536,128]{1,0:T(8,128)(2,1)} async-done(((bf16[512,128]{1,0:T(8,128)(2,1)}), bf16[65536,128]{1,0:T(8,128)(2,1)}) %all-gather.3.cloned.1.call-update) | async-done | bytes 16777232 | tf_op jit(solution)/shard_map/all_gather | solution.py:99
  127.5 118.2 %all-gather.5.cloned.1.call-done = bf16[65536,128]{1,0:T(8,128)(2,1)} async-done(((bf16[512,128]{1,0:T(8,128)(2,1)}), bf16[65536,128]{1,0:T(8,128)(2,1)}) %all-gather.5.cloned.1.call-update) | async-done | bytes 16777232 | tf_op jit(solution)/shard_map/all_gather | solution.py:98
  246.2 824.6 %while.15 = (s32[]{:T(128)}, f32[512,128]{0,1:T(8,128)S(1)}, f32[4,512]{1,0:T(4,128)S(1)}, s32[128]{0:T(128)}, s32[4,32]{1,0:T(4,128)}, /*index=5*/s32[4,32]{1,0...) while((s32[]{:T(128)}, f32[512,128]{0,1:T(8,128)S(1)}, ...), condition=%wide.region_5.6_spmd.clone, body=%wide.region_1.5_spmd.clone.sunk | while | flops 34736664 | bytes 2594593 | solution.py:108
  248.8 1.3 select_reduce_fusion.2
  255.3 1.3 select_reduce_fusion.2
  261.7 1.3 select_reduce_fusion.2
  268.2 1.3 select_reduce_fusion.2
  274.6 1.3 select_reduce_fusion.2
  281.0 1.3 select_reduce_fusion.2
  287.5 1.3 select_reduce_fusion.2
  293.9 1.3 select_reduce_fusion.2
  300.4 1.3 select_reduce_fusion.2
  306.8 1.3 select_reduce_fusion.2
  1070.9 1.9 fusion.38
  1072.8 2.5 convert_add_fusion
  1075.3 1.9 fusion.11
  1077.3 20.1 %reduce-scatter.2.cloned.1.call-done = f32[512,128]{1,0:T(8,128)} async-done(((f32[512,256]{1,0:T(8,128)}), f32[512,128]{1,0:T(8,128)}) %reduce-scatter.2.cloned.1.call-update) | async-done | bytes 262160 | tf_op jit(solution)/shard_map/reduce_scatter | solution.py:112
  1097.4 1.7 add_convert_fusion
  (1571 shorter events, 653.6 us)
Async XLA Ops:
  6.5 51.6 %copy-start = (bf16[2,256,128]{2,1,0:T(8,128)(2,1)S(1)}, bf16[2,256,128]{2,1,0:T(8,128)(2,1)}, u32[]{:S(2)}) copy-start(bf16[2,256,128]{2,1,0:T(8,128)(2,1)} %param.18) | copy-start | bytes 393220
  6.5 15.5 %copy-start.4 = (s32[512,8]{0,1:T(8,128)S(1)}, s32[512,8]{0,1:T(8,128)}, u32[]{:S(2)}) copy-start(s32[512,8]{0,1:T(8,128)} %param.22) | copy-start | bytes 49156
  6.5 121.0 %all-gather.3.cloned.1.call-start = ((), (), s32[]{:S(2)}) async-start(), calls=%async_computation.1 | async-start | bytes 16908288 | tf_op jit(solution)/shard_map/all_gather | solution.py:99
  14.8 7.8 copy-start.1
  14.8 230.9 %all-gather.5.cloned.1.call-start = ((), (), s32[]{:S(2)}) async-start(), calls=%async_computation.2 | async-start | bytes 16908288 | tf_op jit(solution)/shard_map/all_gather | solution.py:98
  16.6 1080.8 %reduce-scatter.2.cloned.1.call-start = ((), (), s32[]{:S(2)}) async-start(), calls=%async_computation.3 | async-start | bytes 786432 | tf_op jit(solution)/shard_map/reduce_scatter | solution.py:112
  18.1 42.4 %collective-permute-start = (bf16[512,256]{1,0:T(8,128)(2,1)S(1)}, bf16[512,256]{1,0:T(8,128)(2,1)S(1)}, u32[]{:S(2)}, u32[]{:S(2)}) collective-permute-start(bf16[512,256]{1,0:T(8,128)(2,1)S(1)} %copy.28), channel_id=1, source_target_pairs={{0,2},{2,4},{4,6},{6,8},{8,10},{10,12},{12,14},{14,16},{16,18},{18... | collective-permute-start | bytes 786440 | tf_op jit(solution)/shard_map/ppermute | solution.py:17
  18.2 42.3 %collective-permute-start.1 = (bf16[512,256]{1,0:T(8,128)(2,1)S(1)}, bf16[512,256]{1,0:T(8,128)(2,1)S(1)}, u32[]{:S(2)}, u32[]{:S(2)}) collective-permute-start(bf16[512,256]{1,0:T(8,128)(2,1)S(1)} %copy.28), channel_id=1, source_target_pairs={{2,0},{4,2},{6,4},{8,6},{10,8},{12,10},{14,12},{16,14},{18,16},{20... | collective-permute-start | bytes 786440 | tf_op jit(solution)/shard_map/ppermute | solution.py:18
  22.6 35.6 %copy-start.6 = (f32[2,128]{1,0:T(2,128)S(1)}, f32[2,128]{1,0:T(2,128)}, u32[]{:S(2)}) copy-start(f32[2,128]{1,0:T(2,128)} %param.19) | copy-start | bytes 3076
  57.2 1.2 copy-start.5
  57.2 3.0 copy-start.3
  1075.3 22.1 %copy-start.2 = (bf16[512,128]{1,0:T(8,128)(2,1)S(1)}, bf16[512,128]{1,0:T(8,128)(2,1)}, u32[]{:S(2)}) copy-start(bf16[512,128]{1,0:T(8,128)(2,1)} %param.13) | copy-start | bytes 393220
Sparse Core Ops, SparseCore 0:
  14.9 112.5 all-gather.2
  131.1 114.5 all-gather.4
  1072.9 24.4 reduce-scatter.1
where the time goes:
time: 1120 us; the launch traced here: 1110 us
  local copies, waits for them, and re-layouts  348 us (31%)
  other arithmetic  291 us (26%)
  waiting for transfers between devices  191 us (17%)
  loops' own time  164 us (15%)
  matrix products  88.2 us (8%)
  between operations  13.4 us (1%)
    reduce_max x128, other arithmetic, tile(): chosen_local = jnp.max(jnp.where(hit, local_of, -1))  169 us
    another operation x1, loops' own time, body(): lax.scan(advance, carry, jnp.arange(count // rows, dtype=jnp.int32))  164 us
    dynamic_slice x128, local copies, waits for them, and re-layouts, body(): lax.scan(advance, carry, jnp.arange(count // rows, dtype=jnp.int32))  155 us
    all_gather x1, waiting for transfers between devices, body(): key_piece = lax.all_gather(keys, 'blk', axis=0, tiled=True)  118 us
    dynamic_slice x256, local copies, waits for them, and re-layouts, tile(): block_keys = lax.dynamic_slice_in_dim(key_piece, begin, BLOCK, 0)  118 us
    reduce_or x128, other arithmetic, tile(): query_uses = jnp.any(hit, axis=1)  102 us
    dot_general x128, matrix products, tile(): jnp.einsum('qhd,khd->hqk', query_heads, block_keys.reshape(BLOCK, heads_h...  55.5 us
    all_gather x1, waiting for transfers between devices, body(): value_piece = lax.all_gather(values, 'blk', axis=0, tiled=True)  52.4 us
  transfers between devices with their start and end apart: 5, of which 3 were waited for; matrix products, arithmetic and copies ran while one was open for 5% of the time, Pallas kernels for 0%

commit v1 on v0

v1 whole, which is shorter than its diff:
```python
import functools
import math

import jax
import jax.numpy as jnp
from jax import lax
from jax.experimental import pallas as pl
from jax.experimental.pallas import tpu as pltpu
from jax.sharding import Mesh
from jax.sharding import PartitionSpec as P

HEAD_DIM = 32
BLOCK = 128
BLK_DEV = 4
GROUP = 2
UNROLL = 8
EMPTY = 64
STAGES = ((0, 8), (8, 16), (24, 8))
NN = (((1,), (0,)), ((), ()))
NT = (((1,), (1,)), ((), ()))
TN = (((0,), (0,)), ((), ()))
TT = (((0,), (1,)), ((), ()))
F32 = jnp.float32
BF16 = jnp.bfloat16
EXP2_SCALE = math.log2(math.e) / math.sqrt(HEAD_DIM)


def dot(a, b, dims):
    return lax.dot_general(a, b, dims, preferred_element_type=F32)


def full(shape):
    return pl.BlockSpec(shape, lambda *_: (0,) * len(shape))


def call(kernel, outs, args, name, scalars=(), scratch=(), flops=10**6, trans=0, after=()):
    moved = sum(a.size * a.dtype.itemsize for a in args)
    return pl.pallas_call(
        kernel,
        grid_spec=pltpu.PrefetchScalarGridSpec(
            num_scalar_prefetch=len(scalars),
            grid=(1,),
            in_specs=[full(a.shape) for a in args] + [pl.BlockSpec(memory_space=pl.ANY)] * len(after),
            out_specs=[full(o.shape) for o in outs],
            scratch_shapes=list(scratch),
        ),
        out_shape=outs,
        compiler_params=pltpu.CompilerParams(vmem_limit_bytes=48 << 20),
        cost_estimate=pl.CostEstimate(flops=flops, bytes_accessed=moved, transcendentals=trans),
        name=name,
    )(*scalars, *args, *after)


def whole_rows(side_ref, own_ref, other_ref):
    own, other = own_ref[...], other_ref[...]
    first = side_ref[0] == 0
    return jnp.concatenate([jnp.where(first, own, other), jnp.where(first, other, own)], axis=1)


def prepare_kernel(place_ref, cells_ref, wk_ref, wv_ref, wq_ref, blocks_ref, partial_ref, rest_ref, codes_ref):
    side, zh, core = place_ref[0], place_ref[1], place_ref[2]
    mine = pl.ds(pl.multiple_of(side * BLOCK, BLOCK), BLOCK)
    theirs = pl.ds(pl.multiple_of((1 - side) * BLOCK, BLOCK), BLOCK)
    for n, w_ref in enumerate((wk_ref, wv_ref, wq_ref)):
        partial_ref[n] = dot(w_ref[mine, :], cells_ref[...], TT)
        rest_ref[n] = jnp.transpose(w_ref[theirs, :].astype(F32)).astype(BF16)

    def facts(ids):
        owner = ids // BLK_DEV
        far = (owner // 32 - zh) & 3
        stage = jnp.where(far == 0, 0, jnp.where(far == 2, 2, 1))
        mate = jnp.where(stage == 1, 8, 4)
        slot = jnp.where(owner % 2 != core, mate, 0) + owner // 2 % 4 + jnp.where(far == 1, 4, 0)
        return owner // 8 % 4, stage, slot * BLK_DEV + ids % BLK_DEV

    lane = lax.broadcasted_iota(jnp.int32, (32, 32), 1)
    below = lane < lax.broadcasted_iota(jnp.int32, (32, 32), 0)
    found = [[] for _ in range(4)]
    tally = [jnp.zeros((1, 32), F32) for _ in range(4)]
    for block in range(BLK_DEV):
        across = jnp.broadcast_to(blocks_ref[block : block + 1, :], (32, 32))
        down = jnp.transpose(across.astype(F32)).astype(jnp.int32)
        y_across, stage_across, _ = facts(across)
        y_down, stage_down, code = facts(down)
        same = (y_across == y_down) & (stage_across == stage_down) & below
        rank = jnp.sum(same.astype(F32), axis=1, keepdims=True).astype(jnp.int32)
        start = jnp.where(stage_down == 0, 0, jnp.where(stage_down == 1, 8, 24))
        at = rank + start == lane
        for y in range(4):
            row = jnp.sum(jnp.where(at & (y_down == y), code - EMPTY, 0).astype(F32), axis=0, keepdims=True)
            found[y].append(row + EMPTY)
            listed = (y_down == y) & (stage_down + 4 * block == lane)
            tally[y] = tally[y] + jnp.sum(listed.astype(F32), axis=0, keepdims=True)
    rows = []
    for y in range(4):
        units = jnp.maximum((tally[y].astype(jnp.int32) + GROUP - 1) // GROUP, 1).astype(F32)
        rows += [jnp.concatenate(found[y], axis=1), jnp.concatenate([units, jnp.zeros((1, 96), F32)], axis=1)]
    codes_ref[...] = jnp.concatenate(rows + [jnp.zeros((8, BLOCK), F32)], axis=0).astype(BF16)


def keyval_kernel(place_ref, partial_ref, rest_ref, other_ref, own_ref, *outs):
    *sends, keyval = outs
    other = other_ref[...]
    for n in range(2):
        flat = (partial_ref[n] + dot(rest_ref[n], other, NT)).astype(BF16)
        for head in range(4):
            ahead = (head - place_ref[3]) & 3
            for b in range(BLK_DEV):
                part = flat[head * 32 : head * 32 + 32, b * BLOCK : (b + 1) * BLOCK]
                keyval[ahead, n * BLOCK + b * 32 : n * BLOCK + b * 32 + 32, :] = part
    own_ref[...] = keyval[0]
    for d, ref in enumerate(sends):
        ref[...] = keyval[d + 1]


def query_kernel(partial_ref, rest_ref, other_ref, codes_ref, got0_ref, got1_ref, got2_ref, out_ref):
    flat = (partial_ref[2] + dot(rest_ref[2], other_ref[...], NT)).astype(BF16)
    for head in range(4):
        for y in range(4):
            for b in range(BLK_DEV):
                part = flat[head * 32 : head * 32 + 32, b * BLOCK : (b + 1) * BLOCK]
                out_ref[y * 4 + head, b * 32 : b * 32 + 32, :] = part
            out_ref[y * 4 + head, BLOCK : BLOCK + 16, :] = codes_ref[...]


def gather_kernel(place_ref, own_ref, *refs):
    *got, out_ref = refs
    for d, ref in enumerate((own_ref, *got)):
        out_ref[(place_ref[3] - d) & 3] = ref[...]


def relay_kernel(left_ref, right_ref, after_ref, low_ref, high_ref, both_ref):
    low_ref[...] = left_ref[:2]
    high_ref[...] = right_ref[2:]
    both_ref[:4] = left_ref[...]
    both_ref[4:] = right_ref[...]


def pass_kernel(low_ref, high_ref, after_ref, out_ref):
    out_ref[:2] = low_ref[...]
    out_ref[2:] = high_ref[...]


def source_kernel(side_ref, own_ref, other_ref, ws_ref, wt_ref, bias_ref, after_ref, source_ref, target_ref):
    whole = whole_rows(side_ref, own_ref, other_ref)
    for g in range(2):
        cols = slice(g * BLOCK, (g + 1) * BLOCK)
        source_ref[:, cols] = dot(whole, ws_ref[g], NN).astype(BF16)
        target_ref[:, cols] = dot(whole, wt_ref[g], NN) + bias_ref[g : g + 1, :]


def edge_kernel(wb_ref, before_ref, own_ref, after_ref, target_ref, edge_ref, cells_ref, out_ref, win):
    for side, ref in enumerate((before_ref, own_ref, after_ref)):
        for block in range(BLK_DEV):
            win[side * BLK_DEV + block] = ref[block * BLOCK : (block + 1) * BLOCK, :]
    lane = lax.broadcasted_iota(jnp.int32, (BLOCK, 4 * BLOCK), 1)

    def one(block, unused):
        rows = pl.ds(pl.multiple_of(block * BLOCK, BLOCK), BLOCK)
        table = jnp.concatenate([win[wb_ref[block, k]] for k in range(4)], axis=0)
        target = target_ref[rows, :]
        picks = edge_ref[rows, :]
        total = jnp.zeros((BLOCK, BLOCK), F32)
        for e in range(8):
            hot = (picks[:, e : e + 1] == lane).astype(F32).astype(BF16)
            pre = dot(hot, table, NN) + target
            gate = 0.5 + 0.5 * jnp.tanh(0.5 * pre[:, :BLOCK])
            value = pre[:, BLOCK:]
            total = total + gate * (value * (0.5 + 0.5 * jnp.tanh(0.5 * value)))
        out_ref[rows, :] = cells_ref[rows, :].astype(F32) + total * 0.125
        return unused

    lax.fori_loop(0, BLK_DEV, one, 0)


def load_blocks(pieces, keys, values):
    first = 0
    for ref in pieces:
        for x in range(ref.shape[0]):
            for b in range(BLK_DEV):
                part = ref[x, b * 32 : (b + 1) * 32, :].astype(F32)
                keys[first] = jnp.transpose(part).astype(BF16)
                values[first, 0:32, :] = ref[x, BLOCK + b * 32 : BLOCK + (b + 1) * 32, :]
                values[first, 32:48, :] = jnp.ones((16, BLOCK), BF16)
                first += 1
    keys[first] = jnp.zeros((BLOCK, 32), BF16)
    values[first] = jnp.zeros((48, BLOCK), BF16)


def accumulate(stage, unroll, list_ref, start, end, queries, keys, values, acc, scored):
    base = STAGES[stage][0]
    spare = keys.shape[0] - 1

    def length(i):
        return list_ref[(i >> 2) * 2 + 1, ((i & 3) << 2) + stage]

    def following(i, j):
        over = j + 1 >= length(i)
        return jnp.where(over, jnp.minimum(i + 1, end), i), jnp.where(over, 0, j + 1)

    def batch(i, j):
        units = [(i, j)]
        for _ in range(unroll - 1):
            units.append(following(*units[-1]))
        return units

    def picked(table, axis, i, j):
        row, column = (i >> 2) * 2, ((i & 3) << 5) + base + j * GROUP
        blocks = [jnp.where(i < end, jnp.minimum(list_ref[row, column + g], spare), spare) for g in range(GROUP)]
        return jnp.concatenate([table[block] for block in blocks], axis=axis)

    def scores(units):
        for w, (i, j) in enumerate(units):
            scored[w] = dot(picked(keys, 0, i, j), queries[i - start], NN)

    def step(u, state):
        now = [(state[2 * w], state[2 * w + 1]) for w in range(unroll)]
        later = batch(*following(*now[-1]))
        weights = [jnp.exp2(scored[w] * EXP2_SCALE).astype(BF16) for w in range(unroll)]
        scores(later)
        for w, (i, j) in enumerate(now):
            acc[i - start] = acc[i - start] + dot(picked(values, 1, i, j), weights[w], NN)[0:40, :]
        return tuple(v for pair in later for v in pair)

    count = lax.fori_loop(start, end, lambda i, s: s + length(i), jnp.int32(0))
    begin = batch(jnp.int32(0) + start, jnp.int32(0))
    scores(begin)
    lax.fori_loop(0, (count + unroll - 1) // unroll, step, tuple(v for pair in begin for v in pair))


def attend_kernel(stage, npieces, resume, list_ref, q_ref, *refs):
    last = stage == len(STAGES) - 1
    pieces, refs = refs[:npieces], refs[npieces:]
    out_ref, queries, keys, values, scored, *rest = refs[1:] if resume else refs
    acc = rest[0] if last else out_ref
    for m in range(64):
        top = (m % 4) * 32
        queries[m] = q_ref[m // 16, m // 4 % 4, top : top + 32, :]
    queries[64] = jnp.zeros((32, BLOCK), BF16)
    load_blocks(pieces, keys, values)
    acc[...] = refs[0][...] if resume else jnp.zeros(acc.shape, F32)
    accumulate(stage, UNROLL, list_ref, 0, 64, queries, keys, values, acc, scored)
    if last:
        for y in range(4):
            for m in range(16):
                a = acc[y * 16 + m]
                out_ref[y, m * 32 : (m + 1) * 32, :] = a[0:32, :]
                out_ref[y, 512 + m : 513 + m, :] = a[32:33, :]


def attend(stage, lists, q_all, pieces, carry, flops):
    last = stage == len(STAGES) - 1
    blocks = STAGES[stage][1] * BLK_DEV + 1
    scratch = [
        pltpu.VMEM((65, 32, BLOCK), BF16),
        pltpu.VMEM((blocks, BLOCK, 32), BF16),
        pltpu.VMEM((blocks, 48, BLOCK), BF16),
        pltpu.VMEM((UNROLL, BLOCK * GROUP, BLOCK), F32),
    ]
    if last:
        scratch.append(pltpu.VMEM((65, 40, BLOCK), F32))
    (out,) = call(
        functools.partial(attend_kernel, stage, len(pieces), carry is not None),
        [shaped((4, 528, BLOCK) if last else (65, 40, BLOCK), F32)],
        [q_all, *pieces] + ([] if carry is None else [carry]),
        "attend" + str(stage),
        scalars=(lists,),
        scratch=scratch,
        flops=flops,
    )
    return out


def mix_kernel(part_ref, weight_ref, out_ref):
    total = part_ref[0] + part_ref[1] + part_ref[2] + part_ref[3]
    for m in range(16):
        mixed = (total[m * 32 : (m + 1) * 32, :] / total[512 + m : 513 + m, :]).astype(BF16)
        for peer in range(2):
            out_ref[(m // 4) * 2 + peer, (m % 4) * 32 : (m % 4) * 32 + 32, :] = mixed


def final_kernel(place_ref, mixed_ref, w_mine_ref, w_other_ref, base_ref, out_ref):
    side = place_ref[0]
    columns = pl.ds(pl.multiple_of(side * BLOCK, BLOCK), BLOCK)
    mine, other = w_mine_ref[:, columns], w_other_ref[:, columns]
    halves = (jnp.where(side == 0, mine, other), jnp.where(side == 0, other, mine))
    weight = jnp.concatenate([h[x * 32 : x * 32 + 32, :] for x in range(4) for h in halves], axis=0)
    for block in range(BLK_DEV):
        rows = slice(block * BLOCK, (block + 1) * BLOCK)
        mixed = jnp.concatenate([mixed_ref[k, block * 32 : block * 32 + 32, :] for k in range(8)], axis=0)
        out_ref[rows, :] = (base_ref[rows, :] + dot(mixed, weight, TN)).astype(BF16)


def shaped(shape, dtype):
    return jax.ShapeDtypeStruct(shape, dtype)


def body(cells, w_query, w_key, w_value, w_source, w_target, msg_bias, w_out, nbr_block, edge_src, key_blocks):
    rows = cells.shape[0]
    everyone = ("zh", "y", "x", "c")
    nparts = 128
    mine = lax.axis_index(everyone)
    side = lax.axis_index("h")
    swap = [(0, 1), (1, 0)]
    ring = [[(i, (i + d) % 4) for i in range(4)] for d in range(4)]
    other = lax.ppermute(cells, "h", swap)
    w_got = lax.ppermute(w_out, "h", swap)
    sides = side.reshape(1)
    places = jnp.stack([side, lax.axis_index("zh"), lax.axis_index("c"), lax.axis_index("x")])
    partial, rest, codes = call(
        prepare_kernel,
        [shaped((3, BLOCK, rows), F32), shaped((3, BLOCK, BLOCK), BF16), shaped((16, BLOCK), BF16)],
        [cells, w_key, w_value, w_query, key_blocks],
        "prepare",
        scalars=(places,),
    )
    own, *sends = call(
        keyval_kernel,
        [shaped((256, BLOCK), BF16)] * 4,
        [partial, rest, other],
        "keyval",
        scalars=(places,),
        scratch=[pltpu.VMEM((4, 256, BLOCK), BF16)],
    )
    got = [lax.ppermute(v, "x", ring[d + 1]) for d, v in enumerate(sends)]
    (here,) = call(gather_kernel, [shaped((4, 256, BLOCK), BF16)], [own, *got], "gather", scalars=(places,))
    left = lax.ppermute(here, "zh", ring[1])
    right = lax.ppermute(here, "zh", ring[3])
    mate_here = lax.ppermute(here, "c", swap)
    (query,) = call(
        query_kernel, [shaped((16, 144, BLOCK), BF16)], [partial, rest, other, codes], "query", after=got
    )
    q_all = lax.all_to_all(query, ("y", "x"), 0, 0).reshape(4, 4, 144, BLOCK)
    lists = lax.dynamic_slice_in_dim(q_all, BLOCK + 2 * lax.axis_index("y"), 2, 2)
    lists = jnp.pad(lists.reshape(32, BLOCK).astype(jnp.int32), ((0, 8), (0, 0)), constant_values=EMPTY)
    partial = attend(0, lists, q_all, [here, mate_here], None, 10**6)
    shapes = [shaped((n, 256, BLOCK), BF16) for n in (2, 2, 8)]
    low, high, both = call(relay_kernel, shapes, [left, right], "relay", after=[partial])
    far_low = lax.ppermute(low, "zh", ring[1])
    far_high = lax.ppermute(high, "zh", ring[3])
    partial = attend(1, lists, q_all, [both, lax.ppermute(both, "c", swap)], partial, 9 * 10**9)
    (across,) = call(pass_kernel, [shaped((4, 256, BLOCK), BF16)], [far_low, far_high], "across", after=[partial])
    partial = attend(2, lists, q_all, [across, lax.ppermute(across, "c", swap)], partial, 5 * 10**9)
    source, target = call(
        source_kernel,
        [shaped((rows, 256), BF16), shaped((rows, 256), F32)],
        [cells, other, w_source, w_target, msg_bias],
        "source",
        scalars=(sides,),
        after=[partial],
    )
    up = [(i, (i + 1) % nparts) for i in range(nparts)]
    before = lax.ppermute(source, everyone, up)
    after = lax.ppermute(source, everyone, [(j, i) for i, j in up])
    window_block = (nbr_block // BLK_DEV - mine + 1) % nparts * BLK_DEV + nbr_block % BLK_DEV
    (base,) = call(
        edge_kernel,
        [shaped((rows, BLOCK), F32)],
        [before, source, after, target, edge_src, cells],
        "edge",
        scalars=(window_block,),
        scratch=[pltpu.VMEM((12, BLOCK, 256), BF16)],
        flops=3 * 10**9,
        trans=10**6,
    )
    (mixed,) = call(mix_kernel, [shaped((8, BLOCK, BLOCK), BF16)], [lax.all_to_all(partial, "y", 0, 0)], "mix", after=[w_got])
    mixed = lax.all_to_all(mixed, ("x", "h"), 0, 0)
    (out,) = call(
        final_kernel, [shaped((rows, BLOCK), BF16)], [mixed, w_out, w_got, base], "final", scalars=(places,)
    )
    return out


def solution(mesh):
    split = Mesh(mesh.devices.reshape(4, 4, 4, 2, 2), ("zh", "y", "x", "c", "h"))
    blk = ("zh", "y", "x", "c")
    in_specs = (
        P(blk, "h"),
        P(None, "h"),
        P(None, "h"),
        P(None, "h"),
        P(None, None, "h"),
        P(None, None, "h"),
        P(None, "h"),
        P("h", None),
        P(blk, None),
        P(blk, None),
        P(blk, None),
    )
    return jax.shard_map(body, mesh=split, in_specs=in_specs, out_specs=P(blk, "h"), check_vma=False)
```

time: 1120 us -> 106 us (0.09)
  the two profiles are of different devices: /device:TPU:8 before, /device:TPU:24 now
where the time goes in v1:
time: 106 us
  starting transfers between devices  42.7 us (40%)
  Pallas kernels  33.7 us (32%)
  waiting for transfers between devices  24.5 us (23%)
  local copies, waits for them, and re-layouts  4.27 us (4%)
    pallas_call x13, Pallas kernels, call(): pl.pallas_call(kernel, grid_spec=pltpu.PrefetchScalarGridSpec(num_scalar_...  33.7 us
    all_to_all x1, starting transfers between devices, body(): mixed = lax.all_to_all(mixed, ('x', 'h'), 0, 0)  9.4 us
    all_to_all x1, waiting for transfers between devices, body(): lax.all_to_all(partial, 'y', 0, 0)  8.7 us
    all_to_all x1, starting transfers between devices, body(): q_all = lax.all_to_all(query, ('y', 'x'), 0, 0).reshape(4, 4, 144, BLOCK)  6.79 us
    ppermute x3, starting transfers between devices, body(): got = [lax.ppermute(v, 'x', ring[d + 1]) for d, v in enumerate(sends)]  5.73 us
    all_to_all x1, starting transfers between devices, body(): lax.all_to_all(partial, 'y', 0, 0)  4.65 us
    ppermute x1, waiting for transfers between devices, body(): right = lax.ppermute(here, 'zh', ring[3])  4.54 us
    all_to_all x1, waiting for transfers between devices, body(): mixed = lax.all_to_all(mixed, ('x', 'h'), 0, 0)  4.29 us
  transfers between devices with their start and end apart: 17, of which 9 were waited for; matrix products, arithmetic and copies ran while one was open for 0% of the time, Pallas kernels for 21%

profile of v1, /device:TPU:24, one launch (start us, length us, event | category | flops | bytes accessed | tf_op | source)
XLA Modules:
  0.0 105.6 jit_solution(13255589641304828503)
XLA Ops:
  0.0 1.9 %collective-permute-start = (bf16[512,128]{1,0:T(8,128)(2,1)}, bf16[512,128]{1,0:T(8,128)(2,1)S(1)}, u32[]{:S(2)}, u32[]{:S(2)}) collective-permute-start(bf16[512,128]{1,0:T(8,128)(2,1)} %cells_ref.3), channel_id=1, source_target_pairs={{0,1},{1,0},{2,3},{3,2},{4,5},{5,4},{6,7},{7,6},{8,9},{9,8},{10,11... | collective-permute-start | bytes 393224 | tf_op jit(solution)/shard_map/ppermute | solution.py:306
  6.1 1.2 %prepare.1 = (f32[3,128,512]{2,1,0:T(8,128)S(1)}, bf16[3,128,128]{2,1,0:T(8,128)(2,1)S(1)}, bf16[16,128]{1,0:T(8,128)(2,1)S(1)}) custom-call(s32[4]{0:T(128)S(1)} %pad_add_fusion.place_ref, bf16[512,128]{1,0:T(8,128)(2,1)S(1)} %copy-done, bf16[256,128]{1,0:T(8,128)(2,1)S(1)} %copy-done.4, bf16[256,128]{1,0:T(8,128)(2,1)S(1)} %copy-done.5, ...), custom_call_target="tpu_custom_call" | custom-call | flops 1000000 | bytes 328192 | tf_op jit(solution)/shard_map/prepare/pallas_call | solution.py:38
  8.1 1.6 %collective-permute-start.1 = (bf16[256,128]{1,0:T(8,128)(2,1)S(1)}, bf16[256,128]{1,0:T(8,128)(2,1)S(1)}, u32[]{:S(2)}, u32[]{:S(2)}) collective-permute-start(bf16[256,128]{1,0:T(8,128)(2,1)S(1)} %get-tuple-element.20), channel_id=1, source_target_pairs={{0,4},{4,8},{8,12},{12,0},{1,5},{5,9},{9,13},{13,1},{2,6},{6,10},{... | collective-permute-start | bytes 196616 | tf_op jit(solution)/shard_map/ppermute | solution.py:325
  9.6 2.7 %collective-permute-start.2 = (bf16[256,128]{1,0:T(8,128)(2,1)S(1)}, bf16[256,128]{1,0:T(8,128)(2,1)S(1)}, u32[]{:S(2)}, u32[]{:S(2)}) collective-permute-start(bf16[256,128]{1,0:T(8,128)(2,1)S(1)} %get-tuple-element.21), channel_id=1, source_target_pairs={{0,8},{4,12},{8,0},{12,4},{1,9},{5,13},{9,1},{13,5},{2,10},{6,14},... | collective-permute-start | bytes 196616 | tf_op jit(solution)/shard_map/ppermute | solution.py:325
  12.4 1.4 %collective-permute-start.3 = (bf16[256,128]{1,0:T(8,128)(2,1)S(1)}, bf16[256,128]{1,0:T(8,128)(2,1)S(1)}, u32[]{:S(2)}, u32[]{:S(2)}) collective-permute-start(bf16[256,128]{1,0:T(8,128)(2,1)S(1)} %get-tuple-element.22), channel_id=1, source_target_pairs={{0,12},{4,0},{8,4},{12,8},{1,13},{5,1},{9,5},{13,9},{2,14},{6,2},{... | collective-permute-start | bytes 196616 | tf_op jit(solution)/shard_map/ppermute | solution.py:325
  14.3 1.1 %collective-permute-done.2.got1_ref.refs_1_ = bf16[256,128]{1,0:T(8,128)(2,1)S(1)} collective-permute-done((bf16[256,128]{1,0:T(8,128)(2,1)S(1)}, bf16[256,128]{1,0:T(8,128)(2,1)S(1)}, u32[]{:S(2)}, u32[]{:S(2)}) %collective-permute-start.2) | collective-permute-done | bytes 65568 | tf_op jit(solution)/shard_map/ppermute | solution.py:325
  15.4 1.2 %collective-permute-done.3.got2_ref.refs_2_ = bf16[256,128]{1,0:T(8,128)(2,1)S(1)} collective-permute-done((bf16[256,128]{1,0:T(8,128)(2,1)S(1)}, bf16[256,128]{1,0:T(8,128)(2,1)S(1)}, u32[]{:S(2)}, u32[]{:S(2)}) %collective-permute-start.3) | collective-permute-done | bytes 65568 | tf_op jit(solution)/shard_map/ppermute | solution.py:325
  17.6 6.8 %all-to-all-start = ((bf16[16,144,128]{2,1,0:T(8,128)(2,1)}), bf16[16,144,128]{2,1,0:T(8,128)(2,1)S(1)}, u32[]{:S(2)}, u32[]{:S(2)}) async-start(bf16[16,144,128]{2,1,0:T(8,128)(2,1)} %query.1), calls=%async_computation | async-start | bytes 1179648 | tf_op jit(solution)/shard_map/all_to_all | solution.py:333
  25.1 3.4 %collective-permute-start.4 = (bf16[4,256,128]{2,1,0:T(8,128)(2,1)S(1)}, bf16[4,256,128]{2,1,0:T(8,128)(2,1)S(1)}, u32[]{:S(2)}, u32[]{:S(2)}) collective-permute-start(bf16[4,256,128]{2,1,0:T(8,128)(2,1)S(1)} %gather.1.refs_0_), channel_id=1, source_target_pairs={{0,64},{64,128},{128,192},{192,0},{1,65},{65,129},{129,193},{193,1... | collective-permute-start | bytes 786440 | tf_op jit(solution)/shard_map/ppermute | solution.py:327
  28.5 2.2 %collective-permute-start.5 = (bf16[4,256,128]{2,1,0:T(8,128)(2,1)S(1)}, bf16[4,256,128]{2,1,0:T(8,128)(2,1)S(1)}, u32[]{:S(2)}, u32[]{:S(2)}) collective-permute-start(bf16[4,256,128]{2,1,0:T(8,128)(2,1)S(1)} %gather.1.refs_0_), channel_id=1, source_target_pairs={{0,192},{64,0},{128,64},{192,128},{1,193},{65,1},{129,65},{193,129... | collective-permute-start | bytes 786440 | tf_op jit(solution)/shard_map/ppermute | solution.py:328
  30.7 2.4 %all-to-all-done = bf16[16,144,128]{2,1,0:T(8,128)(2,1)S(1)} async-done(((bf16[16,144,128]{2,1,0:T(8,128)(2,1)}), bf16[16,144,128]{2,1,0:T(8,128)(2,1)S(1)}, u32[]{:S(2)}, u32[]{:S(2)}) %all-to-all-start) | async-done | bytes 589856 | tf_op jit(solution)/shard_map/all_to_all | solution.py:333
  33.2 6.4 %attend0.1.after_ref.refs_2_ = f32[65,40,128]{2,1,0:T(8,128)S(1)} custom-call(s32[40,128]{1,0:T(8,128)S(1)} %pad_convert_fusion.list_ref, bf16[4,4,144,128]{3,2,1,0:T(8,128)(2,1)S(1)} %bitcast.7, bf16[4,256,128]{2,1,0:T(8,128)(2,1)S(1)} %gather.1.refs_0_, bf16[4,256,128]{2,1,0:T(8,128)(2,1)S(1)} %collective-permute-done.6.refs_1_), custom_call_target="tpu_custom_call" | custom-call | flops 1000000 | bytes 1114112 | tf_op jit(solution)/shard_map/attend0/pallas_call | solution.py:38
  39.7 4.5 %collective-permute-done.5.right_ref = bf16[4,256,128]{2,1,0:T(8,128)(2,1)S(1)} collective-permute-done((bf16[4,256,128]{2,1,0:T(8,128)(2,1)S(1)}, bf16[4,256,128]{2,1,0:T(8,128)(2,1)S(1)}, u32[]{:S(2)}, u32[]{:S(2)}) %collective-permute-start.5) | collective-permute-done | bytes 262176 | tf_op jit(solution)/shard_map/ppermute | solution.py:328
  44.5 3.8 %collective-permute-start.7 = (bf16[2,256,128]{2,1,0:T(8,128)(2,1)S(1)}, bf16[2,256,128]{2,1,0:T(8,128)(2,1)S(1)}, u32[]{:S(2)}, u32[]{:S(2)}) collective-permute-start(bf16[2,256,128]{2,1,0:T(8,128)(2,1)S(1)} %get-tuple-element.24), channel_id=1, source_target_pairs={{0,64},{64,128},{128,192},{192,0},{1,65},{65,129},{129,193},{193,1... | collective-permute-start | bytes 393224 | tf_op jit(solution)/shard_map/ppermute | solution.py:339
  48.7 10.0 %attend1.1.after_ref.refs_2_ = f32[65,40,128]{2,1,0:T(8,128)S(1)} custom-call(s32[40,128]{1,0:T(8,128)S(1)} %pad_convert_fusion.list_ref, bf16[4,4,144,128]{3,2,1,0:T(8,128)(2,1)S(1)} %bitcast.8, bf16[8,256,128]{2,1,0:T(8,128)(2,1)S(1)} %get-tuple-element.26.refs_0_, bf16[8,256,128]{2,1,0:T(8,128)(2,1)S(1)} %collective-permute-done.9.refs_1_, ...), custom_call_target="tpu_custom_call" | custom-call | flops 8999999488 | bytes 2969600 | tf_op jit(solution)/shard_map/attend1/pallas_call | solution.py:38
  58.8 1.5 %collective-permute-done.10.refs_1_ = bf16[4,256,128]{2,1,0:T(8,128)(2,1)S(1)} collective-permute-done((bf16[4,256,128]{2,1,0:T(8,128)(2,1)S(1)}, bf16[4,256,128]{2,1,0:T(8,128)(2,1)S(1)}, u32[]{:S(2)}, u32[]{:S(2)}) %collective-permute-start.10) | collective-permute-done | bytes 262176 | tf_op jit(solution)/shard_map/ppermute | solution.py:343
  60.3 8.1 %attend2.1.after_ref = f32[4,528,128]{2,1,0:T(8,128)} custom-call(s32[40,128]{1,0:T(8,128)S(1)} %pad_convert_fusion.list_ref, bf16[4,4,144,128]{3,2,1,0:T(8,128)(2,1)S(1)} %bitcast.9, bf16[4,256,128]{2,1,0:T(8,128)(2,1)S(1)} %across.1.refs_0_, bf16[4,256,128]{2,1,0:T(8,128)(2,1)S(1)} %collective-permute-done.10.refs_1_, ...), custom_call_target="tpu_custom_call" | custom-call | flops 5000000000 | bytes 2445312 | tf_op jit(solution)/shard_map/attend2/pallas_call | solution.py:38
  68.5 4.6 %all-to-all-start.1 = ((f32[4,528,128]{2,1,0:T(8,128)}), f32[4,528,128]{2,1,0:T(8,128)S(1)}, u32[]{:S(2)}, u32[]{:S(2)}) async-start(f32[4,528,128]{2,1,0:T(8,128)} %attend2.1.after_ref), calls=%async_computation.1 | async-start | bytes 2162688 | tf_op jit(solution)/shard_map/all_to_all | solution.py:366
  74.0 3.8 %collective-permute-start.13 = (bf16[512,256]{1,0:T(8,128)(2,1)S(1)}, bf16[512,256]{1,0:T(8,128)(2,1)S(1)}, u32[]{:S(2)}, u32[]{:S(2)}) collective-permute-start(bf16[512,256]{1,0:T(8,128)(2,1)S(1)} %get-tuple-element.27.own_ref), channel_id=1, source_target_pairs={{2,0},{4,2},{6,4},{8,6},{10,8},{12,10},{14,12},{16,14},{18,16},{20... | collective-permute-start | bytes 786440 | tf_op jit(solution)/shard_map/ppermute | solution.py:354
  78.0 8.7 %all-to-all-done.1.part_ref = f32[4,528,128]{2,1,0:T(8,128)S(1)} async-done(((f32[4,528,128]{2,1,0:T(8,128)}), f32[4,528,128]{2,1,0:T(8,128)S(1)}, u32[]{:S(2)}, u32[]{:S(2)}) %all-to-all-start.1) | async-done | bytes 1081376 | tf_op jit(solution)/shard_map/all_to_all | solution.py:366
  87.4 9.4 %all-to-all-start.2 = ((bf16[8,128,128]{2,1,0:T(8,128)(2,1)}), bf16[8,128,128]{2,1,0:T(8,128)(2,1)S(1)}, u32[]{:S(2)}, u32[]{:S(2)}) async-start(bf16[8,128,128]{2,1,0:T(8,128)(2,1)} %mix.1), calls=%async_computation.2 | async-start | bytes 524288 | tf_op jit(solution)/shard_map/all_to_all | solution.py:367
  96.9 2.9 %edge.1.base_ref = f32[512,128]{1,0:T(8,128)S(1)} custom-call(s32[4,4]{1,0:T(4,128)S(1)} %fusion.4.wb_ref, bf16[512,256]{1,0:T(8,128)(2,1)S(1)} %collective-permute-done.12.before_ref, bf16[512,256]{1,0:T(8,128)(2,1)S(1)} %get-tuple-element.27.own_ref, bf16[512,256]{1,0:T(8,128)(2,1)S(1)} %collective-permute-done.13.after_ref, ...), custom_call_target="tpu_custom_call" | custom-call | flops 3000000000 | bytes 1458176 | tf_op jit(solution)/shard_map/edge/pallas_call | solution.py:38
  99.8 4.3 %all-to-all-done.2.mixed_ref = bf16[8,128,128]{2,1,0:T(8,128)(2,1)S(1)} async-done(((bf16[8,128,128]{2,1,0:T(8,128)(2,1)}), bf16[8,128,128]{2,1,0:T(8,128)(2,1)S(1)}, u32[]{:S(2)}, u32[]{:S(2)}) %all-to-all-start.2) | async-done | bytes 262176 | tf_op jit(solution)/shard_map/all_to_all | solution.py:367
  104.1 1.5 %final.1 = bf16[512,128]{1,0:T(8,128)(2,1)} custom-call(s32[4]{0:T(128)S(1)} %pad_add_fusion.place_ref, bf16[8,128,128]{2,1,0:T(8,128)(2,1)S(1)} %all-to-all-done.2.mixed_ref, bf16[128,256]{1,0:T(8,128)(2,1)S(1)} %copy-done.7, bf16[128,256]{1,0:T(8,128)(2,1)S(1)} %collective-permute-done.11.weight_ref.w_other_ref, f32[512,128]{1,0:T(8,128)S(1)} %edge.1.base_ref), custom_call_target="tpu_custom_call" | custom-call | flops 1000000 | bytes 655360 | tf_op jit(solution)/shard_map/final/pallas_call | solution.py:38
  (52 shorter events, 9.7 us)
Async XLA Ops:
  0.0 7.3 %collective-permute-start = (bf16[512,128]{1,0:T(8,128)(2,1)}, bf16[512,128]{1,0:T(8,128)(2,1)S(1)}, u32[]{:S(2)}, u32[]{:S(2)}) collective-permute-start(bf16[512,128]{1,0:T(8,128)(2,1)} %cells_ref.3), channel_id=1, source_target_pairs={{0,1},{1,0},{2,3},{3,2},{4,5},{5,4},{6,7},{7,6},{8,9},{9,8},{10,11... | collective-permute-start | bytes 393224 | tf_op jit(solution)/shard_map/ppermute | solution.py:306
  8.1 6.3 %collective-permute-start.1 = (bf16[256,128]{1,0:T(8,128)(2,1)S(1)}, bf16[256,128]{1,0:T(8,128)(2,1)S(1)}, u32[]{:S(2)}, u32[]{:S(2)}) collective-permute-start(bf16[256,128]{1,0:T(8,128)(2,1)S(1)} %get-tuple-element.20), channel_id=1, source_target_pairs={{0,4},{4,8},{8,12},{12,0},{1,5},{5,9},{9,13},{13,1},{2,6},{6,10},{... | collective-permute-start | bytes 196616 | tf_op jit(solution)/shard_map/ppermute | solution.py:325
  9.6 5.8 %collective-permute-start.2 = (bf16[256,128]{1,0:T(8,128)(2,1)S(1)}, bf16[256,128]{1,0:T(8,128)(2,1)S(1)}, u32[]{:S(2)}, u32[]{:S(2)}) collective-permute-start(bf16[256,128]{1,0:T(8,128)(2,1)S(1)} %get-tuple-element.21), channel_id=1, source_target_pairs={{0,8},{4,12},{8,0},{12,4},{1,9},{5,13},{9,1},{13,5},{2,10},{6,14},... | collective-permute-start | bytes 196616 | tf_op jit(solution)/shard_map/ppermute | solution.py:325
  12.4 4.3 %collective-permute-start.3 = (bf16[256,128]{1,0:T(8,128)(2,1)S(1)}, bf16[256,128]{1,0:T(8,128)(2,1)S(1)}, u32[]{:S(2)}, u32[]{:S(2)}) collective-permute-start(bf16[256,128]{1,0:T(8,128)(2,1)S(1)} %get-tuple-element.22), channel_id=1, source_target_pairs={{0,12},{4,0},{8,4},{12,8},{1,13},{5,1},{9,5},{13,9},{2,14},{6,2},{... | collective-permute-start | bytes 196616 | tf_op jit(solution)/shard_map/ppermute | solution.py:325
  17.6 15.5 %all-to-all-start = ((bf16[16,144,128]{2,1,0:T(8,128)(2,1)}), bf16[16,144,128]{2,1,0:T(8,128)(2,1)S(1)}, u32[]{:S(2)}, u32[]{:S(2)}) async-start(bf16[16,144,128]{2,1,0:T(8,128)(2,1)} %query.1), calls=%async_computation | async-start | bytes 1179648 | tf_op jit(solution)/shard_map/all_to_all | solution.py:333
  25.0 8.1 %collective-permute-start.6 = (bf16[4,256,128]{2,1,0:T(8,128)(2,1)S(1)}, bf16[4,256,128]{2,1,0:T(8,128)(2,1)S(1)}, u32[]{:S(2)}, u32[]{:S(2)}) collective-permute-start(bf16[4,256,128]{2,1,0:T(8,128)(2,1)S(1)} %gather.1.refs_0_), channel_id=1, source_target_pairs={{0,2},{2,0},{1,3},{3,1},{4,6},{6,4},{5,7},{7,5},{8,10},{10,8},{9,1... | collective-permute-start | bytes 786440 | tf_op jit(solution)/shard_map/ppermute | solution.py:329
  25.1 14.6 %collective-permute-start.4 = (bf16[4,256,128]{2,1,0:T(8,128)(2,1)S(1)}, bf16[4,256,128]{2,1,0:T(8,128)(2,1)S(1)}, u32[]{:S(2)}, u32[]{:S(2)}) collective-permute-start(bf16[4,256,128]{2,1,0:T(8,128)(2,1)S(1)} %gather.1.refs_0_), channel_id=1, source_target_pairs={{0,64},{64,128},{128,192},{192,0},{1,65},{65,129},{129,193},{193,1... | collective-permute-start | bytes 786440 | tf_op jit(solution)/shard_map/ppermute | solution.py:327
  28.5 15.8 %collective-permute-start.5 = (bf16[4,256,128]{2,1,0:T(8,128)(2,1)S(1)}, bf16[4,256,128]{2,1,0:T(8,128)(2,1)S(1)}, u32[]{:S(2)}, u32[]{:S(2)}) collective-permute-start(bf16[4,256,128]{2,1,0:T(8,128)(2,1)S(1)} %gather.1.refs_0_), channel_id=1, source_target_pairs={{0,192},{64,0},{128,64},{192,128},{1,193},{65,1},{129,65},{193,129... | collective-permute-start | bytes 786440 | tf_op jit(solution)/shard_map/ppermute | solution.py:328
  44.4 4.3 %collective-permute-start.9 = (bf16[8,256,128]{2,1,0:T(8,128)(2,1)S(1)}, bf16[8,256,128]{2,1,0:T(8,128)(2,1)S(1)}, u32[]{:S(2)}, u32[]{:S(2)}) collective-permute-start(bf16[8,256,128]{2,1,0:T(8,128)(2,1)S(1)} %get-tuple-element.26.refs_0_), channel_id=1, source_target_pairs={{0,2},{2,0},{1,3},{3,1},{4,6},{6,4},{5,7},{7,5},{8,10},{10,8},{9,1... | collective-permute-start | bytes 1572872 | tf_op jit(solution)/shard_map/ppermute | solution.py:341
  44.5 14.2 %collective-permute-start.7 = (bf16[2,256,128]{2,1,0:T(8,128)(2,1)S(1)}, bf16[2,256,128]{2,1,0:T(8,128)(2,1)S(1)}, u32[]{:S(2)}, u32[]{:S(2)}) collective-permute-start(bf16[2,256,128]{2,1,0:T(8,128)(2,1)S(1)} %get-tuple-element.24), channel_id=1, source_target_pairs={{0,64},{64,128},{128,192},{192,0},{1,65},{65,129},{129,193},{193,1... | collective-permute-start | bytes 393224 | tf_op jit(solution)/shard_map/ppermute | solution.py:339
  48.3 10.4 %collective-permute-start.8 = (bf16[2,256,128]{2,1,0:T(8,128)(2,1)S(1)}, bf16[2,256,128]{2,1,0:T(8,128)(2,1)S(1)}, u32[]{:S(2)}, u32[]{:S(2)}) collective-permute-start(bf16[2,256,128]{2,1,0:T(8,128)(2,1)S(1)} %get-tuple-element.25), channel_id=1, source_target_pairs={{0,192},{64,0},{128,64},{192,128},{1,193},{65,1},{129,65},{193,129... | collective-permute-start | bytes 393224 | tf_op jit(solution)/shard_map/ppermute | solution.py:340
  58.7 1.6 %collective-permute-start.10 = (bf16[4,256,128]{2,1,0:T(8,128)(2,1)S(1)}, bf16[4,256,128]{2,1,0:T(8,128)(2,1)S(1)}, u32[]{:S(2)}, u32[]{:S(2)}) collective-permute-start(bf16[4,256,128]{2,1,0:T(8,128)(2,1)S(1)} %across.1.refs_0_), channel_id=1, source_target_pairs={{0,2},{2,0},{1,3},{3,1},{4,6},{6,4},{5,7},{7,5},{8,10},{10,8},{9,1... | collective-permute-start | bytes 786440 | tf_op jit(solution)/shard_map/ppermute | solution.py:343
  68.5 4.7 %copy-start.7 = (bf16[128,256]{1,0:T(8,128)(2,1)S(1)}, bf16[128,256]{1,0:T(8,128)(2,1)}, u32[]{:S(2)}) copy-start(bf16[128,256]{1,0:T(8,128)(2,1)} %w_mine_ref.1) | copy-start | bytes 196612
  68.5 4.9 %copy-start.1 = (bf16[512,128]{1,0:T(8,128)(2,1)S(1)}, bf16[512,128]{1,0:T(8,128)(2,1)}, u32[]{:S(2)}) copy-start(bf16[512,128]{1,0:T(8,128)(2,1)} %cells_ref.3) | copy-start | bytes 393220
  68.5 4.9 %copy-start.2 = (bf16[2,256,128]{2,1,0:T(8,128)(2,1)S(1)}, bf16[2,256,128]{2,1,0:T(8,128)(2,1)}, u32[]{:S(2)}) copy-start(bf16[2,256,128]{2,1,0:T(8,128)(2,1)} %ws_ref.1) | copy-start | bytes 393220
  68.5 4.9 %copy-start.3 = (bf16[2,256,128]{2,1,0:T(8,128)(2,1)S(1)}, bf16[2,256,128]{2,1,0:T(8,128)(2,1)}, u32[]{:S(2)}) copy-start(bf16[2,256,128]{2,1,0:T(8,128)(2,1)} %wt_ref.1) | copy-start | bytes 393220
  68.5 4.9 %copy-start.9 = (f32[2,128]{1,0:T(2,128)S(1)}, f32[2,128]{1,0:T(2,128)}, u32[]{:S(2)}) copy-start(f32[2,128]{1,0:T(2,128)} %bias_ref.1) | copy-start | bytes 3076
  68.5 18.2 %all-to-all-start.1 = ((f32[4,528,128]{2,1,0:T(8,128)}), f32[4,528,128]{2,1,0:T(8,128)S(1)}, u32[]{:S(2)}, u32[]{:S(2)}) async-start(f32[4,528,128]{2,1,0:T(8,128)} %attend2.1.after_ref), calls=%async_computation.1 | async-start | bytes 2162688 | tf_op jit(solution)/shard_map/all_to_all | solution.py:366
  73.1 4.7 %copy-start.10 = (s32[512,8]{0,1:T(8,128)S(1)}, s32[512,8]{0,1:T(8,128)}, u32[]{:S(2)}) copy-start(s32[512,8]{0,1:T(8,128)} %param.20) | copy-start | bytes 49156
  73.1 4.8 %collective-permute-start.11 = (bf16[128,256]{1,0:T(8,128)(2,1)S(1)}, bf16[128,256]{1,0:T(8,128)(2,1)S(1)}, u32[]{:S(2)}, u32[]{:S(2)}) collective-permute-start(bf16[128,256]{1,0:T(8,128)(2,1)S(1)} %copy-done.7), channel_id=1, source_target_pairs={{0,1},{1,0},{2,3},{3,2},{4,5},{5,4},{6,7},{7,6},{8,9},{9,8},{10,11... | collective-permute-start | bytes 196616 | tf_op jit(solution)/shard_map/ppermute | solution.py:307
  73.9 22.9 %copy-start.11 = (s32[4,4]{1,0:T(4,128)S(1)}, s32[4,4]{1,0:T(4,128)}, u32[]{:S(2)}) copy-start(s32[4,4]{1,0:T(4,128)} %param.19) | copy-start | bytes 196
  73.9 23.0 %collective-permute-start.12 = (bf16[512,256]{1,0:T(8,128)(2,1)S(1)}, bf16[512,256]{1,0:T(8,128)(2,1)S(1)}, u32[]{:S(2)}, u32[]{:S(2)}) collective-permute-start(bf16[512,256]{1,0:T(8,128)(2,1)S(1)} %get-tuple-element.27.own_ref), channel_id=1, source_target_pairs={{0,2},{2,4},{4,6},{6,8},{8,10},{10,12},{12,14},{14,16},{16,18},{18... | collective-permute-start | bytes 786440 | tf_op jit(solution)/shard_map/ppermute | solution.py:353
  74.0 22.9 %collective-permute-start.13 = (bf16[512,256]{1,0:T(8,128)(2,1)S(1)}, bf16[512,256]{1,0:T(8,128)(2,1)S(1)}, u32[]{:S(2)}, u32[]{:S(2)}) collective-permute-start(bf16[512,256]{1,0:T(8,128)(2,1)S(1)} %get-tuple-element.27.own_ref), channel_id=1, source_target_pairs={{2,0},{4,2},{6,4},{8,6},{10,8},{12,10},{14,12},{16,14},{18,16},{20... | collective-permute-start | bytes 786440 | tf_op jit(solution)/shard_map/ppermute | solution.py:354
  87.4 16.7 %all-to-all-start.2 = ((bf16[8,128,128]{2,1,0:T(8,128)(2,1)}), bf16[8,128,128]{2,1,0:T(8,128)(2,1)S(1)}, u32[]{:S(2)}, u32[]{:S(2)}) async-start(bf16[8,128,128]{2,1,0:T(8,128)(2,1)} %mix.1), calls=%async_computation.2 | async-start | bytes 524288 | tf_op jit(solution)/shard_map/all_to_all | solution.py:367
  (5 other events, 4.1 us)

commit v2 on v1

--- a/solution.py
+++ b/solution.py
@@ -51,9 +51,8 @@
     )(*scalars, *args, *after)
 
 
-def whole_rows(side_ref, own_ref, other_ref):
-    own, other = own_ref[...], other_ref[...]
-    first = side_ref[0] == 0
+def whole_rows(side, own, other):
+    first = side == 0
     return jnp.concatenate([jnp.where(first, own, other), jnp.where(first, other, own)], axis=1)
 
 
@@ -98,7 +97,7 @@
     codes_ref[...] = jnp.concatenate(rows + [jnp.zeros((8, BLOCK), F32)], axis=0).astype(BF16)
 
 
-def keyval_kernel(place_ref, partial_ref, rest_ref, other_ref, own_ref, *outs):
+def keyval_kernel(place_ref, partial_ref, rest_ref, other_ref, up_ref, down_ref, own_ref, *outs):
     *sends, keyval = outs
     other = other_ref[...]
     for n in range(2):
@@ -141,24 +140,44 @@
     out_ref[2:] = high_ref[...]
 
 
-def source_kernel(side_ref, own_ref, other_ref, ws_ref, wt_ref, bias_ref, after_ref, source_ref, target_ref):
-    whole = whole_rows(side_ref, own_ref, other_ref)
+def ends_kernel(place_ref, cells_ref, up_ref, down_ref, wait_ref, before_ref, after_ref):
+    spot = place_ref[4] * 8 + place_ref[3] * 2 + place_ref[2]
+    cells = cells_ref[...]
+    before_ref[...] = jnp.where(spot == 31, up_ref[...], cells)
+    after_ref[...] = jnp.where(spot == 0, down_ref[...], cells)
+
+
+def pair_kernel(before_ref, after_ref, out_ref):
+    rows = before_ref.shape[0]
+    out_ref[:rows, :] = before_ref[...]
+    out_ref[rows:, :] = after_ref[...]
+
+
+def edge_kernel(
+    wb_ref, place_ref, own_ref, other_ref, near_ref, near_other_ref, ws_ref, wt_ref, bias_ref, edge_ref, out_ref, win, tgt
+):
+    side = place_ref[0]
+    rows = own_ref.shape[0]
+    whole = whole_rows(side, own_ref[...], other_ref[...])
     for g in range(2):
-        cols = slice(g * BLOCK, (g + 1) * BLOCK)
-        source_ref[:, cols] = dot(whole, ws_ref[g], NN).astype(BF16)
-        target_ref[:, cols] = dot(whole, wt_ref[g], NN) + bias_ref[g : g + 1, :]
-
-
-def edge_kernel(wb_ref, before_ref, own_ref, after_ref, target_ref, edge_ref, cells_ref, out_ref, win):
-    for side, ref in enumerate((before_ref, own_ref, after_ref)):
-        for block in range(BLK_DEV):
-            win[side * BLK_DEV + block] = ref[block * BLOCK : (block + 1) * BLOCK, :]
+        tgt[:, g * BLOCK : (g + 1) * BLOCK] = dot(whole, wt_ref[g], NN) + bias_ref[g : g + 1, :]
+    for spot, cells in enumerate(
+        (
+            whole_rows(side, near_ref[:rows, :], near_other_ref[:rows, :]),
+            whole,
+            whole_rows(side, near_ref[rows:, :], near_other_ref[rows:, :]),
+        )
+    ):
+        for g in range(2):
+            source = dot(cells, ws_ref[g], NN).astype(BF16)
+            for block in range(BLK_DEV):
+                win[spot * BLK_DEV + block, :, g * BLOCK : (g + 1) * BLOCK] = source[block * BLOCK : (block + 1) * BLOCK, :]
     lane = lax.broadcasted_iota(jnp.int32, (BLOCK, 4 * BLOCK), 1)
 
     def one(block, unused):
         rows = pl.ds(pl.multiple_of(block * BLOCK, BLOCK), BLOCK)
         table = jnp.concatenate([win[wb_ref[block, k]] for k in range(4)], axis=0)
-        target = target_ref[rows, :]
+        target = tgt[rows, :]
         picks = edge_ref[rows, :]
         total = jnp.zeros((BLOCK, BLOCK), F32)
         for e in range(8):
@@ -167,7 +186,7 @@
             gate = 0.5 + 0.5 * jnp.tanh(0.5 * pre[:, :BLOCK])
             value = pre[:, BLOCK:]
             total = total + gate * (value * (0.5 + 0.5 * jnp.tanh(0.5 * value)))
-        out_ref[rows, :] = cells_ref[rows, :].astype(F32) + total * 0.125
+        out_ref[rows, :] = own_ref[rows, :].astype(F32) + total * 0.125
         return unused
 
     lax.fori_loop(0, BLK_DEV, one, 0)
@@ -279,16 +298,19 @@
             out_ref[(m // 4) * 2 + peer, (m % 4) * 32 : (m % 4) * 32 + 32, :] = mixed
 
 
-def final_kernel(place_ref, mixed_ref, w_mine_ref, w_other_ref, base_ref, out_ref):
+def weight_kernel(place_ref, w_mine_ref, w_other_ref, out_ref):
     side = place_ref[0]
     columns = pl.ds(pl.multiple_of(side * BLOCK, BLOCK), BLOCK)
     mine, other = w_mine_ref[:, columns], w_other_ref[:, columns]
     halves = (jnp.where(side == 0, mine, other), jnp.where(side == 0, other, mine))
-    weight = jnp.concatenate([h[x * 32 : x * 32 + 32, :] for x in range(4) for h in halves], axis=0)
+    out_ref[...] = jnp.concatenate([h[x * 32 : x * 32 + 32, :] for x in range(4) for h in halves], axis=0)
+
+
+def final_kernel(mixed_ref, weight_ref, base_ref, out_ref):
     for block in range(BLK_DEV):
         rows = slice(block * BLOCK, (block + 1) * BLOCK)
         mixed = jnp.concatenate([mixed_ref[k, block * 32 : block * 32 + 32, :] for k in range(8)], axis=0)
-        out_ref[rows, :] = (base_ref[rows, :] + dot(mixed, weight, TN)).astype(BF16)
+        out_ref[rows, :] = (base_ref[rows, :] + dot(mixed, weight_ref[...], TN)).astype(BF16)
 
 
 def shaped(shape, dtype):
@@ -305,8 +327,11 @@
     ring = [[(i, (i + d) % 4) for i in range(4)] for d in range(4)]
     other = lax.ppermute(cells, "h", swap)
     w_got = lax.ppermute(w_out, "h", swap)
-    sides = side.reshape(1)
-    places = jnp.stack([side, lax.axis_index("zh"), lax.axis_index("c"), lax.axis_index("x")])
+    tops = [(z * 32 + 31, (z + 1) % 4 * 32 + 31) for z in range(4)]
+    bottoms = [((z + 1) % 4 * 32, z * 32) for z in range(4)]
+    up = lax.ppermute(cells, everyone, tops)
+    down = lax.ppermute(cells, everyone, bottoms)
+    places = jnp.stack([side, lax.axis_index("zh"), lax.axis_index("c"), lax.axis_index("x"), lax.axis_index("y")])
     partial, rest, codes = call(
         prepare_kernel,
         [shaped((3, BLOCK, rows), F32), shaped((3, BLOCK, BLOCK), BF16), shaped((16, BLOCK), BF16)],
@@ -321,6 +346,7 @@
         "keyval",
         scalars=(places,),
         scratch=[pltpu.VMEM((4, 256, BLOCK), BF16)],
+        after=[up, down],
     )
     got = [lax.ppermute(v, "x", ring[d + 1]) for d, v in enumerate(sends)]
     (here,) = call(gather_kernel, [shaped((4, 256, BLOCK), BF16)], [own, *got], "gather", scalars=(places,))
@@ -341,32 +367,29 @@
     partial = attend(1, lists, q_all, [both, lax.ppermute(both, "c", swap)], partial, 9 * 10**9)
     (across,) = call(pass_kernel, [shaped((4, 256, BLOCK), BF16)], [far_low, far_high], "across", after=[partial])
     partial = attend(2, lists, q_all, [across, lax.ppermute(across, "c", swap)], partial, 5 * 10**9)
-    source, target = call(
-        source_kernel,
-        [shaped((rows, 256), BF16), shaped((rows, 256), F32)],
-        [cells, other, w_source, w_target, msg_bias],
-        "source",
-        scalars=(sides,),
-        after=[partial],
-    )
-    up = [(i, (i + 1) % nparts) for i in range(nparts)]
-    before = lax.ppermute(source, everyone, up)
-    after = lax.ppermute(source, everyone, [(j, i) for i, j in up])
+    plane = [(i, (i + 1) % 32) for i in range(32)]
+    ends = [shaped((rows, BLOCK), BF16)] * 2
+    before, after = call(ends_kernel, ends, [cells, up, down], "ends", scalars=(places,), after=[partial])
+    before = lax.ppermute(before, ("y", "x", "c"), plane)
+    after = lax.ppermute(after, ("y", "x", "c"), [(j, i) for i, j in plane])
+    (around,) = call(pair_kernel, [shaped((2 * rows, BLOCK), BF16)], [before, after], "around")
+    around_other = lax.ppermute(around, "h", swap)
     window_block = (nbr_block // BLK_DEV - mine + 1) % nparts * BLK_DEV + nbr_block % BLK_DEV
     (base,) = call(
         edge_kernel,
         [shaped((rows, BLOCK), F32)],
-        [before, source, after, target, edge_src, cells],
+        [cells, other, around, around_other, w_source, w_target, msg_bias, edge_src],
         "edge",
-        scalars=(window_block,),
-        scratch=[pltpu.VMEM((12, BLOCK, 256), BF16)],
-        flops=3 * 10**9,
+        scalars=(window_block, places),
+        scratch=[pltpu.VMEM((12, BLOCK, 256), BF16), pltpu.VMEM((rows, 256), F32)],
+        flops=4 * 10**9,
         trans=10**6,
     )
-    (mixed,) = call(mix_kernel, [shaped((8, BLOCK, BLOCK), BF16)], [lax.all_to_all(partial, "y", 0, 0)], "mix", after=[w_got])
+    (w_full,) = call(weight_kernel, [shaped((256, BLOCK), BF16)], [w_out, w_got], "weight", scalars=(places,))
+    (mixed,) = call(mix_kernel, [shaped((8, BLOCK, BLOCK), BF16)], [lax.all_to_all(partial, "y", 0, 0)], "mix", after=[w_full])
     mixed = lax.all_to_all(mixed, ("x", "h"), 0, 0)
     (out,) = call(
-        final_kernel, [shaped((rows, BLOCK), BF16)], [mixed, w_out, w_got, base], "final", scalars=(places,)
+        final_kernel, [shaped((rows, BLOCK), BF16)], [mixed, w_full, base], "final"
     )
     return out
 

time: 106 us -> 104 us (0.981)
  the two profiles are of different devices: /device:TPU:24 before, /device:TPU:8 now
where the time goes in v2:
time: 104 us
  starting transfers between devices  42.5 us (41%)
  Pallas kernels  34.6 us (33%)
  waiting for transfers between devices  21.9 us (21%)
  local copies, waits for them, and re-layouts  4.36 us (4%)
    pallas_call x15, Pallas kernels, call(): pl.pallas_call(kernel, grid_spec=pltpu.PrefetchScalarGridSpec(num_scalar_...  34.6 us
    all_to_all x1, starting transfers between devices, body(): q_all = lax.all_to_all(query, ('y', 'x'), 0, 0).reshape(4, 4, 144, BLOCK)  9.32 us
    ppermute x3, starting transfers between devices, body(): got = [lax.ppermute(v, 'x', ring[d + 1]) for d, v in enumerate(sends)]  5.73 us
    all_to_all x1, starting transfers between devices, body(): mixed = lax.all_to_all(mixed, ('x', 'h'), 0, 0)  5.49 us
    all_to_all x1, starting transfers between devices, body(): lax.all_to_all(partial, 'y', 0, 0)  4.93 us
    all_to_all x1, waiting for transfers between devices, body(): lax.all_to_all(partial, 'y', 0, 0)  4.73 us
    unnamed x25, local copies, waits for them, and re-layouts  4.26 us
    all_to_all x1, waiting for transfers between devices, body(): q_all = lax.all_to_all(query, ('y', 'x'), 0, 0).reshape(4, 4, 144, BLOCK)  4.05 us
  transfers between devices with their start and end apart: 20, of which 10 were waited for; matrix products, arithmetic and copies ran while one was open for 0% of the time, Pallas kernels for 23%

profile of v2, /device:TPU:8, one launch (start us, length us, event | category | flops | bytes accessed | tf_op | source)
XLA Modules:
  0.0 103.6 jit_solution(5614297693187726200)
XLA Ops:
  0.0 1.9 %collective-permute-start = (bf16[512,128]{1,0:T(8,128)(2,1)}, bf16[512,128]{1,0:T(8,128)(2,1)S(1)}, u32[]{:S(2)}, u32[]{:S(2)}) collective-permute-start(bf16[512,128]{1,0:T(8,128)(2,1)} %own_ref.1), channel_id=1, source_target_pairs={{0,1},{1,0},{2,3},{3,2},{4,5},{5,4},{6,7},{7,6},{8,9},{9,8},{10,11... | collective-permute-start | bytes 393224 | tf_op jit(solution)/shard_map/ppermute | solution.py:328
  7.5 1.2 %prepare.1 = (f32[3,128,512]{2,1,0:T(8,128)S(1)}, bf16[3,128,128]{2,1,0:T(8,128)(2,1)S(1)}, bf16[16,128]{1,0:T(8,128)(2,1)S(1)}) custom-call(s32[5]{0:T(128)S(1)} %stack.23.place_ref, bf16[512,128]{1,0:T(8,128)(2,1)S(1)} %copy-done, bf16[256,128]{1,0:T(8,128)(2,1)S(1)} %copy-done.2, bf16[256,128]{1,0:T(8,128)(2,1)S(1)} %copy-done.3, ...), custom_call_target="tpu_custom_call" | custom-call | flops 1000000 | bytes 328192 | tf_op jit(solution)/shard_map/prepare/pallas_call | solution.py:38
  9.5 1.6 %collective-permute-start.3 = (bf16[256,128]{1,0:T(8,128)(2,1)S(1)}, bf16[256,128]{1,0:T(8,128)(2,1)S(1)}, u32[]{:S(2)}, u32[]{:S(2)}) collective-permute-start(bf16[256,128]{1,0:T(8,128)(2,1)S(1)} %get-tuple-element.20), channel_id=1, source_target_pairs={{0,4},{4,8},{8,12},{12,0},{1,5},{5,9},{9,13},{13,1},{2,6},{6,10},{... | collective-permute-start | bytes 196616 | tf_op jit(solution)/shard_map/ppermute | solution.py:351
  11.0 2.7 %collective-permute-start.4 = (bf16[256,128]{1,0:T(8,128)(2,1)S(1)}, bf16[256,128]{1,0:T(8,128)(2,1)S(1)}, u32[]{:S(2)}, u32[]{:S(2)}) collective-permute-start(bf16[256,128]{1,0:T(8,128)(2,1)S(1)} %get-tuple-element.21), channel_id=1, source_target_pairs={{0,8},{4,12},{8,0},{12,4},{1,9},{5,13},{9,1},{13,5},{2,10},{6,14},... | collective-permute-start | bytes 196616 | tf_op jit(solution)/shard_map/ppermute | solution.py:351
  13.7 1.4 %collective-permute-start.5 = (bf16[256,128]{1,0:T(8,128)(2,1)S(1)}, bf16[256,128]{1,0:T(8,128)(2,1)S(1)}, u32[]{:S(2)}, u32[]{:S(2)}) collective-permute-start(bf16[256,128]{1,0:T(8,128)(2,1)S(1)} %get-tuple-element.22), channel_id=1, source_target_pairs={{0,12},{4,0},{8,4},{12,8},{1,13},{5,1},{9,5},{13,9},{2,14},{6,2},{... | collective-permute-start | bytes 196616 | tf_op jit(solution)/shard_map/ppermute | solution.py:351
  15.7 1.1 %collective-permute-done.4.got1_ref.refs_1_ = bf16[256,128]{1,0:T(8,128)(2,1)S(1)} collective-permute-done((bf16[256,128]{1,0:T(8,128)(2,1)S(1)}, bf16[256,128]{1,0:T(8,128)(2,1)S(1)}, u32[]{:S(2)}, u32[]{:S(2)}) %collective-permute-start.4) | collective-permute-done | bytes 65568 | tf_op jit(solution)/shard_map/ppermute | solution.py:351
  16.8 1.2 %collective-permute-done.5.got2_ref.refs_2_ = bf16[256,128]{1,0:T(8,128)(2,1)S(1)} collective-permute-done((bf16[256,128]{1,0:T(8,128)(2,1)S(1)}, bf16[256,128]{1,0:T(8,128)(2,1)S(1)}, u32[]{:S(2)}, u32[]{:S(2)}) %collective-permute-start.5) | collective-permute-done | bytes 65568 | tf_op jit(solution)/shard_map/ppermute | solution.py:351
  19.0 9.3 %all-to-all-start = ((bf16[16,144,128]{2,1,0:T(8,128)(2,1)}), bf16[16,144,128]{2,1,0:T(8,128)(2,1)S(1)}, u32[]{:S(2)}, u32[]{:S(2)}) async-start(bf16[16,144,128]{2,1,0:T(8,128)(2,1)} %query.1), calls=%async_computation | async-start | bytes 1179648 | tf_op jit(solution)/shard_map/all_to_all | solution.py:359
  29.0 1.7 %collective-permute-start.6 = (bf16[4,256,128]{2,1,0:T(8,128)(2,1)S(1)}, bf16[4,256,128]{2,1,0:T(8,128)(2,1)S(1)}, u32[]{:S(2)}, u32[]{:S(2)}) collective-permute-start(bf16[4,256,128]{2,1,0:T(8,128)(2,1)S(1)} %gather.1.refs_0_), channel_id=1, source_target_pairs={{0,64},{64,128},{128,192},{192,0},{1,65},{65,129},{129,193},{193,1... | collective-permute-start | bytes 786440 | tf_op jit(solution)/shard_map/ppermute | solution.py:353
  30.8 2.5 %collective-permute-start.7 = (bf16[4,256,128]{2,1,0:T(8,128)(2,1)S(1)}, bf16[4,256,128]{2,1,0:T(8,128)(2,1)S(1)}, u32[]{:S(2)}, u32[]{:S(2)}) collective-permute-start(bf16[4,256,128]{2,1,0:T(8,128)(2,1)S(1)} %gather.1.refs_0_), channel_id=1, source_target_pairs={{0,192},{64,0},{128,64},{192,128},{1,193},{65,1},{129,65},{193,129... | collective-permute-start | bytes 786440 | tf_op jit(solution)/shard_map/ppermute | solution.py:354
  33.2 4.1 %all-to-all-done = bf16[16,144,128]{2,1,0:T(8,128)(2,1)S(1)} async-done(((bf16[16,144,128]{2,1,0:T(8,128)(2,1)}), bf16[16,144,128]{2,1,0:T(8,128)(2,1)S(1)}, u32[]{:S(2)}, u32[]{:S(2)}) %all-to-all-start) | async-done | bytes 589856 | tf_op jit(solution)/shard_map/all_to_all | solution.py:359
  37.3 6.4 %attend0.1.after_ref.refs_2_ = f32[65,40,128]{2,1,0:T(8,128)S(1)} custom-call(s32[40,128]{1,0:T(8,128)S(1)} %pad_convert_fusion.list_ref, bf16[4,4,144,128]{3,2,1,0:T(8,128)(2,1)S(1)} %bitcast.8, bf16[4,256,128]{2,1,0:T(8,128)(2,1)S(1)} %gather.1.refs_0_, bf16[4,256,128]{2,1,0:T(8,128)(2,1)S(1)} %collective-permute-done.8.refs_1_), custom_call_target="tpu_custom_call" | custom-call | flops 1000000 | bytes 1114112 | tf_op jit(solution)/shard_map/attend0/pallas_call | solution.py:38
  43.8 2.2 %collective-permute-done.7.right_ref = bf16[4,256,128]{2,1,0:T(8,128)(2,1)S(1)} collective-permute-done((bf16[4,256,128]{2,1,0:T(8,128)(2,1)S(1)}, bf16[4,256,128]{2,1,0:T(8,128)(2,1)S(1)}, u32[]{:S(2)}, u32[]{:S(2)}) %collective-permute-start.7) | collective-permute-done | bytes 262176 | tf_op jit(solution)/shard_map/ppermute | solution.py:354
  46.1 3.6 %collective-permute-start.9 = (bf16[2,256,128]{2,1,0:T(8,128)(2,1)S(1)}, bf16[2,256,128]{2,1,0:T(8,128)(2,1)S(1)}, u32[]{:S(2)}, u32[]{:S(2)}) collective-permute-start(bf16[2,256,128]{2,1,0:T(8,128)(2,1)S(1)} %get-tuple-element.24), channel_id=1, source_target_pairs={{0,64},{64,128},{128,192},{192,0},{1,65},{65,129},{129,193},{193,1... | collective-permute-start | bytes 393224 | tf_op jit(solution)/shard_map/ppermute | solution.py:365
  50.3 10.3 %attend1.1.after_ref.refs_2_ = f32[65,40,128]{2,1,0:T(8,128)S(1)} custom-call(s32[40,128]{1,0:T(8,128)S(1)} %pad_convert_fusion.list_ref, bf16[4,4,144,128]{3,2,1,0:T(8,128)(2,1)S(1)} %bitcast.9, bf16[8,256,128]{2,1,0:T(8,128)(2,1)S(1)} %get-tuple-element.26.refs_0_, bf16[8,256,128]{2,1,0:T(8,128)(2,1)S(1)} %collective-permute-done.11.refs_1_, ...), custom_call_target="tpu_custom_call" | custom-call | flops 8999999488 | bytes 2969600 | tf_op jit(solution)/shard_map/attend1/pallas_call | solution.py:38
  60.8 1.5 %collective-permute-done.12.refs_1_ = bf16[4,256,128]{2,1,0:T(8,128)(2,1)S(1)} collective-permute-done((bf16[4,256,128]{2,1,0:T(8,128)(2,1)S(1)}, bf16[4,256,128]{2,1,0:T(8,128)(2,1)S(1)}, u32[]{:S(2)}, u32[]{:S(2)}) %collective-permute-start.12) | collective-permute-done | bytes 262176 | tf_op jit(solution)/shard_map/ppermute | solution.py:369
  62.3 7.8 %attend2.1.wait_ref = f32[4,528,128]{2,1,0:T(8,128)} custom-call(s32[40,128]{1,0:T(8,128)S(1)} %pad_convert_fusion.list_ref, bf16[4,4,144,128]{3,2,1,0:T(8,128)(2,1)S(1)} %bitcast.10, bf16[4,256,128]{2,1,0:T(8,128)(2,1)S(1)} %across.1.refs_0_, bf16[4,256,128]{2,1,0:T(8,128)(2,1)S(1)} %collective-permute-done.12.refs_1_, ...), custom_call_target="tpu_custom_call" | custom-call | flops 5000000000 | bytes 2445312 | tf_op jit(solution)/shard_map/attend2/pallas_call | solution.py:38
  70.1 4.9 %all-to-all-start.1 = ((f32[4,528,128]{2,1,0:T(8,128)}), f32[4,528,128]{2,1,0:T(8,128)S(1)}, u32[]{:S(2)}, u32[]{:S(2)}) async-start(f32[4,528,128]{2,1,0:T(8,128)} %attend2.1.wait_ref), calls=%async_computation.1 | async-start | bytes 2162688 | tf_op jit(solution)/shard_map/all_to_all | solution.py:389
  75.8 3.8 %collective-permute-start.15 = (bf16[512,128]{1,0:T(8,128)(2,1)S(1)}, bf16[512,128]{1,0:T(8,128)(2,1)S(1)}, u32[]{:S(2)}, u32[]{:S(2)}) collective-permute-start(bf16[512,128]{1,0:T(8,128)(2,1)S(1)} %get-tuple-element.28), channel_id=1, source_target_pairs={{2,0},{4,2},{6,4},{8,6},{10,8},{12,10},{14,12},{16,14},{18,16},{20... | collective-permute-start | bytes 393224 | tf_op jit(solution)/shard_map/ppermute | solution.py:374
  80.1 2.2 %collective-permute-done.14.before_ref = bf16[512,128]{1,0:T(8,128)(2,1)S(1)} collective-permute-done((bf16[512,128]{1,0:T(8,128)(2,1)S(1)}, bf16[512,128]{1,0:T(8,128)(2,1)S(1)}, u32[]{:S(2)}, u32[]{:S(2)}) %collective-permute-start.14) | collective-permute-done | bytes 131104 | tf_op jit(solution)/shard_map/ppermute | solution.py:373
  84.4 4.7 %all-to-all-done.1.part_ref = f32[4,528,128]{2,1,0:T(8,128)S(1)} async-done(((f32[4,528,128]{2,1,0:T(8,128)}), f32[4,528,128]{2,1,0:T(8,128)S(1)}, u32[]{:S(2)}, u32[]{:S(2)}) %all-to-all-start.1) | async-done | bytes 1081376 | tf_op jit(solution)/shard_map/all_to_all | solution.py:389
  89.9 5.5 %all-to-all-start.2 = ((bf16[8,128,128]{2,1,0:T(8,128)(2,1)}), bf16[8,128,128]{2,1,0:T(8,128)(2,1)S(1)}, u32[]{:S(2)}, u32[]{:S(2)}) async-start(bf16[8,128,128]{2,1,0:T(8,128)(2,1)} %mix.1), calls=%async_computation.2 | async-start | bytes 524288 | tf_op jit(solution)/shard_map/all_to_all | solution.py:390
  95.6 3.6 %edge.1.base_ref = f32[512,128]{1,0:T(8,128)S(1)} custom-call(s32[4,4]{1,0:T(4,128)S(1)} %fusion.4.wb_ref, s32[5]{0:T(128)S(1)} %stack.23.place_ref, bf16[512,128]{1,0:T(8,128)(2,1)S(1)} %copy-done.1, bf16[512,128]{1,0:T(8,128)(2,1)S(1)} %collective-permute-done.other_ref, bf16[1024,128]{1,0:T(8,128)(2,1)S(1)} %around.1.near_ref, ...), custom_call_target="tpu_custom_call" | custom-call | flops 4000000000 | bytes 1065984 | tf_op jit(solution)/shard_map/edge/pallas_call | solution.py:38
  99.2 3.5 %all-to-all-done.2.mixed_ref = bf16[8,128,128]{2,1,0:T(8,128)(2,1)S(1)} async-done(((bf16[8,128,128]{2,1,0:T(8,128)(2,1)}), bf16[8,128,128]{2,1,0:T(8,128)(2,1)S(1)}, u32[]{:S(2)}, u32[]{:S(2)}) %all-to-all-start.2) | async-done | bytes 262176 | tf_op jit(solution)/shard_map/all_to_all | solution.py:390
  (60 shorter events, 14.6 us)
Async XLA Ops:
  0.0 8.6 %collective-permute-start = (bf16[512,128]{1,0:T(8,128)(2,1)}, bf16[512,128]{1,0:T(8,128)(2,1)S(1)}, u32[]{:S(2)}, u32[]{:S(2)}) collective-permute-start(bf16[512,128]{1,0:T(8,128)(2,1)} %own_ref.1), channel_id=1, source_target_pairs={{0,1},{1,0},{2,3},{3,2},{4,5},{5,4},{6,7},{7,6},{8,9},{9,8},{10,11... | collective-permute-start | bytes 393224 | tf_op jit(solution)/shard_map/ppermute | solution.py:328
  1.9 6.7 %collective-permute-start.1 = (bf16[512,128]{1,0:T(8,128)(2,1)}, bf16[512,128]{1,0:T(8,128)(2,1)S(1)}, u32[]{:S(2)}, u32[]{:S(2)}) collective-permute-start(bf16[512,128]{1,0:T(8,128)(2,1)} %own_ref.1), channel_id=1, source_target_pairs={{62,126},{126,190},{190,254},{254,62},{63,127},{127,191},{191,255}... | collective-permute-start | bytes 393224 | tf_op jit(solution)/shard_map/ppermute | solution.py:332
  2.6 6.1 %collective-permute-start.2 = (bf16[512,128]{1,0:T(8,128)(2,1)}, bf16[512,128]{1,0:T(8,128)(2,1)S(1)}, u32[]{:S(2)}, u32[]{:S(2)}) collective-permute-start(bf16[512,128]{1,0:T(8,128)(2,1)} %own_ref.1), channel_id=1, source_target_pairs={{64,0},{128,64},{192,128},{0,192},{65,1},{129,65},{193,129},{1,193}} | collective-permute-start | bytes 393224 | tf_op jit(solution)/shard_map/ppermute | solution.py:333
  9.5 6.3 %collective-permute-start.3 = (bf16[256,128]{1,0:T(8,128)(2,1)S(1)}, bf16[256,128]{1,0:T(8,128)(2,1)S(1)}, u32[]{:S(2)}, u32[]{:S(2)}) collective-permute-start(bf16[256,128]{1,0:T(8,128)(2,1)S(1)} %get-tuple-element.20), channel_id=1, source_target_pairs={{0,4},{4,8},{8,12},{12,0},{1,5},{5,9},{9,13},{13,1},{2,6},{6,10},{... | collective-permute-start | bytes 196616 | tf_op jit(solution)/shard_map/ppermute | solution.py:351
  11.0 5.8 %collective-permute-start.4 = (bf16[256,128]{1,0:T(8,128)(2,1)S(1)}, bf16[256,128]{1,0:T(8,128)(2,1)S(1)}, u32[]{:S(2)}, u32[]{:S(2)}) collective-permute-start(bf16[256,128]{1,0:T(8,128)(2,1)S(1)} %get-tuple-element.21), channel_id=1, source_target_pairs={{0,8},{4,12},{8,0},{12,4},{1,9},{5,13},{9,1},{13,5},{2,10},{6,14},... | collective-permute-start | bytes 196616 | tf_op jit(solution)/shard_map/ppermute | solution.py:351
  13.7 4.3 %collective-permute-start.5 = (bf16[256,128]{1,0:T(8,128)(2,1)S(1)}, bf16[256,128]{1,0:T(8,128)(2,1)S(1)}, u32[]{:S(2)}, u32[]{:S(2)}) collective-permute-start(bf16[256,128]{1,0:T(8,128)(2,1)S(1)} %get-tuple-element.22), channel_id=1, source_target_pairs={{0,12},{4,0},{8,4},{12,8},{1,13},{5,1},{9,5},{13,9},{2,14},{6,2},{... | collective-permute-start | bytes 196616 | tf_op jit(solution)/shard_map/ppermute | solution.py:351
  19.0 18.3 %all-to-all-start = ((bf16[16,144,128]{2,1,0:T(8,128)(2,1)}), bf16[16,144,128]{2,1,0:T(8,128)(2,1)S(1)}, u32[]{:S(2)}, u32[]{:S(2)}) async-start(bf16[16,144,128]{2,1,0:T(8,128)(2,1)} %query.1), calls=%async_computation | async-start | bytes 1179648 | tf_op jit(solution)/shard_map/all_to_all | solution.py:359
  28.9 8.4 %collective-permute-start.8 = (bf16[4,256,128]{2,1,0:T(8,128)(2,1)S(1)}, bf16[4,256,128]{2,1,0:T(8,128)(2,1)S(1)}, u32[]{:S(2)}, u32[]{:S(2)}) collective-permute-start(bf16[4,256,128]{2,1,0:T(8,128)(2,1)S(1)} %gather.1.refs_0_), channel_id=1, source_target_pairs={{0,2},{2,0},{1,3},{3,1},{4,6},{6,4},{5,7},{7,5},{8,10},{10,8},{9,1... | collective-permute-start | bytes 786440 | tf_op jit(solution)/shard_map/ppermute | solution.py:355
  29.0 14.8 %collective-permute-start.6 = (bf16[4,256,128]{2,1,0:T(8,128)(2,1)S(1)}, bf16[4,256,128]{2,1,0:T(8,128)(2,1)S(1)}, u32[]{:S(2)}, u32[]{:S(2)}) collective-permute-start(bf16[4,256,128]{2,1,0:T(8,128)(2,1)S(1)} %gather.1.refs_0_), channel_id=1, source_target_pairs={{0,64},{64,128},{128,192},{192,0},{1,65},{65,129},{129,193},{193,1... | collective-permute-start | bytes 786440 | tf_op jit(solution)/shard_map/ppermute | solution.py:353
  30.8 15.2 %collective-permute-start.7 = (bf16[4,256,128]{2,1,0:T(8,128)(2,1)S(1)}, bf16[4,256,128]{2,1,0:T(8,128)(2,1)S(1)}, u32[]{:S(2)}, u32[]{:S(2)}) collective-permute-start(bf16[4,256,128]{2,1,0:T(8,128)(2,1)S(1)} %gather.1.refs_0_), channel_id=1, source_target_pairs={{0,192},{64,0},{128,64},{192,128},{1,193},{65,1},{129,65},{193,129... | collective-permute-start | bytes 786440 | tf_op jit(solution)/shard_map/ppermute | solution.py:354
  46.0 4.3 %collective-permute-start.11 = (bf16[8,256,128]{2,1,0:T(8,128)(2,1)S(1)}, bf16[8,256,128]{2,1,0:T(8,128)(2,1)S(1)}, u32[]{:S(2)}, u32[]{:S(2)}) collective-permute-start(bf16[8,256,128]{2,1,0:T(8,128)(2,1)S(1)} %get-tuple-element.26.refs_0_), channel_id=1, source_target_pairs={{0,2},{2,0},{1,3},{3,1},{4,6},{6,4},{5,7},{7,5},{8,10},{10,8},{9,1... | collective-permute-start | bytes 1572872 | tf_op jit(solution)/shard_map/ppermute | solution.py:367
  46.1 14.6 %collective-permute-start.9 = (bf16[2,256,128]{2,1,0:T(8,128)(2,1)S(1)}, bf16[2,256,128]{2,1,0:T(8,128)(2,1)S(1)}, u32[]{:S(2)}, u32[]{:S(2)}) collective-permute-start(bf16[2,256,128]{2,1,0:T(8,128)(2,1)S(1)} %get-tuple-element.24), channel_id=1, source_target_pairs={{0,64},{64,128},{128,192},{192,0},{1,65},{65,129},{129,193},{193,1... | collective-permute-start | bytes 393224 | tf_op jit(solution)/shard_map/ppermute | solution.py:365
  49.7 11.0 %collective-permute-start.10 = (bf16[2,256,128]{2,1,0:T(8,128)(2,1)S(1)}, bf16[2,256,128]{2,1,0:T(8,128)(2,1)S(1)}, u32[]{:S(2)}, u32[]{:S(2)}) collective-permute-start(bf16[2,256,128]{2,1,0:T(8,128)(2,1)S(1)} %get-tuple-element.25), channel_id=1, source_target_pairs={{0,192},{64,0},{128,64},{192,128},{1,193},{65,1},{129,65},{193,129... | collective-permute-start | bytes 393224 | tf_op jit(solution)/shard_map/ppermute | solution.py:366
  60.7 1.6 %collective-permute-start.12 = (bf16[4,256,128]{2,1,0:T(8,128)(2,1)S(1)}, bf16[4,256,128]{2,1,0:T(8,128)(2,1)S(1)}, u32[]{:S(2)}, u32[]{:S(2)}) collective-permute-start(bf16[4,256,128]{2,1,0:T(8,128)(2,1)S(1)} %across.1.refs_0_), channel_id=1, source_target_pairs={{0,2},{2,0},{1,3},{3,1},{4,6},{6,4},{5,7},{7,5},{8,10},{10,8},{9,1... | collective-permute-start | bytes 786440 | tf_op jit(solution)/shard_map/ppermute | solution.py:369
  70.1 19.0 %all-to-all-start.1 = ((f32[4,528,128]{2,1,0:T(8,128)}), f32[4,528,128]{2,1,0:T(8,128)S(1)}, u32[]{:S(2)}, u32[]{:S(2)}) async-start(f32[4,528,128]{2,1,0:T(8,128)} %attend2.1.wait_ref), calls=%async_computation.1 | async-start | bytes 2162688 | tf_op jit(solution)/shard_map/all_to_all | solution.py:389
  75.6 6.7 %collective-permute-start.14 = (bf16[512,128]{1,0:T(8,128)(2,1)S(1)}, bf16[512,128]{1,0:T(8,128)(2,1)S(1)}, u32[]{:S(2)}, u32[]{:S(2)}) collective-permute-start(bf16[512,128]{1,0:T(8,128)(2,1)S(1)} %get-tuple-element.27), channel_id=1, source_target_pairs={{0,2},{2,4},{4,6},{6,8},{8,10},{10,12},{12,14},{14,16},{16,18},{18... | collective-permute-start | bytes 393224 | tf_op jit(solution)/shard_map/ppermute | solution.py:373
  75.7 19.7 %copy-start.11 = (s32[4,4]{1,0:T(4,128)S(1)}, s32[4,4]{1,0:T(4,128)}, u32[]{:S(2)}) copy-start(s32[4,4]{1,0:T(4,128)} %param.19) | copy-start | bytes 196
  75.7 19.7 %copy-start.10 = (s32[512,8]{0,1:T(8,128)S(1)}, s32[512,8]{0,1:T(8,128)}, u32[]{:S(2)}) copy-start(s32[512,8]{0,1:T(8,128)} %param.20) | copy-start | bytes 49156
  75.8 6.6 %collective-permute-start.15 = (bf16[512,128]{1,0:T(8,128)(2,1)S(1)}, bf16[512,128]{1,0:T(8,128)(2,1)S(1)}, u32[]{:S(2)}, u32[]{:S(2)}) collective-permute-start(bf16[512,128]{1,0:T(8,128)(2,1)S(1)} %get-tuple-element.28), channel_id=1, source_target_pairs={{2,0},{4,2},{6,4},{8,6},{10,8},{12,10},{14,12},{16,14},{18,16},{20... | collective-permute-start | bytes 393224 | tf_op jit(solution)/shard_map/ppermute | solution.py:374
  79.6 4.3 %collective-permute-start.13 = (bf16[128,256]{1,0:T(8,128)(2,1)S(1)}, bf16[128,256]{1,0:T(8,128)(2,1)S(1)}, u32[]{:S(2)}, u32[]{:S(2)}) collective-permute-start(bf16[128,256]{1,0:T(8,128)(2,1)S(1)} %copy-done.5), channel_id=1, source_target_pairs={{0,1},{1,0},{2,3},{3,2},{4,5},{5,4},{6,7},{7,6},{8,9},{9,8},{10,11... | collective-permute-start | bytes 196616 | tf_op jit(solution)/shard_map/ppermute | solution.py:329
  82.3 13.2 %copy-start.7 = (bf16[2,256,128]{2,1,0:T(8,128)(2,1)S(1)}, bf16[2,256,128]{2,1,0:T(8,128)(2,1)}, u32[]{:S(2)}) copy-start(bf16[2,256,128]{2,1,0:T(8,128)(2,1)} %ws_ref.1) | copy-start | bytes 393220
  82.4 13.2 %copy-start.8 = (bf16[2,256,128]{2,1,0:T(8,128)(2,1)S(1)}, bf16[2,256,128]{2,1,0:T(8,128)(2,1)}, u32[]{:S(2)}) copy-start(bf16[2,256,128]{2,1,0:T(8,128)(2,1)} %wt_ref.1) | copy-start | bytes 393220
  82.4 13.2 %collective-permute-start.16 = (bf16[1024,128]{1,0:T(8,128)(2,1)S(1)}, bf16[1024,128]{1,0:T(8,128)(2,1)S(1)}, u32[]{:S(2)}, u32[]{:S(2)}) collective-permute-start(bf16[1024,128]{1,0:T(8,128)(2,1)S(1)} %around.1.near_ref), channel_id=1, source_target_pairs={{0,1},{1,0},{2,3},{3,2},{4,5},{5,4},{6,7},{7,6},{8,9},{9,8},{10,11... | collective-permute-start | bytes 786440 | tf_op jit(solution)/shard_map/ppermute | solution.py:376
  89.9 12.8 %all-to-all-start.2 = ((bf16[8,128,128]{2,1,0:T(8,128)(2,1)}), bf16[8,128,128]{2,1,0:T(8,128)(2,1)S(1)}, u32[]{:S(2)}, u32[]{:S(2)}) async-start(bf16[8,128,128]{2,1,0:T(8,128)(2,1)} %mix.1), calls=%async_computation.2 | async-start | bytes 524288 | tf_op jit(solution)/shard_map/all_to_all | solution.py:390
  (8 other events, 31.7 us)

commit v3 on v2

--- a/solution.py
+++ b/solution.py
@@ -56,13 +56,8 @@
     return jnp.concatenate([jnp.where(first, own, other), jnp.where(first, other, own)], axis=1)
 
 
-def prepare_kernel(place_ref, cells_ref, wk_ref, wv_ref, wq_ref, blocks_ref, partial_ref, rest_ref, codes_ref):
+def prepare_kernel(place_ref, cells_ref, weights_ref, blocks_ref, partial_ref, rest_ref, codes_ref):
     side, zh, core = place_ref[0], place_ref[1], place_ref[2]
-    mine = pl.ds(pl.multiple_of(side * BLOCK, BLOCK), BLOCK)
-    theirs = pl.ds(pl.multiple_of((1 - side) * BLOCK, BLOCK), BLOCK)
-    for n, w_ref in enumerate((wk_ref, wv_ref, wq_ref)):
-        partial_ref[n] = dot(w_ref[mine, :], cells_ref[...], TT)
-        rest_ref[n] = jnp.transpose(w_ref[theirs, :].astype(F32)).astype(BF16)
 
     def facts(ids):
         owner = ids // BLK_DEV
@@ -95,9 +90,14 @@
         units = jnp.maximum((tally[y].astype(jnp.int32) + GROUP - 1) // GROUP, 1).astype(F32)
         rows += [jnp.concatenate(found[y], axis=1), jnp.concatenate([units, jnp.zeros((1, 96), F32)], axis=1)]
     codes_ref[...] = jnp.concatenate(rows + [jnp.zeros((8, BLOCK), F32)], axis=0).astype(BF16)
-
-
-def keyval_kernel(place_ref, partial_ref, rest_ref, other_ref, up_ref, down_ref, own_ref, *outs):
+    mine = pl.ds(pl.multiple_of(side * BLOCK, BLOCK), BLOCK)
+    theirs = pl.ds(pl.multiple_of((1 - side) * BLOCK, BLOCK), BLOCK)
+    for n in range(3):
+        partial_ref[n] = dot(weights_ref[n, mine, :], cells_ref[...], TT)
+        rest_ref[n] = jnp.transpose(weights_ref[n, theirs, :].astype(F32)).astype(BF16)
+
+
+def keyval_kernel(place_ref, partial_ref, rest_ref, other_ref, own_ref, *outs):
     *sends, keyval = outs
     other = other_ref[...]
     for n in range(2):
@@ -112,14 +112,20 @@
         ref[...] = keyval[d + 1]
 
 
-def query_kernel(partial_ref, rest_ref, other_ref, codes_ref, got0_ref, got1_ref, got2_ref, out_ref):
+def query_kernel(partial_ref, rest_ref, other_ref, codes_ref, cells_ref, wait_ref, out_ref, cells_out):
+    cells_out[...] = cells_ref[...]
     flat = (partial_ref[2] + dot(rest_ref[2], other_ref[...], NT)).astype(BF16)
     for head in range(4):
-        for y in range(4):
-            for b in range(BLK_DEV):
-                part = flat[head * 32 : head * 32 + 32, b * BLOCK : (b + 1) * BLOCK]
-                out_ref[y * 4 + head, b * 32 : b * 32 + 32, :] = part
-            out_ref[y * 4 + head, BLOCK : BLOCK + 16, :] = codes_ref[...]
+        for b in range(BLK_DEV):
+            part = flat[head * 32 : head * 32 + 32, b * BLOCK : (b + 1) * BLOCK]
+            out_ref[head, b * 32 : b * 32 + 32, :] = part
+        out_ref[head, BLOCK : BLOCK + 16, :] = codes_ref[...]
+
+
+def spread_kernel(query_ref, *refs):
+    out_ref = refs[-1]
+    for y in range(4):
+        out_ref[y * 4 : y * 4 + 4] = query_ref[...]
 
 
 def gather_kernel(place_ref, own_ref, *refs):
@@ -329,13 +335,11 @@
     w_got = lax.ppermute(w_out, "h", swap)
     tops = [(z * 32 + 31, (z + 1) % 4 * 32 + 31) for z in range(4)]
     bottoms = [((z + 1) % 4 * 32, z * 32) for z in range(4)]
-    up = lax.ppermute(cells, everyone, tops)
-    down = lax.ppermute(cells, everyone, bottoms)
     places = jnp.stack([side, lax.axis_index("zh"), lax.axis_index("c"), lax.axis_index("x"), lax.axis_index("y")])
     partial, rest, codes = call(
         prepare_kernel,
         [shaped((3, BLOCK, rows), F32), shaped((3, BLOCK, BLOCK), BF16), shaped((16, BLOCK), BF16)],
-        [cells, w_key, w_value, w_query, key_blocks],
+        [cells, jnp.stack([w_key, w_value, w_query]), key_blocks],
         "prepare",
         scalars=(places,),
     )
@@ -346,16 +350,22 @@
         "keyval",
         scalars=(places,),
         scratch=[pltpu.VMEM((4, 256, BLOCK), BF16)],
-        after=[up, down],
     )
     got = [lax.ppermute(v, "x", ring[d + 1]) for d, v in enumerate(sends)]
     (here,) = call(gather_kernel, [shaped((4, 256, BLOCK), BF16)], [own, *got], "gather", scalars=(places,))
     left = lax.ppermute(here, "zh", ring[1])
     right = lax.ppermute(here, "zh", ring[3])
     mate_here = lax.ppermute(here, "c", swap)
-    (query,) = call(
-        query_kernel, [shaped((16, 144, BLOCK), BF16)], [partial, rest, other, codes], "query", after=got
-    )
+    query, passed = call(
+        query_kernel,
+        [shaped((4, 144, BLOCK), BF16), shaped(cells.shape, BF16)],
+        [partial, rest, other, codes, cells],
+        "query",
+        after=[got[0]],
+    )
+    up = lax.ppermute(passed, everyone, tops)
+    down = lax.ppermute(passed, everyone, bottoms)
+    (query,) = call(spread_kernel, [shaped((16, 144, BLOCK), BF16)], [query], "spread", after=[*got, up, down])
     q_all = lax.all_to_all(query, ("y", "x"), 0, 0).reshape(4, 4, 144, BLOCK)
     lists = lax.dynamic_slice_in_dim(q_all, BLOCK + 2 * lax.axis_index("y"), 2, 2)
     lists = jnp.pad(lists.reshape(32, BLOCK).astype(jnp.int32), ((0, 8), (0, 0)), constant_values=EMPTY)

time: 104 us -> 107 us (1.029)
  local copies, waits for them, and re-layouts: 4.36 us -> 1.84 us
  starting transfers between devices: 42.5 us -> 44.6 us
  waiting for transfers between devices: 21.9 us -> 23.7 us
    ppermute x3, waiting for transfers between devices: 2.83 us -> 7.11 us  [body(): got = [lax.ppermute(v, 'x', ring[d + 1]) for d, v in enumerate(sends)]]
    unnamed x25 -> x19, local copies, waits for them, and re-layouts: 4.26 us -> 1.74 us
    ppermute x1, starting transfers between devices: 1.75 us -> 0.08 us  [body(): left = lax.ppermute(here, 'zh', ring[1])]
    ppermute x1, starting transfers between devices: 2.47 us -> 4.12 us  [body(): right = lax.ppermute(here, 'zh', ring[3])]
    all_to_all x1, starting transfers between devices: 9.32 us -> 10.9 us  [body(): q_all = lax.all_to_all(query, ('y', 'x'), 0, 0).reshape(4, 4, 144, BLOCK)]
    ppermute x3, starting transfers between devices: 5.73 us -> 4.6 us  [body(): got = [lax.ppermute(v, 'x', ring[d + 1]) for d, v in enumerate(sends)]]
    pallas_call x15 -> x16, Pallas kernels: 34.6 us -> 34.6 us  [call(): pl.pallas_call(kernel, grid_spec=pltpu.PrefetchScalarGridSpec(num_scalar_...]
  transfers between devices with their start and end apart: 20 -> 20, of which waited for: 10 -> 10; matrix products, arithmetic and copies ran while one was open for 0% -> 1% of each run, Pallas kernels for 23% -> 23%
where the time goes in v3:
time: 107 us; the launch traced here: 106 us
  starting transfers between devices  44.6 us (42%)
  Pallas kernels  34.6 us (32%)
  waiting for transfers between devices  23.7 us (22%)
  local copies, waits for them, and re-layouts  1.84 us (2%)
    pallas_call x16, Pallas kernels, call(): pl.pallas_call(kernel, grid_spec=pltpu.PrefetchScalarGridSpec(num_scalar_...  34.6 us
    all_to_all x1, starting transfers between devices, body(): q_all = lax.all_to_all(query, ('y', 'x'), 0, 0).reshape(4, 4, 144, BLOCK)  10.9 us
    ppermute x3, waiting for transfers between devices, body(): got = [lax.ppermute(v, 'x', ring[d + 1]) for d, v in enumerate(sends)]  7.11 us
    all_to_all x1, starting transfers between devices, body(): mixed = lax.all_to_all(mixed, ('x', 'h'), 0, 0)  6.02 us
    all_to_all x1, waiting for transfers between devices, body(): lax.all_to_all(partial, 'y', 0, 0)  4.79 us
    ppermute x3, starting transfers between devices, body(): got = [lax.ppermute(v, 'x', ring[d + 1]) for d, v in enumerate(sends)]  4.6 us
    all_to_all x1, starting transfers between devices, body(): lax.all_to_all(partial, 'y', 0, 0)  4.31 us
    ppermute x1, starting transfers between devices, body(): right = lax.ppermute(here, 'zh', ring[3])  4.12 us
  transfers between devices with their start and end apart: 20, of which 10 were waited for; matrix products, arithmetic and copies ran while one was open for 1% of the time, Pallas kernels for 23%

profile of v3, /device:TPU:8, one launch (start us, length us, event | category | flops | bytes accessed | tf_op | source)
XLA Modules:
  0.0 106.0 jit_solution(12941959240262626437)
XLA Ops:
  0.0 1.9 %collective-permute-start = (bf16[512,128]{1,0:T(8,128)(2,1)}, bf16[512,128]{1,0:T(8,128)(2,1)S(1)}, u32[]{:S(2)}, u32[]{:S(2)}) collective-permute-start(bf16[512,128]{1,0:T(8,128)(2,1)} %own_ref.1), channel_id=1, source_target_pairs={{0,1},{1,0},{2,3},{3,2},{4,5},{5,4},{6,7},{7,6},{8,9},{9,8},{10,11... | collective-permute-start | bytes 393224 | tf_op jit(solution)/shard_map/ppermute | solution.py:334
  6.5 1.6 %collective-permute-start.1 = (bf16[256,128]{1,0:T(8,128)(2,1)S(1)}, bf16[256,128]{1,0:T(8,128)(2,1)S(1)}, u32[]{:S(2)}, u32[]{:S(2)}) collective-permute-start(bf16[256,128]{1,0:T(8,128)(2,1)S(1)} %get-tuple-element.22), channel_id=1, source_target_pairs={{0,4},{4,8},{8,12},{12,0},{1,5},{5,9},{9,13},{13,1},{2,6},{6,10},{... | collective-permute-start | bytes 196616 | tf_op jit(solution)/shard_map/ppermute | solution.py:354
  8.0 4.0 %collective-permute-done.1.wait_ref.refs_0_ = bf16[256,128]{1,0:T(8,128)(2,1)S(1)} collective-permute-done((bf16[256,128]{1,0:T(8,128)(2,1)S(1)}, bf16[256,128]{1,0:T(8,128)(2,1)S(1)}, u32[]{:S(2)}, u32[]{:S(2)}) %collective-permute-start.1) | collective-permute-done | bytes 65568 | tf_op jit(solution)/shard_map/ppermute | solution.py:354
  13.6 1.9 %collective-permute-start.2 = (bf16[256,128]{1,0:T(8,128)(2,1)S(1)}, bf16[256,128]{1,0:T(8,128)(2,1)S(1)}, u32[]{:S(2)}, u32[]{:S(2)}) collective-permute-start(bf16[256,128]{1,0:T(8,128)(2,1)S(1)} %get-tuple-element.24), channel_id=1, source_target_pairs={{0,8},{4,12},{8,0},{12,4},{1,9},{5,13},{9,1},{13,5},{2,10},{6,14},... | collective-permute-start | bytes 196616 | tf_op jit(solution)/shard_map/ppermute | solution.py:354
  15.5 1.1 %collective-permute-start.3 = (bf16[256,128]{1,0:T(8,128)(2,1)S(1)}, bf16[256,128]{1,0:T(8,128)(2,1)S(1)}, u32[]{:S(2)}, u32[]{:S(2)}) collective-permute-start(bf16[256,128]{1,0:T(8,128)(2,1)S(1)} %get-tuple-element.25), channel_id=1, source_target_pairs={{0,12},{4,0},{8,4},{12,8},{1,13},{5,1},{9,5},{13,9},{2,14},{6,2},{... | collective-permute-start | bytes 196616 | tf_op jit(solution)/shard_map/ppermute | solution.py:354
  16.6 2.8 %collective-permute-done.2.refs_1_ = bf16[256,128]{1,0:T(8,128)(2,1)S(1)} collective-permute-done((bf16[256,128]{1,0:T(8,128)(2,1)S(1)}, bf16[256,128]{1,0:T(8,128)(2,1)S(1)}, u32[]{:S(2)}, u32[]{:S(2)}) %collective-permute-start.2) | collective-permute-done | bytes 65568 | tf_op jit(solution)/shard_map/ppermute | solution.py:354
  20.6 10.9 %all-to-all-start = ((bf16[16,144,128]{2,1,0:T(8,128)(2,1)}), bf16[16,144,128]{2,1,0:T(8,128)(2,1)S(1)}, u32[]{:S(2)}, u32[]{:S(2)}) async-start(bf16[16,144,128]{2,1,0:T(8,128)(2,1)} %spread.1), calls=%async_computation | async-start | bytes 1179648 | tf_op jit(solution)/shard_map/all_to_all | solution.py:369
  32.3 4.1 %collective-permute-start.7 = (bf16[4,256,128]{2,1,0:T(8,128)(2,1)S(1)}, bf16[4,256,128]{2,1,0:T(8,128)(2,1)S(1)}, u32[]{:S(2)}, u32[]{:S(2)}) collective-permute-start(bf16[4,256,128]{2,1,0:T(8,128)(2,1)S(1)} %gather.1.refs_0_), channel_id=1, source_target_pairs={{0,192},{64,0},{128,64},{192,128},{1,193},{65,1},{129,65},{193,129... | collective-permute-start | bytes 786440 | tf_op jit(solution)/shard_map/ppermute | solution.py:357
  36.4 3.6 %all-to-all-done = bf16[16,144,128]{2,1,0:T(8,128)(2,1)S(1)} async-done(((bf16[16,144,128]{2,1,0:T(8,128)(2,1)}), bf16[16,144,128]{2,1,0:T(8,128)(2,1)S(1)}, u32[]{:S(2)}, u32[]{:S(2)}) %all-to-all-start) | async-done | bytes 589856 | tf_op jit(solution)/shard_map/all_to_all | solution.py:369
  40.1 6.4 %attend0.1.after_ref.refs_2_ = f32[65,40,128]{2,1,0:T(8,128)S(1)} custom-call(s32[40,128]{1,0:T(8,128)S(1)} %pad_convert_fusion.list_ref, bf16[4,4,144,128]{3,2,1,0:T(8,128)(2,1)S(1)} %bitcast.11, bf16[4,256,128]{2,1,0:T(8,128)(2,1)S(1)} %gather.1.refs_0_, bf16[4,256,128]{2,1,0:T(8,128)(2,1)S(1)} %collective-permute-done.8.refs_1_), custom_call_target="tpu_custom_call" | custom-call | flops 1000000 | bytes 1114112 | tf_op jit(solution)/shard_map/attend0/pallas_call | solution.py:38
  46.5 1.5 %collective-permute-done.7.right_ref = bf16[4,256,128]{2,1,0:T(8,128)(2,1)S(1)} collective-permute-done((bf16[4,256,128]{2,1,0:T(8,128)(2,1)S(1)}, bf16[4,256,128]{2,1,0:T(8,128)(2,1)S(1)}, u32[]{:S(2)}, u32[]{:S(2)}) %collective-permute-start.7) | collective-permute-done | bytes 262176 | tf_op jit(solution)/shard_map/ppermute | solution.py:357
  48.2 3.6 %collective-permute-start.9 = (bf16[2,256,128]{2,1,0:T(8,128)(2,1)S(1)}, bf16[2,256,128]{2,1,0:T(8,128)(2,1)S(1)}, u32[]{:S(2)}, u32[]{:S(2)}) collective-permute-start(bf16[2,256,128]{2,1,0:T(8,128)(2,1)S(1)} %get-tuple-element.28), channel_id=1, source_target_pairs={{0,64},{64,128},{128,192},{192,0},{1,65},{65,129},{129,193},{193,1... | collective-permute-start | bytes 393224 | tf_op jit(solution)/shard_map/ppermute | solution.py:375
  52.8 10.7 %attend1.1.after_ref.refs_2_ = f32[65,40,128]{2,1,0:T(8,128)S(1)} custom-call(s32[40,128]{1,0:T(8,128)S(1)} %pad_convert_fusion.list_ref, bf16[4,4,144,128]{3,2,1,0:T(8,128)(2,1)S(1)} %bitcast.12, bf16[8,256,128]{2,1,0:T(8,128)(2,1)S(1)} %get-tuple-element.30.refs_0_, bf16[8,256,128]{2,1,0:T(8,128)(2,1)S(1)} %collective-permute-done.11.refs_1_, ...), custom_call_target="tpu_custom_call" | custom-call | flops 8999999488 | bytes 2969600 | tf_op jit(solution)/shard_map/attend1/pallas_call | solution.py:38
  63.7 1.5 %collective-permute-done.12.refs_1_ = bf16[4,256,128]{2,1,0:T(8,128)(2,1)S(1)} collective-permute-done((bf16[4,256,128]{2,1,0:T(8,128)(2,1)S(1)}, bf16[4,256,128]{2,1,0:T(8,128)(2,1)S(1)}, u32[]{:S(2)}, u32[]{:S(2)}) %collective-permute-start.12) | collective-permute-done | bytes 262176 | tf_op jit(solution)/shard_map/ppermute | solution.py:379
  65.2 7.4 %attend2.1.wait_ref = f32[4,528,128]{2,1,0:T(8,128)} custom-call(s32[40,128]{1,0:T(8,128)S(1)} %pad_convert_fusion.list_ref, bf16[4,4,144,128]{3,2,1,0:T(8,128)(2,1)S(1)} %bitcast.13, bf16[4,256,128]{2,1,0:T(8,128)(2,1)S(1)} %across.1.refs_0_, bf16[4,256,128]{2,1,0:T(8,128)(2,1)S(1)} %collective-permute-done.12.refs_1_, ...), custom_call_target="tpu_custom_call" | custom-call | flops 5000000000 | bytes 2445312 | tf_op jit(solution)/shard_map/attend2/pallas_call | solution.py:38
  72.6 4.3 %all-to-all-start.1 = ((f32[4,528,128]{2,1,0:T(8,128)}), f32[4,528,128]{2,1,0:T(8,128)S(1)}, u32[]{:S(2)}, u32[]{:S(2)}) async-start(f32[4,528,128]{2,1,0:T(8,128)} %attend2.1.wait_ref), calls=%async_computation.1 | async-start | bytes 2162688 | tf_op jit(solution)/shard_map/all_to_all | solution.py:399
  77.6 3.8 %collective-permute-start.15 = (bf16[512,128]{1,0:T(8,128)(2,1)S(1)}, bf16[512,128]{1,0:T(8,128)(2,1)S(1)}, u32[]{:S(2)}, u32[]{:S(2)}) collective-permute-start(bf16[512,128]{1,0:T(8,128)(2,1)S(1)} %get-tuple-element.32), channel_id=1, source_target_pairs={{2,0},{4,2},{6,4},{8,6},{10,8},{12,10},{14,12},{16,14},{18,16},{20... | collective-permute-start | bytes 393224 | tf_op jit(solution)/shard_map/ppermute | solution.py:384
  81.4 1.2 %collective-permute-start.13 = (bf16[128,256]{1,0:T(8,128)(2,1)S(1)}, bf16[128,256]{1,0:T(8,128)(2,1)S(1)}, u32[]{:S(2)}, u32[]{:S(2)}) collective-permute-start(bf16[128,256]{1,0:T(8,128)(2,1)S(1)} %copy-done.2), channel_id=1, source_target_pairs={{0,1},{1,0},{2,3},{3,2},{4,5},{5,4},{6,7},{7,6},{8,9},{9,8},{10,11... | collective-permute-start | bytes 196616 | tf_op jit(solution)/shard_map/ppermute | solution.py:335
  82.6 1.5 %collective-permute-done.14.before_ref = bf16[512,128]{1,0:T(8,128)(2,1)S(1)} collective-permute-done((bf16[512,128]{1,0:T(8,128)(2,1)S(1)}, bf16[512,128]{1,0:T(8,128)(2,1)S(1)}, u32[]{:S(2)}, u32[]{:S(2)}) %collective-permute-start.14) | collective-permute-done | bytes 131104 | tf_op jit(solution)/shard_map/ppermute | solution.py:383
  84.2 1.3 %collective-permute-start.16 = (bf16[1024,128]{1,0:T(8,128)(2,1)S(1)}, bf16[1024,128]{1,0:T(8,128)(2,1)S(1)}, u32[]{:S(2)}, u32[]{:S(2)}) collective-permute-start(bf16[1024,128]{1,0:T(8,128)(2,1)S(1)} %around.1.near_ref), channel_id=1, source_target_pairs={{0,1},{1,0},{2,3},{3,2},{4,5},{5,4},{6,7},{7,6},{8,9},{9,8},{10,11... | collective-permute-start | bytes 786440 | tf_op jit(solution)/shard_map/ppermute | solution.py:386
  86.3 4.8 %all-to-all-done.1.part_ref = f32[4,528,128]{2,1,0:T(8,128)S(1)} async-done(((f32[4,528,128]{2,1,0:T(8,128)}), f32[4,528,128]{2,1,0:T(8,128)S(1)}, u32[]{:S(2)}, u32[]{:S(2)}) %all-to-all-start.1) | async-done | bytes 1081376 | tf_op jit(solution)/shard_map/all_to_all | solution.py:399
  91.8 6.0 %all-to-all-start.2 = ((bf16[8,128,128]{2,1,0:T(8,128)(2,1)}), bf16[8,128,128]{2,1,0:T(8,128)(2,1)S(1)}, u32[]{:S(2)}, u32[]{:S(2)}) async-start(bf16[8,128,128]{2,1,0:T(8,128)(2,1)} %mix.1), calls=%async_computation.2 | async-start | bytes 524288 | tf_op jit(solution)/shard_map/all_to_all | solution.py:400
  98.0 3.6 %edge.1.base_ref = f32[512,128]{1,0:T(8,128)S(1)} custom-call(s32[4,4]{1,0:T(4,128)S(1)} %fusion.4.wb_ref, s32[5]{0:T(128)S(1)} %stack.35.place_ref, bf16[512,128]{1,0:T(8,128)(2,1)S(1)} %copy-done.1, bf16[512,128]{1,0:T(8,128)(2,1)S(1)} %collective-permute-done.other_ref, bf16[1024,128]{1,0:T(8,128)(2,1)S(1)} %around.1.near_ref, ...), custom_call_target="tpu_custom_call" | custom-call | flops 4000000000 | bytes 1065984 | tf_op jit(solution)/shard_map/edge/pallas_call | solution.py:38
  101.6 3.5 %all-to-all-done.2.mixed_ref = bf16[8,128,128]{2,1,0:T(8,128)(2,1)S(1)} async-done(((bf16[8,128,128]{2,1,0:T(8,128)(2,1)}), bf16[8,128,128]{2,1,0:T(8,128)(2,1)S(1)}, u32[]{:S(2)}, u32[]{:S(2)}) %all-to-all-start.2) | async-done | bytes 262176 | tf_op jit(solution)/shard_map/all_to_all | solution.py:400
  (56 shorter events, 12.6 us)
Async XLA Ops:
  0.0 5.7 %collective-permute-start = (bf16[512,128]{1,0:T(8,128)(2,1)}, bf16[512,128]{1,0:T(8,128)(2,1)S(1)}, u32[]{:S(2)}, u32[]{:S(2)}) collective-permute-start(bf16[512,128]{1,0:T(8,128)(2,1)} %own_ref.1), channel_id=1, source_target_pairs={{0,1},{1,0},{2,3},{3,2},{4,5},{5,4},{6,7},{7,6},{8,9},{9,8},{10,11... | collective-permute-start | bytes 393224 | tf_op jit(solution)/shard_map/ppermute | solution.py:334
  6.5 5.6 %collective-permute-start.1 = (bf16[256,128]{1,0:T(8,128)(2,1)S(1)}, bf16[256,128]{1,0:T(8,128)(2,1)S(1)}, u32[]{:S(2)}, u32[]{:S(2)}) collective-permute-start(bf16[256,128]{1,0:T(8,128)(2,1)S(1)} %get-tuple-element.22), channel_id=1, source_target_pairs={{0,4},{4,8},{8,12},{12,0},{1,5},{5,9},{9,13},{13,1},{2,6},{6,10},{... | collective-permute-start | bytes 196616 | tf_op jit(solution)/shard_map/ppermute | solution.py:354
  12.2 7.5 %collective-permute-start.4 = (bf16[512,128]{1,0:T(8,128)(2,1)S(1)}, bf16[512,128]{1,0:T(8,128)(2,1)S(1)}, u32[]{:S(2)}, u32[]{:S(2)}) collective-permute-start(bf16[512,128]{1,0:T(8,128)(2,1)S(1)} %get-tuple-element.26), channel_id=1, source_target_pairs={{62,126},{126,190},{190,254},{254,62},{63,127},{127,191},{191,255}... | collective-permute-start | bytes 393224 | tf_op jit(solution)/shard_map/ppermute | solution.py:366
  12.9 6.8 %collective-permute-start.5 = (bf16[512,128]{1,0:T(8,128)(2,1)S(1)}, bf16[512,128]{1,0:T(8,128)(2,1)S(1)}, u32[]{:S(2)}, u32[]{:S(2)}) collective-permute-start(bf16[512,128]{1,0:T(8,128)(2,1)S(1)} %get-tuple-element.26), channel_id=1, source_target_pairs={{64,0},{128,64},{192,128},{0,192},{65,1},{129,65},{193,129},{1,193}} | collective-permute-start | bytes 393224 | tf_op jit(solution)/shard_map/ppermute | solution.py:367
  13.6 5.9 %collective-permute-start.2 = (bf16[256,128]{1,0:T(8,128)(2,1)S(1)}, bf16[256,128]{1,0:T(8,128)(2,1)S(1)}, u32[]{:S(2)}, u32[]{:S(2)}) collective-permute-start(bf16[256,128]{1,0:T(8,128)(2,1)S(1)} %get-tuple-element.24), channel_id=1, source_target_pairs={{0,8},{4,12},{8,0},{12,4},{1,9},{5,13},{9,1},{13,5},{2,10},{6,14},... | collective-permute-start | bytes 196616 | tf_op jit(solution)/shard_map/ppermute | solution.py:354
  15.5 4.3 %collective-permute-start.3 = (bf16[256,128]{1,0:T(8,128)(2,1)S(1)}, bf16[256,128]{1,0:T(8,128)(2,1)S(1)}, u32[]{:S(2)}, u32[]{:S(2)}) collective-permute-start(bf16[256,128]{1,0:T(8,128)(2,1)S(1)} %get-tuple-element.25), channel_id=1, source_target_pairs={{0,12},{4,0},{8,4},{12,8},{1,13},{5,1},{9,5},{13,9},{2,14},{6,2},{... | collective-permute-start | bytes 196616 | tf_op jit(solution)/shard_map/ppermute | solution.py:354
  20.6 19.4 %all-to-all-start = ((bf16[16,144,128]{2,1,0:T(8,128)(2,1)}), bf16[16,144,128]{2,1,0:T(8,128)(2,1)S(1)}, u32[]{:S(2)}, u32[]{:S(2)}) async-start(bf16[16,144,128]{2,1,0:T(8,128)(2,1)} %spread.1), calls=%async_computation | async-start | bytes 1179648 | tf_op jit(solution)/shard_map/all_to_all | solution.py:369
  32.1 8.0 %collective-permute-start.8 = (bf16[4,256,128]{2,1,0:T(8,128)(2,1)S(1)}, bf16[4,256,128]{2,1,0:T(8,128)(2,1)S(1)}, u32[]{:S(2)}, u32[]{:S(2)}) collective-permute-start(bf16[4,256,128]{2,1,0:T(8,128)(2,1)S(1)} %gather.1.refs_0_), channel_id=1, source_target_pairs={{0,2},{2,0},{1,3},{3,1},{4,6},{6,4},{5,7},{7,5},{8,10},{10,8},{9,1... | collective-permute-start | bytes 786440 | tf_op jit(solution)/shard_map/ppermute | solution.py:358
  32.2 14.3 %collective-permute-start.6 = (bf16[4,256,128]{2,1,0:T(8,128)(2,1)S(1)}, bf16[4,256,128]{2,1,0:T(8,128)(2,1)S(1)}, u32[]{:S(2)}, u32[]{:S(2)}) collective-permute-start(bf16[4,256,128]{2,1,0:T(8,128)(2,1)S(1)} %gather.1.refs_0_), channel_id=1, source_target_pairs={{0,64},{64,128},{128,192},{192,0},{1,65},{65,129},{129,193},{193,1... | collective-permute-start | bytes 786440 | tf_op jit(solution)/shard_map/ppermute | solution.py:356
  32.3 15.7 %collective-permute-start.7 = (bf16[4,256,128]{2,1,0:T(8,128)(2,1)S(1)}, bf16[4,256,128]{2,1,0:T(8,128)(2,1)S(1)}, u32[]{:S(2)}, u32[]{:S(2)}) collective-permute-start(bf16[4,256,128]{2,1,0:T(8,128)(2,1)S(1)} %gather.1.refs_0_), channel_id=1, source_target_pairs={{0,192},{64,0},{128,64},{192,128},{1,193},{65,1},{129,65},{193,129... | collective-permute-start | bytes 786440 | tf_op jit(solution)/shard_map/ppermute | solution.py:357
  48.1 4.8 %collective-permute-start.11 = (bf16[8,256,128]{2,1,0:T(8,128)(2,1)S(1)}, bf16[8,256,128]{2,1,0:T(8,128)(2,1)S(1)}, u32[]{:S(2)}, u32[]{:S(2)}) collective-permute-start(bf16[8,256,128]{2,1,0:T(8,128)(2,1)S(1)} %get-tuple-element.30.refs_0_), channel_id=1, source_target_pairs={{0,2},{2,0},{1,3},{3,1},{4,6},{6,4},{5,7},{7,5},{8,10},{10,8},{9,1... | collective-permute-start | bytes 1572872 | tf_op jit(solution)/shard_map/ppermute | solution.py:377
  48.2 15.4 %collective-permute-start.9 = (bf16[2,256,128]{2,1,0:T(8,128)(2,1)S(1)}, bf16[2,256,128]{2,1,0:T(8,128)(2,1)S(1)}, u32[]{:S(2)}, u32[]{:S(2)}) collective-permute-start(bf16[2,256,128]{2,1,0:T(8,128)(2,1)S(1)} %get-tuple-element.28), channel_id=1, source_target_pairs={{0,64},{64,128},{128,192},{192,0},{1,65},{65,129},{129,193},{193,1... | collective-permute-start | bytes 393224 | tf_op jit(solution)/shard_map/ppermute | solution.py:375
  51.8 11.8 %collective-permute-start.10 = (bf16[2,256,128]{2,1,0:T(8,128)(2,1)S(1)}, bf16[2,256,128]{2,1,0:T(8,128)(2,1)S(1)}, u32[]{:S(2)}, u32[]{:S(2)}) collective-permute-start(bf16[2,256,128]{2,1,0:T(8,128)(2,1)S(1)} %get-tuple-element.29), channel_id=1, source_target_pairs={{0,192},{64,0},{128,64},{192,128},{1,193},{65,1},{129,65},{193,129... | collective-permute-start | bytes 393224 | tf_op jit(solution)/shard_map/ppermute | solution.py:376
  63.6 1.6 %collective-permute-start.12 = (bf16[4,256,128]{2,1,0:T(8,128)(2,1)S(1)}, bf16[4,256,128]{2,1,0:T(8,128)(2,1)S(1)}, u32[]{:S(2)}, u32[]{:S(2)}) collective-permute-start(bf16[4,256,128]{2,1,0:T(8,128)(2,1)S(1)} %across.1.refs_0_), channel_id=1, source_target_pairs={{0,2},{2,0},{1,3},{3,1},{4,6},{6,4},{5,7},{7,5},{8,10},{10,8},{9,1... | collective-permute-start | bytes 786440 | tf_op jit(solution)/shard_map/ppermute | solution.py:379
  72.6 18.5 %all-to-all-start.1 = ((f32[4,528,128]{2,1,0:T(8,128)}), f32[4,528,128]{2,1,0:T(8,128)S(1)}, u32[]{:S(2)}, u32[]{:S(2)}) async-start(f32[4,528,128]{2,1,0:T(8,128)} %attend2.1.wait_ref), calls=%async_computation.1 | async-start | bytes 2162688 | tf_op jit(solution)/shard_map/all_to_all | solution.py:399
  77.5 6.7 %collective-permute-start.14 = (bf16[512,128]{1,0:T(8,128)(2,1)S(1)}, bf16[512,128]{1,0:T(8,128)(2,1)S(1)}, u32[]{:S(2)}, u32[]{:S(2)}) collective-permute-start(bf16[512,128]{1,0:T(8,128)(2,1)S(1)} %get-tuple-element.31), channel_id=1, source_target_pairs={{0,2},{2,4},{4,6},{6,8},{8,10},{10,12},{12,14},{14,16},{16,18},{18... | collective-permute-start | bytes 393224 | tf_op jit(solution)/shard_map/ppermute | solution.py:383
  77.6 20.2 %copy-start.8 = (s32[4,4]{1,0:T(4,128)S(1)}, s32[4,4]{1,0:T(4,128)}, u32[]{:S(2)}) copy-start(s32[4,4]{1,0:T(4,128)} %param.19) | copy-start | bytes 196
  77.6 20.3 %copy-start.7 = (s32[512,8]{0,1:T(8,128)S(1)}, s32[512,8]{0,1:T(8,128)}, u32[]{:S(2)}) copy-start(s32[512,8]{0,1:T(8,128)} %param.20) | copy-start | bytes 49156
  77.6 6.6 %collective-permute-start.15 = (bf16[512,128]{1,0:T(8,128)(2,1)S(1)}, bf16[512,128]{1,0:T(8,128)(2,1)S(1)}, u32[]{:S(2)}, u32[]{:S(2)}) collective-permute-start(bf16[512,128]{1,0:T(8,128)(2,1)S(1)} %get-tuple-element.32), channel_id=1, source_target_pairs={{2,0},{4,2},{6,4},{8,6},{10,8},{12,10},{14,12},{16,14},{18,16},{20... | collective-permute-start | bytes 393224 | tf_op jit(solution)/shard_map/ppermute | solution.py:384
  81.4 4.3 %collective-permute-start.13 = (bf16[128,256]{1,0:T(8,128)(2,1)S(1)}, bf16[128,256]{1,0:T(8,128)(2,1)S(1)}, u32[]{:S(2)}, u32[]{:S(2)}) collective-permute-start(bf16[128,256]{1,0:T(8,128)(2,1)S(1)} %copy-done.2), channel_id=1, source_target_pairs={{0,1},{1,0},{2,3},{3,2},{4,5},{5,4},{6,7},{7,6},{8,9},{9,8},{10,11... | collective-permute-start | bytes 196616 | tf_op jit(solution)/shard_map/ppermute | solution.py:335
  84.2 13.8 %copy-start.4 = (bf16[2,256,128]{2,1,0:T(8,128)(2,1)S(1)}, bf16[2,256,128]{2,1,0:T(8,128)(2,1)}, u32[]{:S(2)}) copy-start(bf16[2,256,128]{2,1,0:T(8,128)(2,1)} %ws_ref.1) | copy-start | bytes 393220
  84.2 13.8 %copy-start.5 = (bf16[2,256,128]{2,1,0:T(8,128)(2,1)S(1)}, bf16[2,256,128]{2,1,0:T(8,128)(2,1)}, u32[]{:S(2)}) copy-start(bf16[2,256,128]{2,1,0:T(8,128)(2,1)} %wt_ref.1) | copy-start | bytes 393220
  84.2 13.8 %collective-permute-start.16 = (bf16[1024,128]{1,0:T(8,128)(2,1)S(1)}, bf16[1024,128]{1,0:T(8,128)(2,1)S(1)}, u32[]{:S(2)}, u32[]{:S(2)}) collective-permute-start(bf16[1024,128]{1,0:T(8,128)(2,1)S(1)} %around.1.near_ref), channel_id=1, source_target_pairs={{0,1},{1,0},{2,3},{3,2},{4,5},{5,4},{6,7},{7,6},{8,9},{9,8},{10,11... | collective-permute-start | bytes 786440 | tf_op jit(solution)/shard_map/ppermute | solution.py:386
  91.8 13.3 %all-to-all-start.2 = ((bf16[8,128,128]{2,1,0:T(8,128)(2,1)}), bf16[8,128,128]{2,1,0:T(8,128)(2,1)S(1)}, u32[]{:S(2)}, u32[]{:S(2)}) async-start(bf16[8,128,128]{2,1,0:T(8,128)(2,1)} %mix.1), calls=%async_computation.2 | async-start | bytes 524288 | tf_op jit(solution)/shard_map/all_to_all | solution.py:400
  (5 other events, 28.6 us)

commit v4 on v3

--- a/solution.py
+++ b/solution.py
@@ -112,8 +112,7 @@
         ref[...] = keyval[d + 1]
 
 
-def query_kernel(partial_ref, rest_ref, other_ref, codes_ref, cells_ref, wait_ref, out_ref, cells_out):
-    cells_out[...] = cells_ref[...]
+def query_kernel(partial_ref, rest_ref, other_ref, codes_ref, out_ref):
     flat = (partial_ref[2] + dot(rest_ref[2], other_ref[...], NT)).astype(BF16)
     for head in range(4):
         for b in range(BLK_DEV):
@@ -335,6 +334,8 @@
     w_got = lax.ppermute(w_out, "h", swap)
     tops = [(z * 32 + 31, (z + 1) % 4 * 32 + 31) for z in range(4)]
     bottoms = [((z + 1) % 4 * 32, z * 32) for z in range(4)]
+    up = lax.ppermute(cells, everyone, tops)
+    down = lax.ppermute(cells, everyone, bottoms)
     places = jnp.stack([side, lax.axis_index("zh"), lax.axis_index("c"), lax.axis_index("x"), lax.axis_index("y")])
     partial, rest, codes = call(
         prepare_kernel,
@@ -356,15 +357,7 @@
     left = lax.ppermute(here, "zh", ring[1])
     right = lax.ppermute(here, "zh", ring[3])
     mate_here = lax.ppermute(here, "c", swap)
-    query, passed = call(
-        query_kernel,
-        [shaped((4, 144, BLOCK), BF16), shaped(cells.shape, BF16)],
-        [partial, rest, other, codes, cells],
-        "query",
-        after=[got[0]],
-    )
-    up = lax.ppermute(passed, everyone, tops)
-    down = lax.ppermute(passed, everyone, bottoms)
+    (query,) = call(query_kernel, [shaped((4, 144, BLOCK), BF16)], [partial, rest, other, codes], "query")
     (query,) = call(spread_kernel, [shaped((16, 144, BLOCK), BF16)], [query], "spread", after=[*got, up, down])
     q_all = lax.all_to_all(query, ("y", "x"), 0, 0).reshape(4, 4, 144, BLOCK)
     lists = lax.dynamic_slice_in_dim(q_all, BLOCK + 2 * lax.axis_index("y"), 2, 2)

time: 107 us -> 102 us (0.953)
  starting transfers between devices: 44.6 us -> 43 us
  waiting for transfers between devices: 23.7 us -> 22.2 us
    ppermute x3, waiting for transfers between devices: 7.11 us -> 2.61 us  [body(): got = [lax.ppermute(v, 'x', ring[d + 1]) for d, v in enumerate(sends)]]
    ppermute x1, starting transfers between devices: 0.08 us -> 1.76 us  [body(): left = lax.ppermute(here, 'zh', ring[1])]
    ppermute x1, starting transfers between devices: 4.12 us -> 2.46 us  [body(): right = lax.ppermute(here, 'zh', ring[3])]
    all_to_all x1, starting transfers between devices: 10.9 us -> 9.31 us  [body(): q_all = lax.all_to_all(query, ('y', 'x'), 0, 0).reshape(4, 4, 144, BLOCK)]
    ppermute x3, starting transfers between devices: 4.6 us -> 5.74 us  [body(): got = [lax.ppermute(v, 'x', ring[d + 1]) for d, v in enumerate(sends)]]
  transfers between devices with their start and end apart: 20 -> 20, of which waited for: 10 -> 10; matrix products, arithmetic and copies ran while one was open for 1% -> 1% of each run, Pallas kernels for 23% -> 24%
where the time goes in v4:
time: 102 us
  starting transfers between devices  43 us (42%)
  Pallas kernels  33.8 us (33%)
  waiting for transfers between devices  22.2 us (22%)
  local copies, waits for them, and re-layouts  1.84 us (2%)
    pallas_call x16, Pallas kernels, call(): pl.pallas_call(kernel, grid_spec=pltpu.PrefetchScalarGridSpec(num_scalar_...  33.8 us
    all_to_all x1, starting transfers between devices, body(): q_all = lax.all_to_all(query, ('y', 'x'), 0, 0).reshape(4, 4, 144, BLOCK)  9.31 us
    ppermute x3, starting transfers between devices, body(): got = [lax.ppermute(v, 'x', ring[d + 1]) for d, v in enumerate(sends)]  5.74 us
    all_to_all x1, waiting for transfers between devices, body(): lax.all_to_all(partial, 'y', 0, 0)  5.54 us
    all_to_all x1, starting transfers between devices, body(): mixed = lax.all_to_all(mixed, ('x', 'h'), 0, 0)  5.35 us
    all_to_all x1, starting transfers between devices, body(): lax.all_to_all(partial, 'y', 0, 0)  5.29 us
    all_to_all x1, waiting for transfers between devices, body(): q_all = lax.all_to_all(query, ('y', 'x'), 0, 0).reshape(4, 4, 144, BLOCK)  4.05 us
    ppermute x1, starting transfers between devices, body(): far_low = lax.ppermute(low, 'zh', ring[1])  3.65 us
  transfers between devices with their start and end apart: 20, of which 10 were waited for; matrix products, arithmetic and copies ran while one was open for 1% of the time, Pallas kernels for 24%

profile of v4, /device:TPU:8, one launch (start us, length us, event | category | flops | bytes accessed | tf_op | source)
XLA Modules:
  0.0 102.1 jit_solution(13269539947449283047)
XLA Ops:
  0.0 1.9 %collective-permute-start = (bf16[512,128]{1,0:T(8,128)(2,1)}, bf16[512,128]{1,0:T(8,128)(2,1)S(1)}, u32[]{:S(2)}, u32[]{:S(2)}) collective-permute-start(bf16[512,128]{1,0:T(8,128)(2,1)} %own_ref.1), channel_id=1, source_target_pairs={{0,1},{1,0},{2,3},{3,2},{4,5},{5,4},{6,7},{7,6},{8,9},{9,8},{10,11... | collective-permute-start | bytes 393224 | tf_op jit(solution)/shard_map/ppermute | solution.py:333
  5.9 1.1 %prepare.1 = (f32[3,128,512]{2,1,0:T(8,128)S(1)}, bf16[3,128,128]{2,1,0:T(8,128)(2,1)S(1)}, bf16[16,128]{1,0:T(8,128)(2,1)S(1)}) custom-call(s32[5]{0:T(128)S(1)} %stack.35.place_ref, bf16[512,128]{1,0:T(8,128)(2,1)S(1)} %copy-done, bf16[3,256,128]{2,1,0:T(8,128)(2,1)S(1)} %pad_maximum_fusion.weights_ref, s32[4,32]{1,0:T(4,128)S(1)} %copy-done.3), custom_call_target="tpu_custom_call" | custom-call | flops 1000000 | bytes 328192 | tf_op jit(solution)/shard_map/prepare/pallas_call | solution.py:38
  7.8 1.6 %collective-permute-start.1 = (bf16[256,128]{1,0:T(8,128)(2,1)S(1)}, bf16[256,128]{1,0:T(8,128)(2,1)S(1)}, u32[]{:S(2)}, u32[]{:S(2)}) collective-permute-start(bf16[256,128]{1,0:T(8,128)(2,1)S(1)} %get-tuple-element.20), channel_id=1, source_target_pairs={{0,4},{4,8},{8,12},{12,0},{1,5},{5,9},{9,13},{13,1},{2,6},{6,10},{... | collective-permute-start | bytes 196616 | tf_op jit(solution)/shard_map/ppermute | solution.py:355
  9.4 2.7 %collective-permute-start.2 = (bf16[256,128]{1,0:T(8,128)(2,1)S(1)}, bf16[256,128]{1,0:T(8,128)(2,1)S(1)}, u32[]{:S(2)}, u32[]{:S(2)}) collective-permute-start(bf16[256,128]{1,0:T(8,128)(2,1)S(1)} %get-tuple-element.21), channel_id=1, source_target_pairs={{0,8},{4,12},{8,0},{12,4},{1,9},{5,13},{9,1},{13,5},{2,10},{6,14},... | collective-permute-start | bytes 196616 | tf_op jit(solution)/shard_map/ppermute | solution.py:355
  12.1 1.4 %collective-permute-start.3 = (bf16[256,128]{1,0:T(8,128)(2,1)S(1)}, bf16[256,128]{1,0:T(8,128)(2,1)S(1)}, u32[]{:S(2)}, u32[]{:S(2)}) collective-permute-start(bf16[256,128]{1,0:T(8,128)(2,1)S(1)} %get-tuple-element.22), channel_id=1, source_target_pairs={{0,12},{4,0},{8,4},{12,8},{1,13},{5,1},{9,5},{13,9},{2,14},{6,2},{... | collective-permute-start | bytes 196616 | tf_op jit(solution)/shard_map/ppermute | solution.py:355
  14.1 1.1 %collective-permute-done.2.refs_1_ = bf16[256,128]{1,0:T(8,128)(2,1)S(1)} collective-permute-done((bf16[256,128]{1,0:T(8,128)(2,1)S(1)}, bf16[256,128]{1,0:T(8,128)(2,1)S(1)}, u32[]{:S(2)}, u32[]{:S(2)}) %collective-permute-start.2) | collective-permute-done | bytes 65568 | tf_op jit(solution)/shard_map/ppermute | solution.py:355
  15.2 1.2 %collective-permute-done.3.refs_2_ = bf16[256,128]{1,0:T(8,128)(2,1)S(1)} collective-permute-done((bf16[256,128]{1,0:T(8,128)(2,1)S(1)}, bf16[256,128]{1,0:T(8,128)(2,1)S(1)}, u32[]{:S(2)}, u32[]{:S(2)}) %collective-permute-start.3) | collective-permute-done | bytes 65568 | tf_op jit(solution)/shard_map/ppermute | solution.py:355
  17.3 9.3 %all-to-all-start = ((bf16[16,144,128]{2,1,0:T(8,128)(2,1)}), bf16[16,144,128]{2,1,0:T(8,128)(2,1)S(1)}, u32[]{:S(2)}, u32[]{:S(2)}) async-start(bf16[16,144,128]{2,1,0:T(8,128)(2,1)} %spread.1), calls=%async_computation | async-start | bytes 1179648 | tf_op jit(solution)/shard_map/all_to_all | solution.py:362
  27.2 1.8 %collective-permute-start.6 = (bf16[4,256,128]{2,1,0:T(8,128)(2,1)S(1)}, bf16[4,256,128]{2,1,0:T(8,128)(2,1)S(1)}, u32[]{:S(2)}, u32[]{:S(2)}) collective-permute-start(bf16[4,256,128]{2,1,0:T(8,128)(2,1)S(1)} %gather.1.refs_0_), channel_id=1, source_target_pairs={{0,64},{64,128},{128,192},{192,0},{1,65},{65,129},{129,193},{193,1... | collective-permute-start | bytes 786440 | tf_op jit(solution)/shard_map/ppermute | solution.py:357
  29.0 2.5 %collective-permute-start.7 = (bf16[4,256,128]{2,1,0:T(8,128)(2,1)S(1)}, bf16[4,256,128]{2,1,0:T(8,128)(2,1)S(1)}, u32[]{:S(2)}, u32[]{:S(2)}) collective-permute-start(bf16[4,256,128]{2,1,0:T(8,128)(2,1)S(1)} %gather.1.refs_0_), channel_id=1, source_target_pairs={{0,192},{64,0},{128,64},{192,128},{1,193},{65,1},{129,65},{193,129... | collective-permute-start | bytes 786440 | tf_op jit(solution)/shard_map/ppermute | solution.py:358
  31.5 4.1 %all-to-all-done = bf16[16,144,128]{2,1,0:T(8,128)(2,1)S(1)} async-done(((bf16[16,144,128]{2,1,0:T(8,128)(2,1)}), bf16[16,144,128]{2,1,0:T(8,128)(2,1)S(1)}, u32[]{:S(2)}, u32[]{:S(2)}) %all-to-all-start) | async-done | bytes 589856 | tf_op jit(solution)/shard_map/all_to_all | solution.py:362
  35.5 6.4 %attend0.1.after_ref.refs_2_ = f32[65,40,128]{2,1,0:T(8,128)S(1)} custom-call(s32[40,128]{1,0:T(8,128)S(1)} %pad_convert_fusion.list_ref, bf16[4,4,144,128]{3,2,1,0:T(8,128)(2,1)S(1)} %bitcast.11, bf16[4,256,128]{2,1,0:T(8,128)(2,1)S(1)} %gather.1.refs_0_, bf16[4,256,128]{2,1,0:T(8,128)(2,1)S(1)} %collective-permute-done.8.refs_1_), custom_call_target="tpu_custom_call" | custom-call | flops 1000000 | bytes 1114112 | tf_op jit(solution)/shard_map/attend0/pallas_call | solution.py:38
  42.0 2.2 %collective-permute-done.7.right_ref = bf16[4,256,128]{2,1,0:T(8,128)(2,1)S(1)} collective-permute-done((bf16[4,256,128]{2,1,0:T(8,128)(2,1)S(1)}, bf16[4,256,128]{2,1,0:T(8,128)(2,1)S(1)}, u32[]{:S(2)}, u32[]{:S(2)}) %collective-permute-start.7) | collective-permute-done | bytes 262176 | tf_op jit(solution)/shard_map/ppermute | solution.py:358
  44.3 3.6 %collective-permute-start.9 = (bf16[2,256,128]{2,1,0:T(8,128)(2,1)S(1)}, bf16[2,256,128]{2,1,0:T(8,128)(2,1)S(1)}, u32[]{:S(2)}, u32[]{:S(2)}) collective-permute-start(bf16[2,256,128]{2,1,0:T(8,128)(2,1)S(1)} %get-tuple-element.24), channel_id=1, source_target_pairs={{0,64},{64,128},{128,192},{192,0},{1,65},{65,129},{129,193},{193,1... | collective-permute-start | bytes 393224 | tf_op jit(solution)/shard_map/ppermute | solution.py:368
  48.6 9.6 %attend1.1.after_ref.refs_2_ = f32[65,40,128]{2,1,0:T(8,128)S(1)} custom-call(s32[40,128]{1,0:T(8,128)S(1)} %pad_convert_fusion.list_ref, bf16[4,4,144,128]{3,2,1,0:T(8,128)(2,1)S(1)} %bitcast.12, bf16[8,256,128]{2,1,0:T(8,128)(2,1)S(1)} %get-tuple-element.26.refs_0_, bf16[8,256,128]{2,1,0:T(8,128)(2,1)S(1)} %collective-permute-done.11.refs_1_, ...), custom_call_target="tpu_custom_call" | custom-call | flops 8999999488 | bytes 2969600 | tf_op jit(solution)/shard_map/attend1/pallas_call | solution.py:38
  58.5 1.3 %collective-permute-done.12.refs_1_ = bf16[4,256,128]{2,1,0:T(8,128)(2,1)S(1)} collective-permute-done((bf16[4,256,128]{2,1,0:T(8,128)(2,1)S(1)}, bf16[4,256,128]{2,1,0:T(8,128)(2,1)S(1)}, u32[]{:S(2)}, u32[]{:S(2)}) %collective-permute-start.12) | collective-permute-done | bytes 262176 | tf_op jit(solution)/shard_map/ppermute | solution.py:372
  59.8 7.8 %attend2.1.wait_ref = f32[4,528,128]{2,1,0:T(8,128)} custom-call(s32[40,128]{1,0:T(8,128)S(1)} %pad_convert_fusion.list_ref, bf16[4,4,144,128]{3,2,1,0:T(8,128)(2,1)S(1)} %bitcast.13, bf16[4,256,128]{2,1,0:T(8,128)(2,1)S(1)} %across.1.refs_0_, bf16[4,256,128]{2,1,0:T(8,128)(2,1)S(1)} %collective-permute-done.12.refs_1_, ...), custom_call_target="tpu_custom_call" | custom-call | flops 5000000000 | bytes 2445312 | tf_op jit(solution)/shard_map/attend2/pallas_call | solution.py:38
  67.6 5.3 %all-to-all-start.1 = ((f32[4,528,128]{2,1,0:T(8,128)}), f32[4,528,128]{2,1,0:T(8,128)S(1)}, u32[]{:S(2)}, u32[]{:S(2)}) async-start(f32[4,528,128]{2,1,0:T(8,128)} %attend2.1.wait_ref), calls=%async_computation.1 | async-start | bytes 2162688 | tf_op jit(solution)/shard_map/all_to_all | solution.py:392
  73.8 3.6 %collective-permute-start.15 = (bf16[512,128]{1,0:T(8,128)(2,1)S(1)}, bf16[512,128]{1,0:T(8,128)(2,1)S(1)}, u32[]{:S(2)}, u32[]{:S(2)}) collective-permute-start(bf16[512,128]{1,0:T(8,128)(2,1)S(1)} %get-tuple-element.28), channel_id=1, source_target_pairs={{2,0},{4,2},{6,4},{8,6},{10,8},{12,10},{14,12},{16,14},{18,16},{20... | collective-permute-start | bytes 393224 | tf_op jit(solution)/shard_map/ppermute | solution.py:377
  78.0 2.2 %collective-permute-done.14.before_ref = bf16[512,128]{1,0:T(8,128)(2,1)S(1)} collective-permute-done((bf16[512,128]{1,0:T(8,128)(2,1)S(1)}, bf16[512,128]{1,0:T(8,128)(2,1)S(1)}, u32[]{:S(2)}, u32[]{:S(2)}) %collective-permute-start.14) | collective-permute-done | bytes 131104 | tf_op jit(solution)/shard_map/ppermute | solution.py:376
  82.2 5.5 %all-to-all-done.1.part_ref = f32[4,528,128]{2,1,0:T(8,128)S(1)} async-done(((f32[4,528,128]{2,1,0:T(8,128)}), f32[4,528,128]{2,1,0:T(8,128)S(1)}, u32[]{:S(2)}, u32[]{:S(2)}) %all-to-all-start.1) | async-done | bytes 1081376 | tf_op jit(solution)/shard_map/all_to_all | solution.py:392
  88.5 5.3 %all-to-all-start.2 = ((bf16[8,128,128]{2,1,0:T(8,128)(2,1)}), bf16[8,128,128]{2,1,0:T(8,128)(2,1)S(1)}, u32[]{:S(2)}, u32[]{:S(2)}) async-start(bf16[8,128,128]{2,1,0:T(8,128)(2,1)} %mix.1), calls=%async_computation.2 | async-start | bytes 524288 | tf_op jit(solution)/shard_map/all_to_all | solution.py:393
  94.1 3.6 %edge.1.base_ref = f32[512,128]{1,0:T(8,128)S(1)} custom-call(s32[4,4]{1,0:T(4,128)S(1)} %fusion.4.wb_ref, s32[5]{0:T(128)S(1)} %stack.35.place_ref, bf16[512,128]{1,0:T(8,128)(2,1)S(1)} %copy-done.1, bf16[512,128]{1,0:T(8,128)(2,1)S(1)} %collective-permute-done.other_ref, bf16[1024,128]{1,0:T(8,128)(2,1)S(1)} %around.1.near_ref, ...), custom_call_target="tpu_custom_call" | custom-call | flops 4000000000 | bytes 1065984 | tf_op jit(solution)/shard_map/edge/pallas_call | solution.py:38
  97.7 3.5 %all-to-all-done.2.mixed_ref = bf16[8,128,128]{2,1,0:T(8,128)(2,1)S(1)} async-done(((bf16[8,128,128]{2,1,0:T(8,128)(2,1)}), bf16[8,128,128]{2,1,0:T(8,128)(2,1)S(1)}, u32[]{:S(2)}, u32[]{:S(2)}) %all-to-all-start.2) | async-done | bytes 262176 | tf_op jit(solution)/shard_map/all_to_all | solution.py:393
  (56 shorter events, 13.2 us)
Async XLA Ops:
  0.0 7.0 %collective-permute-start = (bf16[512,128]{1,0:T(8,128)(2,1)}, bf16[512,128]{1,0:T(8,128)(2,1)S(1)}, u32[]{:S(2)}, u32[]{:S(2)}) collective-permute-start(bf16[512,128]{1,0:T(8,128)(2,1)} %own_ref.1), channel_id=1, source_target_pairs={{0,1},{1,0},{2,3},{3,2},{4,5},{5,4},{6,7},{7,6},{8,9},{9,8},{10,11... | collective-permute-start | bytes 393224 | tf_op jit(solution)/shard_map/ppermute | solution.py:333
  1.9 11.8 %collective-permute-start.4 = (bf16[512,128]{1,0:T(8,128)(2,1)}, bf16[512,128]{1,0:T(8,128)(2,1)S(1)}, u32[]{:S(2)}, u32[]{:S(2)}) collective-permute-start(bf16[512,128]{1,0:T(8,128)(2,1)} %own_ref.1), channel_id=1, source_target_pairs={{62,126},{126,190},{190,254},{254,62},{63,127},{127,191},{191,255}... | collective-permute-start | bytes 393224 | tf_op jit(solution)/shard_map/ppermute | solution.py:337
  2.6 11.2 %collective-permute-start.5 = (bf16[512,128]{1,0:T(8,128)(2,1)}, bf16[512,128]{1,0:T(8,128)(2,1)S(1)}, u32[]{:S(2)}, u32[]{:S(2)}) collective-permute-start(bf16[512,128]{1,0:T(8,128)(2,1)} %own_ref.1), channel_id=1, source_target_pairs={{64,0},{128,64},{192,128},{0,192},{65,1},{129,65},{193,129},{1,193}} | collective-permute-start | bytes 393224 | tf_op jit(solution)/shard_map/ppermute | solution.py:338
  7.8 6.3 %collective-permute-start.1 = (bf16[256,128]{1,0:T(8,128)(2,1)S(1)}, bf16[256,128]{1,0:T(8,128)(2,1)S(1)}, u32[]{:S(2)}, u32[]{:S(2)}) collective-permute-start(bf16[256,128]{1,0:T(8,128)(2,1)S(1)} %get-tuple-element.20), channel_id=1, source_target_pairs={{0,4},{4,8},{8,12},{12,0},{1,5},{5,9},{9,13},{13,1},{2,6},{6,10},{... | collective-permute-start | bytes 196616 | tf_op jit(solution)/shard_map/ppermute | solution.py:355
  9.4 5.8 %collective-permute-start.2 = (bf16[256,128]{1,0:T(8,128)(2,1)S(1)}, bf16[256,128]{1,0:T(8,128)(2,1)S(1)}, u32[]{:S(2)}, u32[]{:S(2)}) collective-permute-start(bf16[256,128]{1,0:T(8,128)(2,1)S(1)} %get-tuple-element.21), channel_id=1, source_target_pairs={{0,8},{4,12},{8,0},{12,4},{1,9},{5,13},{9,1},{13,5},{2,10},{6,14},... | collective-permute-start | bytes 196616 | tf_op jit(solution)/shard_map/ppermute | solution.py:355
  12.1 4.3 %collective-permute-start.3 = (bf16[256,128]{1,0:T(8,128)(2,1)S(1)}, bf16[256,128]{1,0:T(8,128)(2,1)S(1)}, u32[]{:S(2)}, u32[]{:S(2)}) collective-permute-start(bf16[256,128]{1,0:T(8,128)(2,1)S(1)} %get-tuple-element.22), channel_id=1, source_target_pairs={{0,12},{4,0},{8,4},{12,8},{1,13},{5,1},{9,5},{13,9},{2,14},{6,2},{... | collective-permute-start | bytes 196616 | tf_op jit(solution)/shard_map/ppermute | solution.py:355
  17.3 18.2 %all-to-all-start = ((bf16[16,144,128]{2,1,0:T(8,128)(2,1)}), bf16[16,144,128]{2,1,0:T(8,128)(2,1)S(1)}, u32[]{:S(2)}, u32[]{:S(2)}) async-start(bf16[16,144,128]{2,1,0:T(8,128)(2,1)} %spread.1), calls=%async_computation | async-start | bytes 1179648 | tf_op jit(solution)/shard_map/all_to_all | solution.py:362
  27.1 8.4 %collective-permute-start.8 = (bf16[4,256,128]{2,1,0:T(8,128)(2,1)S(1)}, bf16[4,256,128]{2,1,0:T(8,128)(2,1)S(1)}, u32[]{:S(2)}, u32[]{:S(2)}) collective-permute-start(bf16[4,256,128]{2,1,0:T(8,128)(2,1)S(1)} %gather.1.refs_0_), channel_id=1, source_target_pairs={{0,2},{2,0},{1,3},{3,1},{4,6},{6,4},{5,7},{7,5},{8,10},{10,8},{9,1... | collective-permute-start | bytes 786440 | tf_op jit(solution)/shard_map/ppermute | solution.py:359
  27.2 14.8 %collective-permute-start.6 = (bf16[4,256,128]{2,1,0:T(8,128)(2,1)S(1)}, bf16[4,256,128]{2,1,0:T(8,128)(2,1)S(1)}, u32[]{:S(2)}, u32[]{:S(2)}) collective-permute-start(bf16[4,256,128]{2,1,0:T(8,128)(2,1)S(1)} %gather.1.refs_0_), channel_id=1, source_target_pairs={{0,64},{64,128},{128,192},{192,0},{1,65},{65,129},{129,193},{193,1... | collective-permute-start | bytes 786440 | tf_op jit(solution)/shard_map/ppermute | solution.py:357
  29.0 15.2 %collective-permute-start.7 = (bf16[4,256,128]{2,1,0:T(8,128)(2,1)S(1)}, bf16[4,256,128]{2,1,0:T(8,128)(2,1)S(1)}, u32[]{:S(2)}, u32[]{:S(2)}) collective-permute-start(bf16[4,256,128]{2,1,0:T(8,128)(2,1)S(1)} %gather.1.refs_0_), channel_id=1, source_target_pairs={{0,192},{64,0},{128,64},{192,128},{1,193},{65,1},{129,65},{193,129... | collective-permute-start | bytes 786440 | tf_op jit(solution)/shard_map/ppermute | solution.py:358
  44.2 4.3 %collective-permute-start.11 = (bf16[8,256,128]{2,1,0:T(8,128)(2,1)S(1)}, bf16[8,256,128]{2,1,0:T(8,128)(2,1)S(1)}, u32[]{:S(2)}, u32[]{:S(2)}) collective-permute-start(bf16[8,256,128]{2,1,0:T(8,128)(2,1)S(1)} %get-tuple-element.26.refs_0_), channel_id=1, source_target_pairs={{0,2},{2,0},{1,3},{3,1},{4,6},{6,4},{5,7},{7,5},{8,10},{10,8},{9,1... | collective-permute-start | bytes 1572872 | tf_op jit(solution)/shard_map/ppermute | solution.py:370
  44.3 13.8 %collective-permute-start.9 = (bf16[2,256,128]{2,1,0:T(8,128)(2,1)S(1)}, bf16[2,256,128]{2,1,0:T(8,128)(2,1)S(1)}, u32[]{:S(2)}, u32[]{:S(2)}) collective-permute-start(bf16[2,256,128]{2,1,0:T(8,128)(2,1)S(1)} %get-tuple-element.24), channel_id=1, source_target_pairs={{0,64},{64,128},{128,192},{192,0},{1,65},{65,129},{129,193},{193,1... | collective-permute-start | bytes 393224 | tf_op jit(solution)/shard_map/ppermute | solution.py:368
  48.0 10.2 %collective-permute-start.10 = (bf16[2,256,128]{2,1,0:T(8,128)(2,1)S(1)}, bf16[2,256,128]{2,1,0:T(8,128)(2,1)S(1)}, u32[]{:S(2)}, u32[]{:S(2)}) collective-permute-start(bf16[2,256,128]{2,1,0:T(8,128)(2,1)S(1)} %get-tuple-element.25), channel_id=1, source_target_pairs={{0,192},{64,0},{128,64},{192,128},{1,193},{65,1},{129,65},{193,129... | collective-permute-start | bytes 393224 | tf_op jit(solution)/shard_map/ppermute | solution.py:369
  58.2 1.6 %collective-permute-start.12 = (bf16[4,256,128]{2,1,0:T(8,128)(2,1)S(1)}, bf16[4,256,128]{2,1,0:T(8,128)(2,1)S(1)}, u32[]{:S(2)}, u32[]{:S(2)}) collective-permute-start(bf16[4,256,128]{2,1,0:T(8,128)(2,1)S(1)} %across.1.refs_0_), channel_id=1, source_target_pairs={{0,2},{2,0},{1,3},{3,1},{4,6},{6,4},{5,7},{7,5},{8,10},{10,8},{9,1... | collective-permute-start | bytes 786440 | tf_op jit(solution)/shard_map/ppermute | solution.py:372
  67.6 20.2 %all-to-all-start.1 = ((f32[4,528,128]{2,1,0:T(8,128)}), f32[4,528,128]{2,1,0:T(8,128)S(1)}, u32[]{:S(2)}, u32[]{:S(2)}) async-start(f32[4,528,128]{2,1,0:T(8,128)} %attend2.1.wait_ref), calls=%async_computation.1 | async-start | bytes 2162688 | tf_op jit(solution)/shard_map/all_to_all | solution.py:392
  73.5 6.7 %collective-permute-start.14 = (bf16[512,128]{1,0:T(8,128)(2,1)S(1)}, bf16[512,128]{1,0:T(8,128)(2,1)S(1)}, u32[]{:S(2)}, u32[]{:S(2)}) collective-permute-start(bf16[512,128]{1,0:T(8,128)(2,1)S(1)} %get-tuple-element.27), channel_id=1, source_target_pairs={{0,2},{2,4},{4,6},{6,8},{8,10},{10,12},{12,14},{14,16},{16,18},{18... | collective-permute-start | bytes 393224 | tf_op jit(solution)/shard_map/ppermute | solution.py:376
  73.8 20.1 %copy-start.8 = (s32[4,4]{1,0:T(4,128)S(1)}, s32[4,4]{1,0:T(4,128)}, u32[]{:S(2)}) copy-start(s32[4,4]{1,0:T(4,128)} %param.19) | copy-start | bytes 196
  73.8 20.1 %copy-start.7 = (s32[512,8]{0,1:T(8,128)S(1)}, s32[512,8]{0,1:T(8,128)}, u32[]{:S(2)}) copy-start(s32[512,8]{0,1:T(8,128)} %param.20) | copy-start | bytes 49156
  73.8 6.4 %collective-permute-start.15 = (bf16[512,128]{1,0:T(8,128)(2,1)S(1)}, bf16[512,128]{1,0:T(8,128)(2,1)S(1)}, u32[]{:S(2)}, u32[]{:S(2)}) collective-permute-start(bf16[512,128]{1,0:T(8,128)(2,1)S(1)} %get-tuple-element.28), channel_id=1, source_target_pairs={{2,0},{4,2},{6,4},{8,6},{10,8},{12,10},{14,12},{16,14},{18,16},{20... | collective-permute-start | bytes 393224 | tf_op jit(solution)/shard_map/ppermute | solution.py:377
  77.4 4.3 %collective-permute-start.13 = (bf16[128,256]{1,0:T(8,128)(2,1)S(1)}, bf16[128,256]{1,0:T(8,128)(2,1)S(1)}, u32[]{:S(2)}, u32[]{:S(2)}) collective-permute-start(bf16[128,256]{1,0:T(8,128)(2,1)S(1)} %copy-done.2), channel_id=1, source_target_pairs={{0,1},{1,0},{2,3},{3,2},{4,5},{5,4},{6,7},{7,6},{8,9},{9,8},{10,11... | collective-permute-start | bytes 196616 | tf_op jit(solution)/shard_map/ppermute | solution.py:334
  80.2 13.9 %copy-start.4 = (bf16[2,256,128]{2,1,0:T(8,128)(2,1)S(1)}, bf16[2,256,128]{2,1,0:T(8,128)(2,1)}, u32[]{:S(2)}) copy-start(bf16[2,256,128]{2,1,0:T(8,128)(2,1)} %ws_ref.1) | copy-start | bytes 393220
  80.2 13.9 %copy-start.5 = (bf16[2,256,128]{2,1,0:T(8,128)(2,1)S(1)}, bf16[2,256,128]{2,1,0:T(8,128)(2,1)}, u32[]{:S(2)}) copy-start(bf16[2,256,128]{2,1,0:T(8,128)(2,1)} %wt_ref.1) | copy-start | bytes 393220
  80.2 13.8 %collective-permute-start.16 = (bf16[1024,128]{1,0:T(8,128)(2,1)S(1)}, bf16[1024,128]{1,0:T(8,128)(2,1)S(1)}, u32[]{:S(2)}, u32[]{:S(2)}) collective-permute-start(bf16[1024,128]{1,0:T(8,128)(2,1)S(1)} %around.1.near_ref), channel_id=1, source_target_pairs={{0,1},{1,0},{2,3},{3,2},{4,5},{5,4},{6,7},{7,6},{8,9},{9,8},{10,11... | collective-permute-start | bytes 786440 | tf_op jit(solution)/shard_map/ppermute | solution.py:379
  88.5 12.6 %all-to-all-start.2 = ((bf16[8,128,128]{2,1,0:T(8,128)(2,1)}), bf16[8,128,128]{2,1,0:T(8,128)(2,1)S(1)}, u32[]{:S(2)}, u32[]{:S(2)}) async-start(bf16[8,128,128]{2,1,0:T(8,128)(2,1)} %mix.1), calls=%async_computation.2 | async-start | bytes 524288 | tf_op jit(solution)/shard_map/all_to_all | solution.py:393
  (5 other events, 30.6 us)

commit v5 on v4

--- a/solution.py
+++ b/solution.py
@@ -133,14 +133,14 @@
         out_ref[(place_ref[3] - d) & 3] = ref[...]
 
 
-def relay_kernel(left_ref, right_ref, after_ref, low_ref, high_ref, both_ref):
+def relay_kernel(left_ref, right_ref, after_ref, up_ref, down_ref, low_ref, high_ref, both_ref):
     low_ref[...] = left_ref[:2]
     high_ref[...] = right_ref[2:]
     both_ref[:4] = left_ref[...]
     both_ref[4:] = right_ref[...]
 
 
-def pass_kernel(low_ref, high_ref, after_ref, out_ref):
+def across_kernel(low_ref, high_ref, after_ref, out_ref):
     out_ref[:2] = low_ref[...]
     out_ref[2:] = high_ref[...]
 
@@ -150,6 +150,10 @@
     cells = cells_ref[...]
     before_ref[...] = jnp.where(spot == 31, up_ref[...], cells)
     after_ref[...] = jnp.where(spot == 0, down_ref[...], cells)
+
+
+def pass_kernel(cells_ref, after_ref, out_ref):
+    out_ref[...] = cells_ref[...]
 
 
 def pair_kernel(before_ref, after_ref, out_ref):
@@ -334,8 +338,6 @@
     w_got = lax.ppermute(w_out, "h", swap)
     tops = [(z * 32 + 31, (z + 1) % 4 * 32 + 31) for z in range(4)]
     bottoms = [((z + 1) % 4 * 32, z * 32) for z in range(4)]
-    up = lax.ppermute(cells, everyone, tops)
-    down = lax.ppermute(cells, everyone, bottoms)
     places = jnp.stack([side, lax.axis_index("zh"), lax.axis_index("c"), lax.axis_index("x"), lax.axis_index("y")])
     partial, rest, codes = call(
         prepare_kernel,
@@ -357,18 +359,21 @@
     left = lax.ppermute(here, "zh", ring[1])
     right = lax.ppermute(here, "zh", ring[3])
     mate_here = lax.ppermute(here, "c", swap)
+    (passed,) = call(pass_kernel, [shaped(cells.shape, BF16)], [cells], "passed", after=[mate_here])
+    up = lax.ppermute(passed, everyone, tops)
+    down = lax.ppermute(passed, everyone, bottoms)
     (query,) = call(query_kernel, [shaped((4, 144, BLOCK), BF16)], [partial, rest, other, codes], "query")
-    (query,) = call(spread_kernel, [shaped((16, 144, BLOCK), BF16)], [query], "spread", after=[*got, up, down])
+    (query,) = call(spread_kernel, [shaped((16, 144, BLOCK), BF16)], [query], "spread", after=got)
     q_all = lax.all_to_all(query, ("y", "x"), 0, 0).reshape(4, 4, 144, BLOCK)
     lists = lax.dynamic_slice_in_dim(q_all, BLOCK + 2 * lax.axis_index("y"), 2, 2)
     lists = jnp.pad(lists.reshape(32, BLOCK).astype(jnp.int32), ((0, 8), (0, 0)), constant_values=EMPTY)
     partial = attend(0, lists, q_all, [here, mate_here], None, 10**6)
     shapes = [shaped((n, 256, BLOCK), BF16) for n in (2, 2, 8)]
-    low, high, both = call(relay_kernel, shapes, [left, right], "relay", after=[partial])
+    low, high, both = call(relay_kernel, shapes, [left, right], "relay", after=[partial, up, down])
     far_low = lax.ppermute(low, "zh", ring[1])
     far_high = lax.ppermute(high, "zh", ring[3])
     partial = attend(1, lists, q_all, [both, lax.ppermute(both, "c", swap)], partial, 9 * 10**9)
-    (across,) = call(pass_kernel, [shaped((4, 256, BLOCK), BF16)], [far_low, far_high], "across", after=[partial])
+    (across,) = call(across_kernel, [shaped((4, 256, BLOCK), BF16)], [far_low, far_high], "across", after=[partial])
     partial = attend(2, lists, q_all, [across, lax.ppermute(across, "c", swap)], partial, 5 * 10**9)
     plane = [(i, (i + 1) % 32) for i in range(32)]
     ends = [shaped((rows, BLOCK), BF16)] * 2

time: 102 us -> 103 us (level); the launches traced: 102 us -> 102 us
    all_to_all x1, waiting for transfers between devices: 4.05 us -> 0.51 us  [body(): q_all = lax.all_to_all(query, ('y', 'x'), 0, 0).reshape(4, 4, 144, BLOCK)]
    ppermute x1, waiting for transfers between devices: 2.15 us -> 4.81 us  [body(): right = lax.ppermute(here, 'zh', ring[3])]
    all_to_all x1, starting transfers between devices: 9.31 us -> 7.01 us  [body(): q_all = lax.all_to_all(query, ('y', 'x'), 0, 0).reshape(4, 4, 144, BLOCK)]
    all_to_all x1, waiting for transfers between devices: 5.54 us -> 3.82 us  [body(): lax.all_to_all(partial, 'y', 0, 0)]
    ppermute x1, starting transfers between devices: 1.76 us -> 3.35 us  [body(): left = lax.ppermute(here, 'zh', ring[1])]
    all_to_all x1, starting transfers between devices: 5.29 us -> 6.52 us  [body(): lax.all_to_all(partial, 'y', 0, 0)]
    pallas_call x16 -> x17, Pallas kernels: 33.8 us -> 34.2 us  [call(): pl.pallas_call(kernel, grid_spec=pltpu.PrefetchScalarGridSpec(num_scalar_...]
  transfers between devices with their start and end apart: 20 -> 20, of which waited for: 10 -> 11; matrix products, arithmetic and copies ran while one was open for 1% -> 1% of each run, Pallas kernels for 24% -> 23%
where the time goes in v5:
time: 103 us; the launch traced here: 102 us
  starting transfers between devices  43.5 us (42%)
  Pallas kernels  34.2 us (33%)
  waiting for transfers between devices  21.2 us (21%)
  local copies, waits for them, and re-layouts  1.84 us (2%)
    pallas_call x17, Pallas kernels, call(): pl.pallas_call(kernel, grid_spec=pltpu.PrefetchScalarGridSpec(num_scalar_...  34.2 us
    all_to_all x1, starting transfers between devices, body(): q_all = lax.all_to_all(query, ('y', 'x'), 0, 0).reshape(4, 4, 144, BLOCK)  7.01 us
    all_to_all x1, starting transfers between devices, body(): lax.all_to_all(partial, 'y', 0, 0)  6.52 us
    ppermute x3, starting transfers between devices, body(): got = [lax.ppermute(v, 'x', ring[d + 1]) for d, v in enumerate(sends)]  5.73 us
    all_to_all x1, starting transfers between devices, body(): mixed = lax.all_to_all(mixed, ('x', 'h'), 0, 0)  5.41 us
    ppermute x1, waiting for transfers between devices, body(): right = lax.ppermute(here, 'zh', ring[3])  4.81 us
    ppermute x1, starting transfers between devices, body(): far_low = lax.ppermute(low, 'zh', ring[1])  3.93 us
    ppermute x1, starting transfers between devices, body(): after = lax.ppermute(after, ('y', 'x', 'c'), [(j, i) for i, j in plane])  3.82 us
  transfers between devices with their start and end apart: 20, of which 11 were waited for; matrix products, arithmetic and copies ran while one was open for 1% of the time, Pallas kernels for 23%

profile of v5, /device:TPU:8, one launch (start us, length us, event | category | flops | bytes accessed | tf_op | source)
XLA Modules:
  0.0 102.0 jit_solution(5186287058153932957)
XLA Ops:
  0.0 1.9 %collective-permute-start = (bf16[512,128]{1,0:T(8,128)(2,1)}, bf16[512,128]{1,0:T(8,128)(2,1)S(1)}, u32[]{:S(2)}, u32[]{:S(2)}) collective-permute-start(bf16[512,128]{1,0:T(8,128)(2,1)} %own_ref.1), channel_id=1, source_target_pairs={{0,1},{1,0},{2,3},{3,2},{4,5},{5,4},{6,7},{7,6},{8,9},{9,8},{10,11... | collective-permute-start | bytes 393224 | tf_op jit(solution)/shard_map/ppermute | solution.py:337
  4.5 1.1 %prepare.1 = (f32[3,128,512]{2,1,0:T(8,128)S(1)}, bf16[3,128,128]{2,1,0:T(8,128)(2,1)S(1)}, bf16[16,128]{1,0:T(8,128)(2,1)S(1)}) custom-call(s32[5]{0:T(128)S(1)} %stack.35.place_ref, bf16[512,128]{1,0:T(8,128)(2,1)S(1)} %copy-done, bf16[3,256,128]{2,1,0:T(8,128)(2,1)S(1)} %pad_maximum_fusion.weights_ref, s32[4,32]{1,0:T(4,128)S(1)} %copy-done.3), custom_call_target="tpu_custom_call" | custom-call | flops 1000000 | bytes 328192 | tf_op jit(solution)/shard_map/prepare/pallas_call | solution.py:38
  6.5 1.6 %collective-permute-start.1 = (bf16[256,128]{1,0:T(8,128)(2,1)S(1)}, bf16[256,128]{1,0:T(8,128)(2,1)S(1)}, u32[]{:S(2)}, u32[]{:S(2)}) collective-permute-start(bf16[256,128]{1,0:T(8,128)(2,1)S(1)} %get-tuple-element.20), channel_id=1, source_target_pairs={{0,4},{4,8},{8,12},{12,0},{1,5},{5,9},{9,13},{13,1},{2,6},{6,10},{... | collective-permute-start | bytes 196616 | tf_op jit(solution)/shard_map/ppermute | solution.py:357
  8.0 2.7 %collective-permute-start.2 = (bf16[256,128]{1,0:T(8,128)(2,1)S(1)}, bf16[256,128]{1,0:T(8,128)(2,1)S(1)}, u32[]{:S(2)}, u32[]{:S(2)}) collective-permute-start(bf16[256,128]{1,0:T(8,128)(2,1)S(1)} %get-tuple-element.21), channel_id=1, source_target_pairs={{0,8},{4,12},{8,0},{12,4},{1,9},{5,13},{9,1},{13,5},{2,10},{6,14},... | collective-permute-start | bytes 196616 | tf_op jit(solution)/shard_map/ppermute | solution.py:357
  10.8 1.4 %collective-permute-start.3 = (bf16[256,128]{1,0:T(8,128)(2,1)S(1)}, bf16[256,128]{1,0:T(8,128)(2,1)S(1)}, u32[]{:S(2)}, u32[]{:S(2)}) collective-permute-start(bf16[256,128]{1,0:T(8,128)(2,1)S(1)} %get-tuple-element.22), channel_id=1, source_target_pairs={{0,12},{4,0},{8,4},{12,8},{1,13},{5,1},{9,5},{13,9},{2,14},{6,2},{... | collective-permute-start | bytes 196616 | tf_op jit(solution)/shard_map/ppermute | solution.py:357
  12.7 1.1 %collective-permute-done.2.refs_1_ = bf16[256,128]{1,0:T(8,128)(2,1)S(1)} collective-permute-done((bf16[256,128]{1,0:T(8,128)(2,1)S(1)}, bf16[256,128]{1,0:T(8,128)(2,1)S(1)}, u32[]{:S(2)}, u32[]{:S(2)}) %collective-permute-start.2) | collective-permute-done | bytes 65568 | tf_op jit(solution)/shard_map/ppermute | solution.py:357
  13.8 1.2 %collective-permute-done.3.refs_2_ = bf16[256,128]{1,0:T(8,128)(2,1)S(1)} collective-permute-done((bf16[256,128]{1,0:T(8,128)(2,1)S(1)}, bf16[256,128]{1,0:T(8,128)(2,1)S(1)}, u32[]{:S(2)}, u32[]{:S(2)}) %collective-permute-start.3) | collective-permute-done | bytes 65568 | tf_op jit(solution)/shard_map/ppermute | solution.py:357
  15.9 7.0 %all-to-all-start = ((bf16[16,144,128]{2,1,0:T(8,128)(2,1)}), bf16[16,144,128]{2,1,0:T(8,128)(2,1)S(1)}, u32[]{:S(2)}, u32[]{:S(2)}) async-start(bf16[16,144,128]{2,1,0:T(8,128)(2,1)} %spread.1), calls=%async_computation | async-start | bytes 1179648 | tf_op jit(solution)/shard_map/all_to_all | solution.py:367
  23.6 3.3 %collective-permute-start.4 = (bf16[4,256,128]{2,1,0:T(8,128)(2,1)S(1)}, bf16[4,256,128]{2,1,0:T(8,128)(2,1)S(1)}, u32[]{:S(2)}, u32[]{:S(2)}) collective-permute-start(bf16[4,256,128]{2,1,0:T(8,128)(2,1)S(1)} %gather.1.refs_0_), channel_id=1, source_target_pairs={{0,64},{64,128},{128,192},{192,0},{1,65},{65,129},{129,193},{193,1... | collective-permute-start | bytes 786440 | tf_op jit(solution)/shard_map/ppermute | solution.py:359
  26.9 2.9 %collective-permute-start.5 = (bf16[4,256,128]{2,1,0:T(8,128)(2,1)S(1)}, bf16[4,256,128]{2,1,0:T(8,128)(2,1)S(1)}, u32[]{:S(2)}, u32[]{:S(2)}) collective-permute-start(bf16[4,256,128]{2,1,0:T(8,128)(2,1)S(1)} %gather.1.refs_0_), channel_id=1, source_target_pairs={{0,192},{64,0},{128,64},{192,128},{1,193},{65,1},{129,65},{193,129... | collective-permute-start | bytes 786440 | tf_op jit(solution)/shard_map/ppermute | solution.py:360
  31.8 6.4 %attend0.1.after_ref.refs_2_ = f32[65,40,128]{2,1,0:T(8,128)S(1)} custom-call(s32[40,128]{1,0:T(8,128)S(1)} %pad_convert_fusion.list_ref, bf16[4,4,144,128]{3,2,1,0:T(8,128)(2,1)S(1)} %bitcast.11, bf16[4,256,128]{2,1,0:T(8,128)(2,1)S(1)} %gather.1.refs_0_, bf16[4,256,128]{2,1,0:T(8,128)(2,1)S(1)} %collective-permute-done.6.refs_1_.after_ref), custom_call_target="tpu_custom_call" | custom-call | flops 1000000 | bytes 1114112 | tf_op jit(solution)/shard_map/attend0/pallas_call | solution.py:38
  38.6 4.8 %collective-permute-done.5.right_ref = bf16[4,256,128]{2,1,0:T(8,128)(2,1)S(1)} collective-permute-done((bf16[4,256,128]{2,1,0:T(8,128)(2,1)S(1)}, bf16[4,256,128]{2,1,0:T(8,128)(2,1)S(1)}, u32[]{:S(2)}, u32[]{:S(2)}) %collective-permute-start.5) | collective-permute-done | bytes 262176 | tf_op jit(solution)/shard_map/ppermute | solution.py:360
  43.6 3.9 %collective-permute-start.9 = (bf16[2,256,128]{2,1,0:T(8,128)(2,1)S(1)}, bf16[2,256,128]{2,1,0:T(8,128)(2,1)S(1)}, u32[]{:S(2)}, u32[]{:S(2)}) collective-permute-start(bf16[2,256,128]{2,1,0:T(8,128)(2,1)S(1)} %get-tuple-element.24), channel_id=1, source_target_pairs={{0,64},{64,128},{128,192},{192,0},{1,65},{65,129},{129,193},{193,1... | collective-permute-start | bytes 393224 | tf_op jit(solution)/shard_map/ppermute | solution.py:373
  47.9 9.9 %attend1.1.after_ref.refs_2_ = f32[65,40,128]{2,1,0:T(8,128)S(1)} custom-call(s32[40,128]{1,0:T(8,128)S(1)} %pad_convert_fusion.list_ref, bf16[4,4,144,128]{3,2,1,0:T(8,128)(2,1)S(1)} %bitcast.12, bf16[8,256,128]{2,1,0:T(8,128)(2,1)S(1)} %get-tuple-element.26.refs_0_, bf16[8,256,128]{2,1,0:T(8,128)(2,1)S(1)} %collective-permute-done.11.refs_1_, ...), custom_call_target="tpu_custom_call" | custom-call | flops 8999999488 | bytes 2969600 | tf_op jit(solution)/shard_map/attend1/pallas_call | solution.py:38
  58.0 1.5 %collective-permute-done.12.refs_1_ = bf16[4,256,128]{2,1,0:T(8,128)(2,1)S(1)} collective-permute-done((bf16[4,256,128]{2,1,0:T(8,128)(2,1)S(1)}, bf16[4,256,128]{2,1,0:T(8,128)(2,1)S(1)}, u32[]{:S(2)}, u32[]{:S(2)}) %collective-permute-start.12) | collective-permute-done | bytes 262176 | tf_op jit(solution)/shard_map/ppermute | solution.py:377
  59.5 7.8 %attend2.1.wait_ref = f32[4,528,128]{2,1,0:T(8,128)} custom-call(s32[40,128]{1,0:T(8,128)S(1)} %pad_convert_fusion.list_ref, bf16[4,4,144,128]{3,2,1,0:T(8,128)(2,1)S(1)} %bitcast.13, bf16[4,256,128]{2,1,0:T(8,128)(2,1)S(1)} %across.1.refs_0_, bf16[4,256,128]{2,1,0:T(8,128)(2,1)S(1)} %collective-permute-done.12.refs_1_, ...), custom_call_target="tpu_custom_call" | custom-call | flops 5000000000 | bytes 2445312 | tf_op jit(solution)/shard_map/attend2/pallas_call | solution.py:38
  67.2 6.5 %all-to-all-start.1 = ((f32[4,528,128]{2,1,0:T(8,128)}), f32[4,528,128]{2,1,0:T(8,128)S(1)}, u32[]{:S(2)}, u32[]{:S(2)}) async-start(f32[4,528,128]{2,1,0:T(8,128)} %attend2.1.wait_ref), calls=%async_computation.1 | async-start | bytes 2162688 | tf_op jit(solution)/shard_map/all_to_all | solution.py:397
  74.5 3.8 %collective-permute-start.15 = (bf16[512,128]{1,0:T(8,128)(2,1)S(1)}, bf16[512,128]{1,0:T(8,128)(2,1)S(1)}, u32[]{:S(2)}, u32[]{:S(2)}) collective-permute-start(bf16[512,128]{1,0:T(8,128)(2,1)S(1)} %get-tuple-element.28), channel_id=1, source_target_pairs={{2,0},{4,2},{6,4},{8,6},{10,8},{12,10},{14,12},{16,14},{18,16},{20... | collective-permute-start | bytes 393224 | tf_op jit(solution)/shard_map/ppermute | solution.py:382
  78.7 2.3 %collective-permute-done.14.before_ref = bf16[512,128]{1,0:T(8,128)(2,1)S(1)} collective-permute-done((bf16[512,128]{1,0:T(8,128)(2,1)S(1)}, bf16[512,128]{1,0:T(8,128)(2,1)S(1)}, u32[]{:S(2)}, u32[]{:S(2)}) %collective-permute-start.14) | collective-permute-done | bytes 131104 | tf_op jit(solution)/shard_map/ppermute | solution.py:381
  81.6 1.6 %collective-permute-done.13.w_other_ref = bf16[128,256]{1,0:T(8,128)(2,1)S(1)} collective-permute-done((bf16[128,256]{1,0:T(8,128)(2,1)S(1)}, bf16[128,256]{1,0:T(8,128)(2,1)S(1)}, u32[]{:S(2)}, u32[]{:S(2)}) %collective-permute-start.13) | collective-permute-done | bytes 65568 | tf_op jit(solution)/shard_map/ppermute | solution.py:338
  83.8 3.8 %all-to-all-done.1.part_ref = f32[4,528,128]{2,1,0:T(8,128)S(1)} async-done(((f32[4,528,128]{2,1,0:T(8,128)}), f32[4,528,128]{2,1,0:T(8,128)S(1)}, u32[]{:S(2)}, u32[]{:S(2)}) %all-to-all-start.1) | async-done | bytes 1081376 | tf_op jit(solution)/shard_map/all_to_all | solution.py:397
  88.4 5.4 %all-to-all-start.2 = ((bf16[8,128,128]{2,1,0:T(8,128)(2,1)}), bf16[8,128,128]{2,1,0:T(8,128)(2,1)S(1)}, u32[]{:S(2)}, u32[]{:S(2)}) async-start(bf16[8,128,128]{2,1,0:T(8,128)(2,1)} %mix.1), calls=%async_computation.2 | async-start | bytes 524288 | tf_op jit(solution)/shard_map/all_to_all | solution.py:398
  94.0 3.6 %edge.1.base_ref = f32[512,128]{1,0:T(8,128)S(1)} custom-call(s32[4,4]{1,0:T(4,128)S(1)} %fusion.4.wb_ref, s32[5]{0:T(128)S(1)} %stack.35.place_ref, bf16[512,128]{1,0:T(8,128)(2,1)S(1)} %copy-done.1, bf16[512,128]{1,0:T(8,128)(2,1)S(1)} %collective-permute-done.other_ref, bf16[1024,128]{1,0:T(8,128)(2,1)S(1)} %around.1.near_ref, ...), custom_call_target="tpu_custom_call" | custom-call | flops 4000000000 | bytes 1065984 | tf_op jit(solution)/shard_map/edge/pallas_call | solution.py:38
  97.6 3.5 %all-to-all-done.2.mixed_ref = bf16[8,128,128]{2,1,0:T(8,128)(2,1)S(1)} async-done(((bf16[8,128,128]{2,1,0:T(8,128)(2,1)}), bf16[8,128,128]{2,1,0:T(8,128)(2,1)S(1)}, u32[]{:S(2)}, u32[]{:S(2)}) %all-to-all-start.2) | async-done | bytes 262176 | tf_op jit(solution)/shard_map/all_to_all | solution.py:398
  (57 shorter events, 12.4 us)
Async XLA Ops:
  0.0 5.7 %collective-permute-start = (bf16[512,128]{1,0:T(8,128)(2,1)}, bf16[512,128]{1,0:T(8,128)(2,1)S(1)}, u32[]{:S(2)}, u32[]{:S(2)}) collective-permute-start(bf16[512,128]{1,0:T(8,128)(2,1)} %own_ref.1), channel_id=1, source_target_pairs={{0,1},{1,0},{2,3},{3,2},{4,5},{5,4},{6,7},{7,6},{8,9},{9,8},{10,11... | collective-permute-start | bytes 393224 | tf_op jit(solution)/shard_map/ppermute | solution.py:337
  6.5 6.3 %collective-permute-start.1 = (bf16[256,128]{1,0:T(8,128)(2,1)S(1)}, bf16[256,128]{1,0:T(8,128)(2,1)S(1)}, u32[]{:S(2)}, u32[]{:S(2)}) collective-permute-start(bf16[256,128]{1,0:T(8,128)(2,1)S(1)} %get-tuple-element.20), channel_id=1, source_target_pairs={{0,4},{4,8},{8,12},{12,0},{1,5},{5,9},{9,13},{13,1},{2,6},{6,10},{... | collective-permute-start | bytes 196616 | tf_op jit(solution)/shard_map/ppermute | solution.py:357
  8.0 5.8 %collective-permute-start.2 = (bf16[256,128]{1,0:T(8,128)(2,1)S(1)}, bf16[256,128]{1,0:T(8,128)(2,1)S(1)}, u32[]{:S(2)}, u32[]{:S(2)}) collective-permute-start(bf16[256,128]{1,0:T(8,128)(2,1)S(1)} %get-tuple-element.21), channel_id=1, source_target_pairs={{0,8},{4,12},{8,0},{12,4},{1,9},{5,13},{9,1},{13,5},{2,10},{6,14},... | collective-permute-start | bytes 196616 | tf_op jit(solution)/shard_map/ppermute | solution.py:357
  10.8 4.3 %collective-permute-start.3 = (bf16[256,128]{1,0:T(8,128)(2,1)S(1)}, bf16[256,128]{1,0:T(8,128)(2,1)S(1)}, u32[]{:S(2)}, u32[]{:S(2)}) collective-permute-start(bf16[256,128]{1,0:T(8,128)(2,1)S(1)} %get-tuple-element.22), channel_id=1, source_target_pairs={{0,12},{4,0},{8,4},{12,8},{1,13},{5,1},{9,5},{13,9},{2,14},{6,2},{... | collective-permute-start | bytes 196616 | tf_op jit(solution)/shard_map/ppermute | solution.py:357
  12.4 17.5 %copy-start.1 = (bf16[512,128]{1,0:T(8,128)(2,1)S(1)}, bf16[512,128]{1,0:T(8,128)(2,1)}, u32[]{:S(2)}) copy-start(bf16[512,128]{1,0:T(8,128)(2,1)} %own_ref.1) | copy-start | bytes 393220
  15.9 15.8 %all-to-all-start = ((bf16[16,144,128]{2,1,0:T(8,128)(2,1)}), bf16[16,144,128]{2,1,0:T(8,128)(2,1)S(1)}, u32[]{:S(2)}, u32[]{:S(2)}) async-start(bf16[16,144,128]{2,1,0:T(8,128)(2,1)} %spread.1), calls=%async_computation | async-start | bytes 1179648 | tf_op jit(solution)/shard_map/all_to_all | solution.py:367
  23.5 6.4 %collective-permute-start.6 = (bf16[4,256,128]{2,1,0:T(8,128)(2,1)S(1)}, bf16[4,256,128]{2,1,0:T(8,128)(2,1)S(1)}, u32[]{:S(2)}, u32[]{:S(2)}) collective-permute-start(bf16[4,256,128]{2,1,0:T(8,128)(2,1)S(1)} %gather.1.refs_0_), channel_id=1, source_target_pairs={{0,2},{2,0},{1,3},{3,1},{4,6},{6,4},{5,7},{7,5},{8,10},{10,8},{9,1... | collective-permute-start | bytes 786440 | tf_op jit(solution)/shard_map/ppermute | solution.py:361
  23.6 15.0 %collective-permute-start.4 = (bf16[4,256,128]{2,1,0:T(8,128)(2,1)S(1)}, bf16[4,256,128]{2,1,0:T(8,128)(2,1)S(1)}, u32[]{:S(2)}, u32[]{:S(2)}) collective-permute-start(bf16[4,256,128]{2,1,0:T(8,128)(2,1)S(1)} %gather.1.refs_0_), channel_id=1, source_target_pairs={{0,64},{64,128},{128,192},{192,0},{1,65},{65,129},{129,193},{193,1... | collective-permute-start | bytes 786440 | tf_op jit(solution)/shard_map/ppermute | solution.py:359
  26.9 16.5 %collective-permute-start.5 = (bf16[4,256,128]{2,1,0:T(8,128)(2,1)S(1)}, bf16[4,256,128]{2,1,0:T(8,128)(2,1)S(1)}, u32[]{:S(2)}, u32[]{:S(2)}) collective-permute-start(bf16[4,256,128]{2,1,0:T(8,128)(2,1)S(1)} %gather.1.refs_0_), channel_id=1, source_target_pairs={{0,192},{64,0},{128,64},{192,128},{1,193},{65,1},{129,65},{193,129... | collective-permute-start | bytes 786440 | tf_op jit(solution)/shard_map/ppermute | solution.py:360
  29.9 13.6 %collective-permute-start.7 = (bf16[512,128]{1,0:T(8,128)(2,1)S(1)}, bf16[512,128]{1,0:T(8,128)(2,1)S(1)}, u32[]{:S(2)}, u32[]{:S(2)}) collective-permute-start(bf16[512,128]{1,0:T(8,128)(2,1)S(1)} %passed.1), channel_id=1, source_target_pairs={{62,126},{126,190},{190,254},{254,62},{63,127},{127,191},{191,255}... | collective-permute-start | bytes 393224 | tf_op jit(solution)/shard_map/ppermute | solution.py:363
  30.5 12.9 %collective-permute-start.8 = (bf16[512,128]{1,0:T(8,128)(2,1)S(1)}, bf16[512,128]{1,0:T(8,128)(2,1)S(1)}, u32[]{:S(2)}, u32[]{:S(2)}) collective-permute-start(bf16[512,128]{1,0:T(8,128)(2,1)S(1)} %passed.1), channel_id=1, source_target_pairs={{64,0},{128,64},{192,128},{0,192},{65,1},{129,65},{193,129},{1,193}} | collective-permute-start | bytes 393224 | tf_op jit(solution)/shard_map/ppermute | solution.py:364
  43.5 4.3 %collective-permute-start.11 = (bf16[8,256,128]{2,1,0:T(8,128)(2,1)S(1)}, bf16[8,256,128]{2,1,0:T(8,128)(2,1)S(1)}, u32[]{:S(2)}, u32[]{:S(2)}) collective-permute-start(bf16[8,256,128]{2,1,0:T(8,128)(2,1)S(1)} %get-tuple-element.26.refs_0_), channel_id=1, source_target_pairs={{0,2},{2,0},{1,3},{3,1},{4,6},{6,4},{5,7},{7,5},{8,10},{10,8},{9,1... | collective-permute-start | bytes 1572872 | tf_op jit(solution)/shard_map/ppermute | solution.py:375
  43.6 14.2 %collective-permute-start.9 = (bf16[2,256,128]{2,1,0:T(8,128)(2,1)S(1)}, bf16[2,256,128]{2,1,0:T(8,128)(2,1)S(1)}, u32[]{:S(2)}, u32[]{:S(2)}) collective-permute-start(bf16[2,256,128]{2,1,0:T(8,128)(2,1)S(1)} %get-tuple-element.24), channel_id=1, source_target_pairs={{0,64},{64,128},{128,192},{192,0},{1,65},{65,129},{129,193},{193,1... | collective-permute-start | bytes 393224 | tf_op jit(solution)/shard_map/ppermute | solution.py:373
  47.6 10.3 %collective-permute-start.10 = (bf16[2,256,128]{2,1,0:T(8,128)(2,1)S(1)}, bf16[2,256,128]{2,1,0:T(8,128)(2,1)S(1)}, u32[]{:S(2)}, u32[]{:S(2)}) collective-permute-start(bf16[2,256,128]{2,1,0:T(8,128)(2,1)S(1)} %get-tuple-element.25), channel_id=1, source_target_pairs={{0,192},{64,0},{128,64},{192,128},{1,193},{65,1},{129,65},{193,129... | collective-permute-start | bytes 393224 | tf_op jit(solution)/shard_map/ppermute | solution.py:374
  57.9 1.6 %collective-permute-start.12 = (bf16[4,256,128]{2,1,0:T(8,128)(2,1)S(1)}, bf16[4,256,128]{2,1,0:T(8,128)(2,1)S(1)}, u32[]{:S(2)}, u32[]{:S(2)}) collective-permute-start(bf16[4,256,128]{2,1,0:T(8,128)(2,1)S(1)} %across.1.refs_0_), channel_id=1, source_target_pairs={{0,2},{2,0},{1,3},{3,1},{4,6},{6,4},{5,7},{7,5},{8,10},{10,8},{9,1... | collective-permute-start | bytes 786440 | tf_op jit(solution)/shard_map/ppermute | solution.py:377
  67.2 20.4 %all-to-all-start.1 = ((f32[4,528,128]{2,1,0:T(8,128)}), f32[4,528,128]{2,1,0:T(8,128)S(1)}, u32[]{:S(2)}, u32[]{:S(2)}) async-start(f32[4,528,128]{2,1,0:T(8,128)} %attend2.1.wait_ref), calls=%async_computation.1 | async-start | bytes 2162688 | tf_op jit(solution)/shard_map/all_to_all | solution.py:397
  74.4 6.7 %collective-permute-start.14 = (bf16[512,128]{1,0:T(8,128)(2,1)S(1)}, bf16[512,128]{1,0:T(8,128)(2,1)S(1)}, u32[]{:S(2)}, u32[]{:S(2)}) collective-permute-start(bf16[512,128]{1,0:T(8,128)(2,1)S(1)} %get-tuple-element.27), channel_id=1, source_target_pairs={{0,2},{2,4},{4,6},{6,8},{8,10},{10,12},{12,14},{14,16},{16,18},{18... | collective-permute-start | bytes 393224 | tf_op jit(solution)/shard_map/ppermute | solution.py:381
  74.5 19.4 %copy-start.8 = (s32[4,4]{1,0:T(4,128)S(1)}, s32[4,4]{1,0:T(4,128)}, u32[]{:S(2)}) copy-start(s32[4,4]{1,0:T(4,128)} %param.19) | copy-start | bytes 196
  74.5 19.4 %copy-start.7 = (s32[512,8]{0,1:T(8,128)S(1)}, s32[512,8]{0,1:T(8,128)}, u32[]{:S(2)}) copy-start(s32[512,8]{0,1:T(8,128)} %param.20) | copy-start | bytes 49156
  74.5 6.6 %collective-permute-start.15 = (bf16[512,128]{1,0:T(8,128)(2,1)S(1)}, bf16[512,128]{1,0:T(8,128)(2,1)S(1)}, u32[]{:S(2)}, u32[]{:S(2)}) collective-permute-start(bf16[512,128]{1,0:T(8,128)(2,1)S(1)} %get-tuple-element.28), channel_id=1, source_target_pairs={{2,0},{4,2},{6,4},{8,6},{10,8},{12,10},{14,12},{16,14},{18,16},{20... | collective-permute-start | bytes 393224 | tf_op jit(solution)/shard_map/ppermute | solution.py:382
  78.3 5.0 %collective-permute-start.13 = (bf16[128,256]{1,0:T(8,128)(2,1)S(1)}, bf16[128,256]{1,0:T(8,128)(2,1)S(1)}, u32[]{:S(2)}, u32[]{:S(2)}) collective-permute-start(bf16[128,256]{1,0:T(8,128)(2,1)S(1)} %copy-done.2), channel_id=1, source_target_pairs={{0,1},{1,0},{2,3},{3,2},{4,5},{5,4},{6,7},{7,6},{8,9},{9,8},{10,11... | collective-permute-start | bytes 196616 | tf_op jit(solution)/shard_map/ppermute | solution.py:338
  81.1 12.9 %copy-start.4 = (bf16[2,256,128]{2,1,0:T(8,128)(2,1)S(1)}, bf16[2,256,128]{2,1,0:T(8,128)(2,1)}, u32[]{:S(2)}) copy-start(bf16[2,256,128]{2,1,0:T(8,128)(2,1)} %ws_ref.1) | copy-start | bytes 393220
  81.1 12.9 %collective-permute-start.16 = (bf16[1024,128]{1,0:T(8,128)(2,1)S(1)}, bf16[1024,128]{1,0:T(8,128)(2,1)S(1)}, u32[]{:S(2)}, u32[]{:S(2)}) collective-permute-start(bf16[1024,128]{1,0:T(8,128)(2,1)S(1)} %around.1.near_ref), channel_id=1, source_target_pairs={{0,1},{1,0},{2,3},{3,2},{4,5},{5,4},{6,7},{7,6},{8,9},{9,8},{10,11... | collective-permute-start | bytes 786440 | tf_op jit(solution)/shard_map/ppermute | solution.py:384
  88.4 12.7 %all-to-all-start.2 = ((bf16[8,128,128]{2,1,0:T(8,128)(2,1)}), bf16[8,128,128]{2,1,0:T(8,128)(2,1)S(1)}, u32[]{:S(2)}, u32[]{:S(2)}) async-start(bf16[8,128,128]{2,1,0:T(8,128)(2,1)} %mix.1), calls=%async_computation.2 | async-start | bytes 524288 | tf_op jit(solution)/shard_map/all_to_all | solution.py:398
  (5 other events, 38.5 us)
